TPU v7x, 32 devices: a whole 2x2x4 slice. The times are simulated.
32 devices in a mesh: sec: 4 (over y, x), tile: 8 (over z, core).
Axes of the slice: x: 2, y: 2, z: 4, core: 2. Of those that a mesh axis runs over, the one named last changes fastest.
Arguments:
- patches: bfloat16 [4, 32, 512, 512], P('sec', 'tile'), may hold values from -6 to 6
- zoom: float32 [4, 2, 32], P('sec'), may hold values from 0.75 to 0.9
- frac: float32 [4, 2, 32], P('sec'), may hold values from 0 to 1
- offset: int32 [4, 2, 32], P('sec'), may hold values from 0 to 15
- owner: int32 [4, 32, 16, 1], P('sec'), may hold values from 0 to 7; in each aligned block of 64 rows (0 to 63, 64 to 127, ..., all dimensions but the last counted through in order) at most 16 rows name the same one
- top_grid: bfloat16 [8, 256, 256], P('tile'), may hold values from -3 to 3
Outputs:
- grid_image: bfloat16 [4, 8, 256, 256], P('sec', 'tile')
- corrections: float32 [6, 4, 32], P(None, 'sec', 'tile')
Inputs may be any that keep to these rules, and one draw needn't show every extreme that they name: `owner`: in each section, the bands of one device's 4 tiles (aligned blocks of 64 rows) name no grid tile more than 16 times; in some blocks one grid tile is named exactly 16 times.
All inputs are finite; a program needn't handle non-finite values.
Results may differ from a plain program's by a relative error of at most 0.0018.
The roundings to bfloat16 on the way count: a program that leaves them out, or rounds other values in their place, can miss the bound.
Values may be sent and summed in bfloat16 or wider, within the bound.
No kernel may reach another device: no remote copies, remote signals or barrier semaphores. Data moves between devices by JAX's collectives and lax.ppermute only.
A program may use at most 64 MiB of HBM per device.

v0:
```python
import math

import jax
import jax.numpy as jnp
from jax import lax
from jax.sharding import PartitionSpec as P

BAND = 16
ITERS = 2


COUPLING = 0.25


def passed_along(block, axis, distance):
    devices = range(lax.axis_size(axis))
    route = [(i - distance, i) for i in devices if i - distance in devices]
    return lax.ppermute(block, axis, route)


def padded_2(cells, sides, width):
    for axis, dim in sides:
        count = lax.axis_size(axis)
        ends = count - 1
        head = lax.slice_in_dim(cells, 0, width, axis=dim)
        tail = lax.slice_in_dim(cells, cells.shape[dim] - width, cells.shape[dim], axis=dim)
        cells = jnp.concatenate(
            [
                lax.ppermute(tail, axis, [(i, (i + 1) % count) for i in range(ends)]),
                cells,
                lax.ppermute(head, axis, [((i + 1) % count, i) for i in range(ends)]),
            ],
            axis=dim,
        )
    return cells


def hat_weight(distance):
    return jnp.maximum(0.0, 1.0 - jnp.abs(distance))


def sample_points(zoom, frac, offset, frame, source):
    scale = zoom * (frame / source)
    spots = jnp.arange(frame, dtype=jnp.float32)
    return (spots - offset.astype(jnp.float32)[..., None] - frac[..., None]) / scale[..., None]


def coverage(points, source):
    return jnp.clip(jnp.minimum(points + 1.0, source - points), 0.0, 1.0)


def moments(intensity, target, row_cover, col_cover, row_pos, frame):
    middle = (frame - 1) / 2.0
    level = intensity.astype(jnp.float32)
    error = target.astype(jnp.float32) - level
    weight = row_cover[:, :, None] * col_cover[:, None, :] / (frame * frame)
    columns = (jnp.arange(frame, dtype=jnp.float32) - middle) / (frame / 2.0)
    row_coord = (row_pos - middle) / (frame / 2.0)
    x_grid = jnp.broadcast_to(columns[None, None, :], level.shape)
    y_grid = jnp.broadcast_to(row_coord[:, :, None], level.shape)
    features = jnp.stack(
        [jnp.ones_like(level), x_grid, y_grid, level, level * x_grid, level * y_grid], axis=1
    )
    weighted = features * weight[:, None]
    normal = jnp.einsum("bfrq,bgrq->bfg", weighted, features, precision=lax.Precision.HIGHEST)
    gradient = jnp.einsum("bfrq,brq->bf", weighted, error, precision=lax.Precision.HIGHEST)
    return (normal, gradient)


def blocked_moments(intensity, target, row_cover, col_cover, row_pos, frame):
    count = intensity.shape[0]
    block_size = math.gcd(count, 64)

    def block_moments(block_args):
        return moments(
            block_args[0], block_args[1], block_args[2], block_args[3], block_args[4], frame
        )

    shaped = tuple(
        (
            member.reshape((count // block_size, block_size) + member.shape[1:])
            for member in (intensity, target, row_cover, col_cover, row_pos)
        )
    )
    normal, gradient = lax.map(block_moments, shaped)
    return (normal.reshape(count, 6, 6), gradient.reshape(count, 6))


def slot_table(routes, devices):
    matches = (routes[..., None] == jnp.arange(devices, dtype=jnp.int32)).astype(jnp.int32)
    before = jnp.cumsum(matches, axis=-2) - matches
    return jnp.sum(before * matches, axis=-1)


def precond_norm(residual, scaled):
    return lax.psum(jnp.sum(residual * scaled), ("sec", "tile"))


def shards(patches, zoom, frac, offset, owner, top_grid):
    sections, tile_count, source, _ = patches.shape
    frame = top_grid.shape[1]
    devices = lax.axis_size("tile")
    my_tile = lax.axis_index("tile")
    band_count = frame // BAND
    row_count = tile_count * band_count
    capacity = max(2, 2 * row_count // devices)
    slot_total = devices * capacity
    all_tiles = tile_count * devices
    points = sample_points(zoom, frac, offset, frame, source)
    covered = coverage(points, source)
    own_points = lax.dynamic_slice_in_dim(points, my_tile * tile_count, tile_count, 2)
    spots = jnp.arange(source, dtype=jnp.float32)
    weights = hat_weight(own_points[..., None] - spots).astype(jnp.bfloat16)
    halfway = jnp.einsum(
        "stqp,stpr->stqr", weights[:, 0], patches, preferred_element_type=jnp.float32
    ).astype(jnp.bfloat16)
    rendered = jnp.einsum(
        "stqr,stwr->stqw", halfway, weights[:, 1], preferred_element_type=jnp.float32
    ).astype(jnp.bfloat16)
    band_data = rendered.reshape(sections, row_count, BAND * frame)
    routes = owner[..., 0].reshape(sections, devices, row_count)
    slots = slot_table(routes, devices)
    own_routes = lax.dynamic_index_in_dim(routes, my_tile, 1, keepdims=False)
    own_slots = lax.dynamic_index_in_dim(slots, my_tile, 1, keepdims=False)
    positions = own_routes * capacity + own_slots
    slot_ids = jnp.arange(slot_total, dtype=jnp.int32)
    send_select = (positions[:, None, :] == slot_ids[None, :, None]).astype(jnp.bfloat16)
    outgoing = jnp.einsum(
        "smr,srx->smx", send_select, band_data, preferred_element_type=jnp.float32
    ).astype(jnp.bfloat16)
    incoming = lax.all_to_all(
        outgoing.reshape(sections, devices, capacity, BAND * frame),
        "tile",
        split_axis=1,
        concat_axis=1,
        tiled=True,
    )
    incoming = incoming.reshape(sections, slot_total, BAND * frame)
    is_mine = routes == my_tile
    cap_ids = jnp.arange(capacity, dtype=jnp.int32)
    receive_hit = (
        is_mine[:, :, None, :] & (slots[:, :, None, :] == cap_ids[None, None, :, None])
    ).astype(jnp.float32)
    receive_hit = receive_hit.reshape(sections, slot_total, row_count)
    band_of_row = jnp.arange(row_count, dtype=jnp.int32) % band_count
    band_onehot = (band_of_row[:, None] == jnp.arange(band_count, dtype=jnp.int32)[None, :]).astype(
        jnp.float32
    )
    slot_band = jnp.einsum("smr,rk->smk", receive_hit, band_onehot, precision=lax.Precision.HIGHEST)
    band_select = jnp.einsum(
        "smr,rk->skm", receive_hit, band_onehot, precision=lax.Precision.HIGHEST
    ).astype(jnp.bfloat16)
    image_sum = jnp.einsum(
        "skm,smx->skx", band_select, incoming, preferred_element_type=jnp.float32
    )
    own_share = (routes.reshape(sections, all_tiles, band_count) == my_tile).astype(jnp.float32)
    row_bands = covered[:, 0].reshape(sections, all_tiles, band_count, BAND)
    cover_sum = jnp.einsum(
        "sik,sikr,siw->skrw", own_share, row_bands, covered[:, 1], precision=lax.Precision.HIGHEST
    )
    grid_local = (image_sum.reshape(sections, band_count, BAND, frame) / (1.0 + cover_sum)).astype(
        jnp.bfloat16
    )
    grid_local = grid_local.reshape(sections, frame, frame)
    from_next = passed_along(grid_local[0], "sec", -1)
    at_top = lax.axis_index("sec") == lax.axis_size("sec") - 1
    boundary = jnp.where(at_top, top_grid[0], from_next)
    above = jnp.concatenate([grid_local[1:], boundary[None]], axis=0).reshape(
        sections, band_count, BAND * frame
    )
    slot_target = jnp.einsum(
        "smk,skx->smx", slot_band.astype(jnp.bfloat16), above, preferred_element_type=jnp.float32
    ).astype(jnp.bfloat16)
    band_spots = jnp.arange(BAND, dtype=jnp.float32)
    returned = lax.all_to_all(
        slot_target.reshape(sections, devices, capacity, BAND * frame),
        "tile",
        split_axis=1,
        concat_axis=1,
        tiled=True,
    )
    returned = returned.reshape(sections, slot_total, BAND * frame)
    row_target = jnp.einsum(
        "smr,smx->srx", send_select, returned, preferred_element_type=jnp.float32
    ).astype(jnp.bfloat16)
    own_cover = lax.dynamic_slice_in_dim(covered, my_tile * tile_count, tile_count, 2)
    own_rows = own_cover[:, 0].reshape(sections, row_count, BAND)
    own_cols = jnp.broadcast_to(
        own_cover[:, 1][:, :, None, :], (sections, tile_count, band_count, frame)
    ).reshape(sections, row_count, frame)
    row_pos = (band_of_row.astype(jnp.float32) * BAND)[:, None] + band_spots
    row_pos = row_pos[None]
    normal, gradient = blocked_moments(
        band_data.reshape(-1, BAND, frame),
        row_target.reshape(-1, BAND, frame),
        own_rows.reshape(-1, BAND),
        own_cols.reshape(-1, frame),
        row_pos.reshape(-1, BAND),
        frame,
    )
    tile_normal = normal.reshape(sections, tile_count, band_count, 6, 6).sum(axis=2)
    tile_gradient = gradient.reshape(sections, tile_count, band_count, 6).sum(axis=2)
    right_side = jnp.transpose(tile_gradient, (2, 0, 1))
    diagonal_part = jnp.transpose(jnp.diagonal(tile_normal, axis1=2, axis2=3), (2, 0, 1))
    precond = 1.0 / (diagonal_part + 4.0 * COUPLING)
    solution = jnp.zeros_like(right_side)
    residual = right_side
    scaled = precond * residual
    direction = scaled
    current = precond_norm(residual, scaled)
    for step in range(ITERS):
        padded = padded_2(direction, (("sec", 1), ("tile", 2)), 1)
        beside = (
            padded[:, 2:, 1:-1] + padded[:, :-2, 1:-1] + padded[:, 1:-1, 2:] + padded[:, 1:-1, :-2]
        )
        image = jnp.einsum(
            "stfg,gst->fst", tile_normal, direction, precision=lax.Precision.HIGHEST
        ) + COUPLING * (4.0 * direction - beside)
        alpha = current / lax.psum(jnp.sum(direction * image), ("sec", "tile"))
        solution = solution + alpha * direction
        if step + 1 < ITERS:
            residual = residual - alpha * image
            scaled = precond * residual
            following = precond_norm(residual, scaled)
            direction = scaled + following / current * direction
            current = following
    return (grid_local[:, None], solution)


def solution(mesh):
    placed = (
        P("sec", "tile", None, None),
        P("sec", None, None),
        P("sec", None, None),
        P("sec", None, None),
        P("sec", None, None, None),
        P("tile", None, None),
    )
    return jax.shard_map(
        shards,
        mesh=mesh,
        in_specs=placed,
        out_specs=(P("sec", "tile", None, None), P(None, "sec", "tile")),
        check_vma=False,
    )
```

profile of v0, /device:TPU:0, one launch (start us, length us, event | category | flops | bytes accessed | tf_op | source)
XLA Modules:
  0.0 287.5 jit_solution(8670080170377180339)
XLA Ops:
  0.6 0.9 copy.78
  1.8 1.4 fusion.49
  3.2 0.7 multiply_bitcast_fusion
  3.9 0.7 convert_bitcast_fusion
  4.5 0.8 minimum_clamp_fusion
  5.4 2.0 maximum_convert_fusion
  7.4 3.3 %fusion.50 = (f32[4,256,256]{2,1,0:T(8,128)S(1)}, bf16[4,256,256]{2,1,0:T(8,128)(2,1)}) fusion(bf16[1,2,4,256,512]{4,3,2,1,0:T(8,128)(2,1)} %maximum_convert_fusion, bf16[1,4,512,512]{3,2,1,0:T(8,128)(2,1)S(1)} %copy-done), kind=kOutput, calls=%fused_computation.112 | convolution fusion | flops 806354944 | bytes 5767168 | tf_op jit(solution)/shard_map/stqr,stwr->stqw/dot_general | solution.py:117
  10.7 2.1 reshape.361
  13.0 2.4 convolution_convert_fusion.1
  15.4 6.3 %all-to-all-start = ((bf16[1,8,16,4096]{3,2,0,1:T(8,128)(2,1)}), bf16[1,8,16,4096]{3,2,0,1:T(8,128)(2,1)}, u32[]{:S(2)}, u32[]{:S(2)}) async-start(bf16[1,8,16,4096]{3,2,0,1:T(8,128)(2,1)} %bitcast.153), calls=%async_computation | async-start | bytes 2097152 | tf_op jit(solution)/shard_map/all_to_all | solution.py:131
  21.8 1.2 broadcast_dynamic-update-slice_fusion.2
  23.7 1.2 broadcast_dynamic-update-slice_fusion.1
  24.9 1.2 broadcast_dynamic-update-slice_fusion
  26.1 1.1 constant_dynamic-update-slice_fusion
  27.3 0.7 broadcast_multiply_fusion.1
  27.9 1.1 multiply_dynamic-update-slice_fusion.1
  29.1 1.2 multiply_dynamic-update-slice_fusion
  30.3 18.2 %all-to-all-done = bf16[1,8,16,4096]{3,2,0,1:T(8,128)(2,1)} async-done(((bf16[1,8,16,4096]{3,2,0,1:T(8,128)(2,1)}), bf16[1,8,16,4096]{3,2,0,1:T(8,128)(2,1)}, u32[]{:S(2)}, u32[]{:S(2)}) %all-to-all-start) | async-done | bytes 1048608 | tf_op jit(solution)/shard_map/all_to_all | solution.py:131
  48.5 2.3 copy.83
  50.7 1.6 fusion.53
  52.8 1.3 collective-permute-start
  54.3 5.4 %collective-permute-done = bf16[256,256]{1,0:T(8,128)(2,1)S(1)} collective-permute-done((bf16[256,256]{1,0:T(8,128)(2,1)S(1)}, bf16[256,256]{1,0:T(8,128)(2,1)S(1)}, u32[]{:S(2)}, u32[]{:S(2)}) %collective-permute-start) | collective-permute-done | bytes 131104 | tf_op jit(solution)/shard_map/ppermute | solution.py:18
  59.7 0.9 bitcast_select_fusion
  60.7 1.4 convolution_convert_fusion
  62.1 4.7 %all-to-all-start.1 = ((bf16[1,8,16,4096]{3,2,0,1:T(8,128)(2,1)}), bf16[1,8,16,4096]{3,2,0,1:T(8,128)(2,1)}, u32[]{:S(2)}, u32[]{:S(2)}) async-start(bf16[1,8,16,4096]{3,2,0,1:T(8,128)(2,1)} %bitcast.154), calls=%async_computation.1 | async-start | bytes 2097152 | tf_op jit(solution)/shard_map/all_to_all | solution.py:175
  67.1 4.0 %broadcast_multiply_fusion = f32[64,6,16,256]{3,2,1,0:T(8,128)S(1)} fusion(f32[64,6,16,256]{3,2,1,0:T(8,128)} %multiply_dynamic-update-slice_fusion, f32[64,16,256]{2,1,0:T(8,128)S(1)} %multiply_multiply_fusion), kind=kLoop, calls=%fused_computation.11 | loop fusion | flops 1572864 | bytes 13631488 | tf_op jit(solution)/shard_map/while/body/eval_jaxpr/mul | solution.py:64
  71.6 26.8 %fusion.2 = f32[64,6,6,1]{2,1,3,0:T(8,128)S(1)} fusion(f32[64,6,16,256]{3,2,1,0:T(8,128)S(1)} %broadcast_multiply_fusion, f32[64,6,16,256]{3,2,1,0:T(8,128)S(1)} %bitcast.145), kind=kOutput, calls=%fused_computation.3 | convolution fusion | flops 113246208 | bytes 12592128 | tf_op jit(solution)/shard_map/while/body/eval_jaxpr/bfrq,bgrq->bfg/dot_general | solution.py:65
  99.3 1.7 fusion.5
  101.6 0.8 copy-done.2
  102.4 22.2 %fusion = f32[64,1,6,1]{2,1,3,0:T(1,128)S(1)} fusion(f32[64,6,16,256]{3,2,1,0:T(8,128)S(1)} %copy-done.2, f32[64,16,256,1]{2,1,0,3:T(8,128)S(1)} %bitcast.150), kind=kOutput, calls=%fused_computation.1 | convolution fusion | flops 18874368 | bytes 7341568 | tf_op jit(solution)/shard_map/while/body/eval_jaxpr/bfrq,brq->bf/dot_general | solution.py:66
  124.9 1.3 collective-permute-start.1
  126.2 4.9 %collective-permute-start.2 = (f32[6,1,4]{0,2,1:T(4,128)S(1)}, f32[6,1,4]{0,2,1:T(4,128)S(1)}, u32[]{:S(2)}, u32[]{:S(2)}) collective-permute-start(f32[6,1,4]{0,2,1:T(4,128)S(1)} %bitcast_multiply_fusion.1), channel_id=1, source_target_pairs={{0,8},{8,16},{16,24},{1,9},{9,17},{17,25},{2,10},{10,18},{18,26},{... | collective-permute-start | bytes 296 | tf_op jit(solution)/shard_map/ppermute | solution.py:29
  131.4 1.1 collective-permute-done.2
  132.5 1.4 collective-permute-start.4
  133.9 1.3 collective-permute-start.3
  135.2 3.7 %collective-permute-done.3 = f32[6,3,1]{0,2,1:T(1,128)S(1)} collective-permute-done((f32[6,3,1]{0,2,1:T(1,128)S(1)}, f32[6,3,1]{0,2,1:T(1,128)S(1)}, u32[]{:S(2)}, u32[]{:S(2)}) %collective-permute-start.3) | collective-permute-done | bytes 104 | tf_op jit(solution)/shard_map/ppermute | solution.py:31
  138.9 0.7 multiply_reduce_fusion.1
  139.6 44.5 %all-reduce = (f32[]{:T(128)}, f32[]{:T(128)}) all-reduce(f32[]{:T(128)} %get-tuple-element.19, f32[]{:T(128)} %get-tuple-element.18), channel_id=1, replica_groups=mesh['sec'=4,'tile'=8] {'sec','tile'}, use_global_device_ids=true, to_apply=%region_5.6 | all-reduce | flops 2 | bytes 16 | tf_op jit(solution)/shard_map/psum | solution.py:96
  185.4 0.6 multiply_reduce_fusion
  186.0 40.3 %psum.30 = f32[]{:T(128)} all-reduce(f32[]{:T(128)} %multiply_reduce_fusion), channel_id=1, replica_groups=mesh['sec'=4,'tile'=8] {'sec','tile'}, use_global_device_ids=true, to_apply=%region_9.10 | all-reduce | flops 1 | bytes 8 | tf_op jit(solution)/shard_map/psum | solution.py:96
  227.5 1.3 collective-permute-start.5
  228.8 4.8 %collective-permute-start.6 = (f32[6,1,4]{0,2,1:T(4,128)S(1)}, f32[6,1,4]{0,2,1:T(4,128)S(1)}, u32[]{:S(2)}, u32[]{:S(2)}) collective-permute-start(f32[6,1,4]{0,2,1:T(4,128)S(1)} %multiply_add_fusion.1), channel_id=1, source_target_pairs={{0,8},{8,16},{16,24},{1,9},{9,17},{17,25},{2,10},{10,18},{18,26},{... | collective-permute-start | bytes 296 | tf_op jit(solution)/shard_map/ppermute | solution.py:29
  233.8 1.1 collective-permute-done.6
  235.0 1.3 collective-permute-start.8
  236.2 1.3 collective-permute-start.7
  237.6 2.6 collective-permute-done.7
  240.1 0.7 fusion.44
  240.8 44.3 %psum.31 = f32[]{:T(128)} all-reduce(f32[]{:T(128)} %fusion.44), channel_id=1, replica_groups=mesh['sec'=4,'tile'=8] {'sec','tile'}, use_global_device_ids=true, to_apply=%region_11.12 | all-reduce | flops 1 | bytes 8 | tf_op jit(solution)/shard_map/psum | solution.py:219
  (67 shorter events, 5.3 us)
Async XLA Ops:
  0.6 6.8 %copy-start = (bf16[1,4,512,512]{3,2,1,0:T(8,128)(2,1)S(1)}, bf16[1,4,512,512]{3,2,1,0:T(8,128)(2,1)}, u32[]{:S(2)}) copy-start(bf16[1,4,512,512]{3,2,1,0:T(8,128)(2,1)} %param.6) | copy-start | bytes 6291460
  10.7 16.6 %copy-start.5 = (s32[1,32,16,1]{1,3,2,0:T(1,128)S(1)}, s32[1,32,16,1]{1,3,2,0:T(1,128)}, u32[]{:S(2)}) copy-start(s32[1,32,16,1]{1,3,2,0:T(1,128)} %param.10) | copy-start | bytes 6148
  15.4 33.0 %all-to-all-start = ((bf16[1,8,16,4096]{3,2,0,1:T(8,128)(2,1)}), bf16[1,8,16,4096]{3,2,0,1:T(8,128)(2,1)}, u32[]{:S(2)}, u32[]{:S(2)}) async-start(bf16[1,8,16,4096]{3,2,0,1:T(8,128)(2,1)} %bitcast.153), calls=%async_computation | async-start | bytes 2097152 | tf_op jit(solution)/shard_map/all_to_all | solution.py:131
  27.9 24.4 %copy-start.4 = (f32[32,16,16]{0,2,1:T(8,128)S(1)}, f32[32,16,16]{0,2,1:T(8,128)}, u32[]{:S(2)}) copy-start(f32[32,16,16]{0,2,1:T(8,128)} %broadcast_multiply_fusion.1) | copy-start | bytes 98308
  52.8 6.9 %copy-start.3 = (bf16[16,16,256]{2,1,0:T(8,128)(2,1)}, bf16[16,16,256]{2,1,0:T(8,128)(2,1)S(1)}, u32[]{:S(2)}) copy-start(bf16[16,16,256]{2,1,0:T(8,128)(2,1)S(1)} %copy.86) | copy-start | bytes 393220
  52.8 6.9 %collective-permute-start = (bf16[256,256]{1,0:T(8,128)(2,1)S(1)}, bf16[256,256]{1,0:T(8,128)(2,1)S(1)}, u32[]{:S(2)}, u32[]{:S(2)}) collective-permute-start(bf16[256,256]{1,0:T(8,128)(2,1)S(1)} %bitcast.158), channel_id=1, source_target_pairs={{8,0},{16,8},{24,16},{9,1},{17,9},{25,17},{10,2},{18,10},{26,18},{... | collective-permute-start | bytes 393224 | tf_op jit(solution)/shard_map/ppermute | solution.py:18
  62.1 37.2 %all-to-all-start.1 = ((bf16[1,8,16,4096]{3,2,0,1:T(8,128)(2,1)}), bf16[1,8,16,4096]{3,2,0,1:T(8,128)(2,1)}, u32[]{:S(2)}, u32[]{:S(2)}) async-start(bf16[1,8,16,4096]{3,2,0,1:T(8,128)(2,1)} %bitcast.154), calls=%async_computation.1 | async-start | bytes 2097152 | tf_op jit(solution)/shard_map/all_to_all | solution.py:175
  66.9 4.3 %slice-start = ((s8[6291456]{0:T(1024)(128)(4,1)}), s8[4194304]{0:T(1024)(128)(4,1)S(1)}, s32[]{:S(2)}) async-start(s8[6291456]{0:T(1024)(128)(4,1)} %bitcast.144), calls=%async_computation.2 | async-start | bytes 8388608
  67.1 4.5 %slice-start.1 = ((s8[6291456]{0:T(1024)(128)(4,1)}), s8[2097152]{0:T(1024)(128)(4,1)S(1)}, s32[]{:S(2)}) async-start(s8[6291456]{0:T(1024)(128)(4,1)} %bitcast.144), calls=%async_computation.3 | async-start | bytes 4194304
  71.6 26.8 %copy-start.1 = (f32[64,6,16,256]{3,2,1,0:T(8,128)}, f32[64,6,16,256]{3,2,1,0:T(8,128)S(1)}, u32[]{:S(2)}) copy-start(f32[64,6,16,256]{3,2,1,0:T(8,128)S(1)} %broadcast_multiply_fusion) | copy-start | bytes 18874372
  99.3 3.1 %copy-start.2 = (f32[64,6,16,256]{3,2,1,0:T(8,128)S(1)}, f32[64,6,16,256]{3,2,1,0:T(8,128)}, u32[]{:S(2)}) copy-start(f32[64,6,16,256]{3,2,1,0:T(8,128)} %copy-done.1) | copy-start | bytes 18874372
  124.9 6.4 %collective-permute-start.1 = (f32[6,1,4]{0,2,1:T(4,128)S(1)}, f32[6,1,4]{0,2,1:T(4,128)S(1)}, u32[]{:S(2)}, u32[]{:S(2)}) collective-permute-start(f32[6,1,4]{0,2,1:T(4,128)S(1)} %bitcast_multiply_fusion.1), channel_id=1, source_target_pairs={{8,0},{16,8},{24,16},{9,1},{17,9},{25,17},{10,2},{18,10},{26,18},{... | collective-permute-start | bytes 296 | tf_op jit(solution)/shard_map/ppermute | solution.py:31
  126.2 6.2 %collective-permute-start.2 = (f32[6,1,4]{0,2,1:T(4,128)S(1)}, f32[6,1,4]{0,2,1:T(4,128)S(1)}, u32[]{:S(2)}, u32[]{:S(2)}) collective-permute-start(f32[6,1,4]{0,2,1:T(4,128)S(1)} %bitcast_multiply_fusion.1), channel_id=1, source_target_pairs={{0,8},{8,16},{16,24},{1,9},{9,17},{17,25},{2,10},{10,18},{18,26},{... | collective-permute-start | bytes 296 | tf_op jit(solution)/shard_map/ppermute | solution.py:29
  132.5 2.7 collective-permute-start.4
  133.9 5.0 %collective-permute-start.3 = (f32[6,3,1]{0,2,1:T(1,128)S(1)}, f32[6,3,1]{0,2,1:T(1,128)S(1)}, u32[]{:S(2)}, u32[]{:S(2)}) collective-permute-start(f32[6,3,1]{0,2,1:T(1,128)S(1)} %get-tuple-element.35), channel_id=1, source_target_pairs={{1,0},{2,1},{3,2},{4,3},{5,4},{6,5},{7,6},{9,8},{10,9},{11,10},{12... | collective-permute-start | bytes 224 | tf_op jit(solution)/shard_map/ppermute | solution.py:31
  227.5 6.3 %collective-permute-start.5 = (f32[6,1,4]{0,2,1:T(4,128)S(1)}, f32[6,1,4]{0,2,1:T(4,128)S(1)}, u32[]{:S(2)}, u32[]{:S(2)}) collective-permute-start(f32[6,1,4]{0,2,1:T(4,128)S(1)} %multiply_add_fusion.1), channel_id=1, source_target_pairs={{8,0},{16,8},{24,16},{9,1},{17,9},{25,17},{10,2},{18,10},{26,18},{... | collective-permute-start | bytes 296 | tf_op jit(solution)/shard_map/ppermute | solution.py:31
  228.8 6.1 %collective-permute-start.6 = (f32[6,1,4]{0,2,1:T(4,128)S(1)}, f32[6,1,4]{0,2,1:T(4,128)S(1)}, u32[]{:S(2)}, u32[]{:S(2)}) collective-permute-start(f32[6,1,4]{0,2,1:T(4,128)S(1)} %multiply_add_fusion.1), channel_id=1, source_target_pairs={{0,8},{8,16},{16,24},{1,9},{9,17},{17,25},{2,10},{10,18},{18,26},{... | collective-permute-start | bytes 296 | tf_op jit(solution)/shard_map/ppermute | solution.py:29
  235.0 2.6 collective-permute-start.8
  236.2 3.9 %collective-permute-start.7 = (f32[6,3,1]{0,2,1:T(1,128)S(1)}, f32[6,3,1]{0,2,1:T(1,128)S(1)}, u32[]{:S(2)}, u32[]{:S(2)}) collective-permute-start(f32[6,3,1]{0,2,1:T(1,128)S(1)} %get-tuple-element.33), channel_id=1, source_target_pairs={{1,0},{2,1},{3,2},{4,3},{5,4},{6,5},{7,6},{9,8},{10,9},{11,10},{12... | collective-permute-start | bytes 224 | tf_op jit(solution)/shard_map/ppermute | solution.py:31
where the time goes:
time: 293 us; the launch traced here: 288 us
  blocking collectives  129 us (44%)
  matrix products  60.7 us (21%)
  waiting for transfers between devices  32.1 us (11%)
  starting transfers between devices  29.9 us (10%)
  other arithmetic  16.9 us (6%)
  local copies, waits for them, and re-layouts  13.6 us (5%)
  between operations  5.29 us (2%)
    psum x2, blocking collectives, precond_norm(): return lax.psum(jnp.sum(residual * scaled), ('sec', 'tile'))  84.8 us
    psum x1, blocking collectives, shards(): alpha = current / lax.psum(jnp.sum(direction * image), ('sec', 'tile'))  44.3 us
    dot_general x1, matrix products, moments(): jnp.einsum('bfrq,bgrq->bfg', weighted, features, precision=lax.Precision....  26.8 us
    dot_general x1, matrix products, moments(): jnp.einsum('bfrq,brq->bf', weighted, error, precision=lax.Precision.HIGHEST)  22.2 us
    all_to_all x1, waiting for transfers between devices, shards(): lax.all_to_all(outgoing.reshape(sections, devices, capacity, BAND * frame...  18.2 us
    ppermute x4, starting transfers between devices, padded_2(): lax.ppermute(tail, axis, [(i, (i + 1) % count) for i in range(ends)])  12.4 us
    unnamed x22, local copies, waits for them, and re-layouts  7.3 us
    ppermute x4, waiting for transfers between devices, padded_2(): lax.ppermute(head, axis, [((i + 1) % count, i) for i in range(ends)])  6.32 us
  transfers between devices with their start and end apart: 11, of which 6 were waited for; matrix products, arithmetic and copies ran while one was open for 14% of the time, Pallas kernels for 0%

commit v1 on v0

v1 whole, which is shorter than its diff:
```python
import functools

import jax
import jax.numpy as jnp
from jax import lax
from jax.experimental import pallas as pl
from jax.experimental.pallas import tpu as pltpu
from jax.sharding import PartitionSpec as P

BAND = 16
ITERS = 2
COUPLING = 0.25
LANES = 128
ROWS = 8
SMEM = pl.BlockSpec(memory_space=pltpu.SMEM)
VMEM = pl.BlockSpec(memory_space=pltpu.VMEM)


def params(mebibytes):
    return pltpu.CompilerParams(vmem_limit_bytes=mebibytes * 1024 * 1024)


def cost(flops, size):
    return pl.CostEstimate(flops=flops, bytes_accessed=size, transcendentals=0)


def exact_dot(left, right):
    return lax.dot_general(
        left,
        right,
        (((1,), (1,)), ((), ())),
        precision=lax.Precision.HIGHEST,
        preferred_element_type=jnp.float32,
    )


def points_of(spots, zoom, frac, offset, axis, tile, ratio):
    scale = zoom[axis, tile] * ratio
    return (spots - offset[axis, tile].astype(jnp.float32) - frac[axis, tile]) / scale


def cover_of(points, source):
    return jnp.clip(jnp.minimum(points + 1.0, source - points), 0.0, 1.0)


def hat_weight(distance):
    return jnp.maximum(0.0, 1.0 - jnp.abs(distance))


def spots_along(shape, dim, start=0):
    return (lax.broadcasted_iota(jnp.int32, shape, dim) + start).astype(jnp.float32)


def coords(spots, frame):
    return (spots - (frame - 1) / 2.0) / (frame / 2.0)


def render_kernel(sizes, zoom, frac, offset, owner, patch, outgoing, frames, named):
    tiles, bands, frame, source, capacity, devices = sizes
    step = pl.program_id(0)
    tile = lax.axis_index("tile") * tiles + step

    @pl.when(step == 0)
    def _():
        for g in range(devices):
            named[g] = 0
        outgoing[...] = jnp.zeros_like(outgoing)

    ratio = frame / source
    row_points = points_of(spots_along((frame, LANES), 0), zoom, frac, offset, 0, tile, ratio)
    row_weights = jnp.concatenate(
        [
            hat_weight(row_points - spots_along((frame, LANES), 1, first)).astype(jnp.bfloat16)
            for first in range(0, source, LANES)
        ],
        axis=1,
    )
    col_points = points_of(spots_along((ROWS, frame), 1), zoom, frac, offset, 1, tile, ratio)
    col_points = jnp.broadcast_to(col_points[:1], (source, frame))
    col_weights = hat_weight(col_points - spots_along((source, frame), 0)).astype(jnp.bfloat16)
    halfway = jnp.dot(row_weights, patch[0], preferred_element_type=jnp.float32)
    rendered = jnp.dot(
        halfway.astype(jnp.bfloat16), col_weights, preferred_element_type=jnp.float32
    ).astype(jnp.bfloat16)
    frames[0] = rendered
    for band in range(bands):
        target = owner[band, 0, tile]
        slot = named[target]
        named[target] = slot + 1
        outgoing[target * capacity + slot] = rendered[band * BAND : (band + 1) * BAND]


def feature_rows(frame, wanted):
    shape = (ROWS, frame)
    x = coords(spots_along(shape, 1), frame)
    row = lax.broadcasted_iota(jnp.int32, shape, 0)
    rows = jnp.zeros(shape, jnp.float32)
    for r, power in wanted.items():
        rows = jnp.where(row == r, (jnp.ones_like(x), x, x * x)[power], rows)
    return rows


MOMENT_ROWS = ({0: 0, 1: 1, 3: 2}, {2: 0, 4: 1}, {5: 0})


def moment_kernel(
    sizes,
    zoom,
    frac,
    offset,
    owner,
    frames,
    base,
    cover_sum,
    col_cover,
    codes,
    parts,
):
    tiles, bands, frame, source, capacity, devices = sizes
    me = lax.axis_index("tile")
    sec = lax.axis_index("sec")
    sections = lax.axis_size("sec")
    all_tiles = tiles * devices
    ratio = frame / source

    for device in range(devices):

        def note(position, count):
            tile = device * tiles + position // bands
            band = position % bands
            codes[device * capacity + count] = tile * bands + band
            return count + (owner[band, 0, tile] == me).astype(jnp.int32)

        count = lax.fori_loop(0, tiles * bands, note, 0, unroll=8)

        def blank(position, carry):
            codes[device * capacity + position] = -1
            return carry

        lax.fori_loop(count, capacity, blank, 0)

    def cover_row(tile, carry):
        points = points_of(spots_along((1, frame), 1), zoom, frac, offset, 1, tile, ratio)
        col_cover[pl.ds(tile, 1), :] = cover_of(points, source)
        return carry

    lax.fori_loop(0, all_tiles, cover_row, 0, unroll=8)

    cover_sum[...] = jnp.zeros_like(cover_sum)

    def add_cover(slot, carry):
        code = codes[slot]

        @pl.when(code >= 0)
        def _():
            tile, band = code // bands, code % bands
            points = points_of(
                spots_along((BAND, frame), 0, band * BAND), zoom, frac, offset, 0, tile, ratio
            )
            cover_sum[band] += cover_of(points, source) * col_cover[pl.ds(tile, 1), :]

        return carry

    lax.fori_loop(0, devices * capacity, add_cover, 0)

    parts[...] = jnp.zeros_like(parts)
    for j in range(tiles):
        tile = me * tiles + j
        spots = spots_along((frame, frame), 0)
        y = coords(spots, frame)
        cover = cover_of(points_of(spots, zoom, frac, offset, 0, tile, ratio), source)
        level = frames[j].astype(jnp.float32)
        columns = col_cover[pl.ds(tile, 1), :]
        weighted = (cover, cover * y, cover * y * y)
        for power, image in enumerate((None, level, level * level)):
            block = (sec + 1 + power) % sections
            place = block * all_tiles + tile
            for a, rows in enumerate(weighted):
                total = rows if image is None else rows * image
                parts[a, pl.ds(place, 1), :] = columns * jnp.sum(total, axis=0, keepdims=True)
    total = exact_dot(feature_rows(frame, MOMENT_ROWS[0]), parts[0])
    for a in (1, 2):
        total += exact_dot(feature_rows(frame, MOMENT_ROWS[a]), parts[a])
    base[...] = total


def blend_kernel(sizes, codes, incoming, cover_sum, grid, total):
    tiles, bands, frame, source, capacity, devices = sizes
    total[...] = jnp.zeros_like(total)

    def add(slot, carry):
        code = codes[slot]

        @pl.when(code >= 0)
        def _():
            total[code % bands] += incoming[slot].astype(jnp.float32)

        return carry

    lax.fori_loop(0, devices * capacity, add, 0)
    grid[...] = (total[...] / (1.0 + cover_sum[...])).astype(jnp.bfloat16)


GRADIENT_ROWS = ({0: 0, 1: 1}, {2: 0}, {3: 0, 4: 1}, {5: 0})


def gradient_kernel(
    sizes,
    zoom,
    frac,
    offset,
    codes,
    incoming,
    from_next,
    top_grid,
    col_cover,
    base,
    payload,
    above,
    parts,
):
    tiles, bands, frame, source, capacity, devices = sizes
    sec = lax.axis_index("sec")
    sections = lax.axis_size("sec")
    all_tiles = tiles * devices
    ratio = frame / source

    @pl.when(sec == sections - 1)
    def _():
        above[...] = top_grid[...].astype(jnp.float32)

    @pl.when(sec != sections - 1)
    def _():
        above[...] = from_next[...].astype(jnp.float32)

    parts[...] = jnp.zeros_like(parts)

    def add(slot, carry):
        code = codes[slot]

        @pl.when(code >= 0)
        def _():
            tile, band = code // bands, code % bands
            spots = spots_along((BAND, frame), 0, band * BAND)
            cover = cover_of(points_of(spots, zoom, frac, offset, 0, tile, ratio), source)
            lifted = cover * coords(spots, frame)
            level = incoming[slot].astype(jnp.float32)
            error = above[band] - level
            product = error * level
            place = sec * all_tiles + tile
            for part, term in enumerate(
                (cover * error, lifted * error, cover * product, lifted * product)
            ):
                parts[part, pl.ds(place, 1), :] += jnp.sum(term, axis=0, keepdims=True)

        return carry

    lax.fori_loop(0, devices * capacity, add, 0)
    first = pl.multiple_of(sec * all_tiles, all_tiles)
    total = base[...]
    for part, wanted in enumerate(GRADIENT_ROWS):
        parts[part, pl.ds(first, all_tiles), :] *= col_cover[...]
        total += exact_dot(feature_rows(frame, wanted), parts[part])
    payload[...] = jnp.broadcast_to(total[None], payload.shape)


def solve_kernel(sizes, received, corrections):
    tiles, bands, frame, source, capacity, devices = sizes
    sec, me = lax.axis_index("sec"), lax.axis_index("tile")
    sections = lax.axis_size("sec")
    all_tiles = tiles * devices
    lanes = sections * all_tiles
    lane = lax.broadcasted_iota(jnp.int32, (ROWS, lanes), 1)
    within = lane % all_tiles
    area = frame * frame

    gradients = jnp.zeros((ROWS, lanes), jnp.float32)
    moments = [jnp.zeros((ROWS, lanes), jnp.float32) for _ in range(3)]
    for s in range(sections):
        own = received[s * devices]
        for t in range(1, devices):
            own += received[s * devices + t]
        here = lane // all_tiles == s
        gradients = jnp.where(here, own, gradients)
        for power in range(3):
            shift = ((sections - 1 - power) * all_tiles) % lanes
            moved = pltpu.roll(own, shift, 1) if shift else own
            moments[power] = jnp.where(here, moved, moments[power])
    gradients = gradients * (1.0 / area)
    moments = [m * (1.0 / area) for m in moments]

    where = ((0, 1, 2), (1, 3, 4), (2, 4, 5))
    row = lax.broadcasted_iota(jnp.int32, (ROWS, lanes), 0)

    def entry(f, g):
        kind = moments[(f >= 3) + (g >= 3)]
        index = where[f % 3][g % 3]
        return kind[index : index + 1]

    def stacked(rows):
        result = jnp.zeros((ROWS, lanes), jnp.float32)
        for f, value in enumerate(rows):
            result = jnp.where(row == f, value, result)
        return result

    normal = [stacked([entry(f, g) for f in range(6)]) for g in range(6)]
    diagonal = stacked([entry(f, f) for f in range(6)])
    precond = 1.0 / (diagonal + 4.0 * COUPLING)

    def total(values):
        return jnp.sum(jnp.sum(values, axis=1, keepdims=True), axis=0, keepdims=True)

    def operator(vector):
        beside = jnp.where(within < all_tiles - 1, pltpu.roll(vector, lanes - 1, 1), 0.0)
        beside += jnp.where(within > 0, pltpu.roll(vector, 1, 1), 0.0)
        upward = pltpu.roll(vector, lanes - all_tiles, 1)
        beside += jnp.where(lane < lanes - all_tiles, upward, 0.0)
        beside += jnp.where(lane >= all_tiles, pltpu.roll(vector, all_tiles, 1), 0.0)
        image = COUPLING * (4.0 * vector - beside)
        for g in range(6):
            image += normal[g] * vector[g : g + 1]
        return image

    answer = jnp.zeros((ROWS, lanes), jnp.float32)
    residual = gradients
    scaled = precond * residual
    direction = scaled
    current = total(residual * scaled)
    for step in range(ITERS):
        image = operator(direction)
        alpha = current / total(direction * image)
        answer = answer + alpha * direction
        if step + 1 < ITERS:
            residual = residual - alpha * image
            scaled = precond * residual
            following = total(residual * scaled)
            direction = scaled + following / current * direction
            current = following

    first = sec * all_tiles + me * tiles
    chosen = lax.broadcasted_iota(jnp.int32, (ROWS, lanes), 0) + first == lane
    own = exact_dot(chosen.astype(jnp.float32), answer)
    corrections[...] = own[:tiles, :6]


def shards(patches, zoom, frac, offset, owner, top_grid):
    _, tiles, source, _ = patches.shape
    frame = top_grid.shape[1]
    devices, sections = lax.axis_size("tile"), lax.axis_size("sec")
    bands = frame // BAND
    capacity = max(2, 2 * tiles * bands // devices)
    slots = devices * capacity
    all_tiles = tiles * devices
    lanes = sections * all_tiles
    sizes = (tiles, bands, frame, source, capacity, devices)
    place = (zoom[0], frac[0], offset[0])
    routes = jnp.transpose(owner, (0, 2, 3, 1))[0]

    whole = lambda *shape: pl.BlockSpec(shape, lambda i: (0,) * len(shape))
    outgoing, frames = pl.pallas_call(
        functools.partial(render_kernel, sizes),
        name="render",
        grid=(tiles,),
        in_specs=[SMEM] * 4 + [pl.BlockSpec((1, source, source), lambda i: (i, 0, 0))],
        out_specs=[
            whole(slots, BAND, frame),
            pl.BlockSpec((1, frame, frame), lambda i: (i, 0, 0)),
        ],
        out_shape=[
            jax.ShapeDtypeStruct((slots, BAND, frame), jnp.bfloat16),
            jax.ShapeDtypeStruct((tiles, frame, frame), jnp.bfloat16),
        ],
        scratch_shapes=[pltpu.SMEM((devices,), jnp.int32)],
        compiler_params=params(24),
        cost_estimate=cost(800_000_000, 4 << 20),
    )(*place, routes, patches[0])

    incoming = lax.all_to_all(
        outgoing.reshape(devices, capacity, BAND, frame),
        "tile",
        split_axis=0,
        concat_axis=0,
        tiled=True,
    ).reshape(slots, BAND, frame)

    base, cover_sum, col_cover, codes = pl.pallas_call(
        functools.partial(moment_kernel, sizes),
        name="moments",
        in_specs=[SMEM] * 4 + [VMEM],
        out_specs=[VMEM, VMEM, VMEM, SMEM],
        out_shape=[
            jax.ShapeDtypeStruct((ROWS, lanes), jnp.float32),
            jax.ShapeDtypeStruct((bands, BAND, frame), jnp.float32),
            jax.ShapeDtypeStruct((all_tiles, frame), jnp.float32),
            jax.ShapeDtypeStruct((slots + 1,), jnp.int32),
        ],
        scratch_shapes=[pltpu.VMEM((3, lanes, frame), jnp.float32)],
        compiler_params=params(24),
        cost_estimate=cost(20_000_000, 1 << 20),
    )(*place, routes, frames)

    grid = pl.pallas_call(
        functools.partial(blend_kernel, sizes),
        name="blend",
        in_specs=[SMEM, VMEM, VMEM],
        out_specs=VMEM,
        out_shape=jax.ShapeDtypeStruct((bands, BAND, frame), jnp.bfloat16),
        scratch_shapes=[pltpu.VMEM((bands, BAND, frame), jnp.float32)],
        compiler_params=params(24),
        cost_estimate=cost(1_000_000, 2 << 20),
    )(codes, incoming, cover_sum)

    from_next = lax.ppermute(grid, "sec", [(i, (i - 1) % sections) for i in range(sections)])

    payload = pl.pallas_call(
        functools.partial(gradient_kernel, sizes),
        name="gradient",
        in_specs=[SMEM] * 4 + [VMEM] * 5,
        out_specs=VMEM,
        out_shape=jax.ShapeDtypeStruct((sections * devices, ROWS, lanes), jnp.float32),
        scratch_shapes=[
            pltpu.VMEM((bands, BAND, frame), jnp.float32),
            pltpu.VMEM((4, lanes, frame), jnp.float32),
        ],
        compiler_params=params(24),
        cost_estimate=cost(8_000_000, 2 << 20),
    )(
        *place,
        codes,
        incoming,
        from_next,
        top_grid.reshape(bands, BAND, frame),
        col_cover,
        base,
    )

    received = lax.all_to_all(
        payload, ("sec", "tile"), split_axis=0, concat_axis=0, tiled=True
    )

    corrections = pl.pallas_call(
        functools.partial(solve_kernel, sizes),
        name="solve",
        in_specs=[VMEM],
        out_specs=VMEM,
        out_shape=jax.ShapeDtypeStruct((tiles, 6), jnp.float32),
        compiler_params=params(24),
        cost_estimate=cost(100_000, 1 << 18),
    )(received)
    return (
        grid.reshape(1, 1, frame, frame),
        jnp.transpose(corrections[None], (2, 0, 1)),
    )


def solution(mesh):
    placed = (
        P("sec", "tile", None, None),
        P("sec", None, None),
        P("sec", None, None),
        P("sec", None, None),
        P("sec", None, None, None),
        P("tile", None, None),
    )
    return jax.shard_map(
        shards,
        mesh=mesh,
        in_specs=placed,
        out_specs=(P("sec", "tile", None, None), P(None, "sec", "tile")),
        check_vma=False,
    )
```

time: 293 us -> 70 us (0.24); the launches traced: 288 us -> 68.7 us
  blocking collectives: 129 us -> 12.5 us
  matrix products: 60.7 us -> 0 us
  Pallas kernels: 0 us -> 23.2 us
  starting transfers between devices: 29.9 us -> 8.86 us
  other arithmetic: 16.9 us -> 0 us
  waiting for transfers between devices: 32.1 us -> 19.2 us
  local copies, waits for them, and re-layouts: 13.6 us -> 4.33 us
  between operations: 5.29 us -> 0.7 us
    psum x3 -> x0, blocking collectives: 129 us -> none  [the longest x2 84.8 us: precond_norm(): return lax.psum(jnp.sum(residual * scaled), ('sec', 'tile'))]
    dot_general x12 -> x0, matrix products: 60.7 us -> none  [the longest x1 26.8 us: moments(): jnp.einsum('bfrq,bgrq->bfg', weighted, features, precision=lax.Precision....]
    pallas_call x0 -> x5, Pallas kernels: none -> 23.2 us  [the longest x1 10.3 us: shards(): pl.pallas_call(functools.partial(moment_kernel, sizes), name='moments', i...]
    ppermute x9 -> x1, starting transfers between devices: 18.9 us -> 2.41 us  [shards(): lax.ppermute(grid, 'sec', [(i, (i - 1) % sections) for i in range(section...]
    all_to_all x0 -> x1, blocking collectives: none -> 12.5 us  [shards(): lax.all_to_all(payload, ('sec', 'tile'), split_axis=0, concat_axis=0, til...]
    ppermute x9 -> x1, waiting for transfers between devices: 14 us -> 2.95 us  [shards(): lax.ppermute(grid, 'sec', [(i, (i - 1) % sections) for i in range(section...]
    another operation x8 -> x0, local copies, waits for them, and re-layouts: 4.91 us -> none
    all_to_all x2 -> x1, starting transfers between devices: 11 us -> 6.45 us  [shards(): lax.all_to_all(outgoing.reshape(devices, capacity, BAND, frame), 'tile',...]
  transfers between devices with their start and end apart: 11 -> 2, of which waited for: 6 -> 2; matrix products, arithmetic and copies ran while one was open for 14% -> 0% of each run, Pallas kernels for 0% -> 15%
where the time goes in v1:
time: 70 us; the launch traced here: 68.7 us
  Pallas kernels  23.2 us (33%)
  waiting for transfers between devices  19.2 us (27%)
  blocking collectives  12.5 us (18%)
  starting transfers between devices  8.86 us (13%)
  local copies, waits for them, and re-layouts  4.33 us (6%)
    all_to_all x1, waiting for transfers between devices, shards(): lax.all_to_all(outgoing.reshape(devices, capacity, BAND, frame), 'tile',...  16.2 us
    all_to_all x1, blocking collectives, shards(): lax.all_to_all(payload, ('sec', 'tile'), split_axis=0, concat_axis=0, til...  12.5 us
    pallas_call x1, Pallas kernels, shards(): pl.pallas_call(functools.partial(moment_kernel, sizes), name='moments', i...  10.3 us
    all_to_all x1, starting transfers between devices, shards(): lax.all_to_all(outgoing.reshape(devices, capacity, BAND, frame), 'tile',...  6.45 us
    pallas_call x1, Pallas kernels, shards(): pl.pallas_call(functools.partial(gradient_kernel, sizes), name='gradient'...  4.39 us
    unnamed x20, local copies, waits for them, and re-layouts  4.33 us
    pallas_call x1, Pallas kernels, shards(): pl.pallas_call(functools.partial(render_kernel, sizes), name='render', gr...  3.92 us
    pallas_call x1, Pallas kernels, shards(): pl.pallas_call(functools.partial(blend_kernel, sizes), name='blend', in_s...  3.3 us
  transfers between devices with their start and end apart: 2, of which 2 were waited for; matrix products, arithmetic and copies ran while one was open for 0% of the time, Pallas kernels for 15%

profile of v1, /device:TPU:0, one launch (start us, length us, event | category | flops | bytes accessed | tf_op | source)
XLA Modules:
  0.0 68.7 jit_solution(9748243071841358711)
XLA Ops:
  0.6 0.0 copy-start.1
  0.6 0.7 %copy-done.1 = s32[1,32,16,1]{1,3,2,0:T(1,128)S(1)} copy-done((s32[1,32,16,1]{1,3,2,0:T(1,128)S(1)}, s32[1,32,16,1]{1,3,2,0:T(1,128)}, u32[]{:S(2)}) %copy-start.1) | copy-done | bytes 2072
  1.3 0.0 copy-start.3
  1.3 0.7 copy-done.3
  2.0 0.0 copy-start.5
  2.0 0.7 copy-done.5
  2.7 0.0 copy-start.7
  2.7 0.7 copy-done.7
  3.4 0.0 copy-start.9
  3.4 1.6 %copy-done.9 = bf16[1,4,512,512]{3,2,1,0:T(8,128)(2,1)S(1)} copy-done((bf16[1,4,512,512]{3,2,1,0:T(8,128)(2,1)S(1)}, bf16[1,4,512,512]{3,2,1,0:T(8,128)(2,1)}, u32[]{:S(2)}) %copy-start.9) | copy-done | bytes 2097176
  5.0 0.0 copy-start.2
  5.0 0.0 copy-start.4
  5.0 0.0 copy-start.6
  5.0 0.0 copy-start.8
  5.0 3.9 %render.1 = (bf16[128,16,256]{2,1,0:T(8,128)(2,1)}, bf16[4,256,256]{2,1,0:T(8,128)(2,1)S(1)}) custom-call(f32[2,32]{1,0:T(2,128)S(1)} %bitcast.21, f32[2,32]{1,0:T(2,128)S(1)} %bitcast.24, s32[2,32]{1,0:T(2,128)S(1)} %bitcast.27, s32[16,1,32]{2,1,0:T(1,128)S(1)} %bitcast.19, bf16[4,512,512]{2,1,0:T(8,128)(2,1)S(1)} %bitcast.30), custom_call_target="tpu_custom_call" | custom-call | flops 800000000 | bytes 4194304 | tf_op jit(solution)/shard_map/render/pallas_call | solution.py:360
  8.9 0.0 copy-start
  8.9 6.5 %all-to-all-start = ((bf16[8,16,16,256]{3,2,1,0:T(8,128)(2,1)}), bf16[8,16,16,256]{3,2,1,0:T(8,128)(2,1)S(1)}, u32[]{:S(2)}, u32[]{:S(2)}) async-start(bf16[8,16,16,256]{3,2,1,0:T(8,128)(2,1)} %bitcast.9), calls=%async_computation | async-start | bytes 2097152 | tf_op jit(solution)/shard_map/all_to_all | solution.py:378
  15.3 0.0 copy-done.2
  15.4 0.0 copy-done.4
  15.4 0.0 copy-done.6
  15.4 0.0 copy-done.8
  15.4 10.3 %moments.1 = (f32[8,128]{1,0:T(8,128)S(1)}, f32[16,16,256]{2,1,0:T(8,128)S(1)}, f32[32,256]{1,0:T(8,128)S(1)}, s32[129]{0:T(256)S(1)}) custom-call(f32[2,32]{1,0:T(2,128)S(1)} %bitcast.22, f32[2,32]{1,0:T(2,128)S(1)} %bitcast.25, s32[2,32]{1,0:T(2,128)S(1)} %bitcast.28, s32[16,1,32]{2,1,0:T(1,128)S(1)} %bitcast.20, ...), custom_call_target="tpu_custom_call" | custom-call | flops 20000000 | bytes 1048576 | tf_op jit(solution)/shard_map/moments/pallas_call | solution.py:386
  25.7 16.2 %all-to-all-done = bf16[8,16,16,256]{3,2,1,0:T(8,128)(2,1)S(1)} async-done(((bf16[8,16,16,256]{3,2,1,0:T(8,128)(2,1)}), bf16[8,16,16,256]{3,2,1,0:T(8,128)(2,1)S(1)}, u32[]{:S(2)}, u32[]{:S(2)}) %all-to-all-start) | async-done | bytes 1048608 | tf_op jit(solution)/shard_map/all_to_all | solution.py:378
  41.9 3.3 %blend.1 = bf16[16,16,256]{2,1,0:T(8,128)(2,1)} custom-call(s32[129]{0:T(256)S(1)} %get-tuple-element.9.codes, bf16[128,16,256]{2,1,0:T(8,128)(2,1)S(1)} %bitcast.16, f32[16,16,256]{2,1,0:T(8,128)S(1)} %get-tuple-element.11.cover_sum), custom_call_target="tpu_custom_call" | custom-call | flops 1000000 | bytes 2097152 | tf_op jit(solution)/shard_map/blend/pallas_call | solution.py:402
  45.2 2.4 %collective-permute-start = (bf16[16,16,256]{2,1,0:T(8,128)(2,1)}, bf16[16,16,256]{2,1,0:T(8,128)(2,1)S(1)}, u32[]{:S(2)}, u32[]{:S(2)}) collective-permute-start(bf16[16,16,256]{2,1,0:T(8,128)(2,1)} %blend.1), channel_id=1, source_target_pairs={{0,24},{8,0},{16,8},{24,16},{1,25},{9,1},{17,9},{25,17},{2,26},{10... | collective-permute-start | bytes 393224 | tf_op jit(solution)/shard_map/ppermute | solution.py:413
  47.7 2.9 %collective-permute-done.from_next = bf16[16,16,256]{2,1,0:T(8,128)(2,1)S(1)} collective-permute-done((bf16[16,16,256]{2,1,0:T(8,128)(2,1)}, bf16[16,16,256]{2,1,0:T(8,128)(2,1)S(1)}, u32[]{:S(2)}, u32[]{:S(2)}) %collective-permute-start) | collective-permute-done | bytes 131104 | tf_op jit(solution)/shard_map/ppermute | solution.py:413
  50.6 0.0 copy-done
  50.6 4.4 %gradient.1 = f32[32,8,128]{2,1,0:T(8,128)S(1)} custom-call(f32[2,32]{1,0:T(2,128)S(1)} %bitcast.23, f32[2,32]{1,0:T(2,128)S(1)} %bitcast.26, s32[2,32]{1,0:T(2,128)S(1)} %bitcast.29, s32[129]{0:T(256)S(1)} %get-tuple-element.9.codes, bf16[128,16,256]{2,1,0:T(8,128)(2,1)S(1)} %bitcast.17, bf16[16,16,256]{2,1,0:T(8,128)(2,1)S(1)} %collective-permute-done.from_next, ...), custom_call_target="tpu_custom_call" | custom-call | flops 8000000 | bytes 2097152 | tf_op jit(solution)/shard_map/gradient/pallas_call | solution.py:415
  55.0 12.5 %all_to_all.10.received = f32[32,8,128]{2,1,0:T(8,128)S(1)} all-to-all(f32[32,8,128]{2,1,0:T(8,128)S(1)} %gradient.1), channel_id=1, replica_groups=mesh['sec'=4,'tile'=8] {'sec','tile'}, dimensions={0} | all-to-all | bytes 262144 | tf_op jit(solution)/shard_map/all_to_all | solution.py:437
  67.5 1.2 %solve.1 = f32[4,6]{1,0:T(4,128)} custom-call(f32[32,8,128]{2,1,0:T(8,128)S(1)} %all_to_all.10.received), custom_call_target="tpu_custom_call" | custom-call | flops 100000 | bytes 262144 | tf_op jit(solution)/shard_map/solve/pallas_call | solution.py:441
Async XLA Ops:
  0.6 0.7 %copy-start.1 = (s32[1,32,16,1]{1,3,2,0:T(1,128)S(1)}, s32[1,32,16,1]{1,3,2,0:T(1,128)}, u32[]{:S(2)}) copy-start(s32[1,32,16,1]{1,3,2,0:T(1,128)} %param.10) | copy-start | bytes 6148
  1.3 0.7 copy-start.3
  2.0 0.7 copy-start.5
  2.7 0.7 copy-start.7
  3.4 1.6 %copy-start.9 = (bf16[1,4,512,512]{3,2,1,0:T(8,128)(2,1)S(1)}, bf16[1,4,512,512]{3,2,1,0:T(8,128)(2,1)}, u32[]{:S(2)}) copy-start(bf16[1,4,512,512]{3,2,1,0:T(8,128)(2,1)} %param.6) | copy-start | bytes 6291460
  5.0 10.4 %copy-start.2 = (s32[1,32,16,1]{1,3,2,0:T(1,128)S(1)}, s32[1,32,16,1]{1,3,2,0:T(1,128)}, u32[]{:S(2)}) copy-start(s32[1,32,16,1]{1,3,2,0:T(1,128)} %param.10) | copy-start | bytes 6148
  5.0 10.4 %copy-start.4 = (f32[1,2,32]{2,1,0:T(2,128)S(1)}, f32[1,2,32]{2,1,0:T(2,128)}, u32[]{:S(2)}) copy-start(f32[1,2,32]{2,1,0:T(2,128)} %param.7) | copy-start | bytes 772
  5.0 10.4 %copy-start.6 = (f32[1,2,32]{2,1,0:T(2,128)S(1)}, f32[1,2,32]{2,1,0:T(2,128)}, u32[]{:S(2)}) copy-start(f32[1,2,32]{2,1,0:T(2,128)} %param.8) | copy-start | bytes 772
  5.0 10.4 %copy-start.8 = (s32[1,2,32]{2,1,0:T(2,128)S(1)}, s32[1,2,32]{2,1,0:T(2,128)}, u32[]{:S(2)}) copy-start(s32[1,2,32]{2,1,0:T(2,128)} %param.9) | copy-start | bytes 772
  8.9 41.7 %copy-start = (bf16[1,256,256]{2,1,0:T(8,128)(2,1)S(1)}, bf16[1,256,256]{2,1,0:T(8,128)(2,1)}, u32[]{:S(2)}) copy-start(bf16[1,256,256]{2,1,0:T(8,128)(2,1)} %param.11) | copy-start | bytes 393220
  8.9 33.0 %all-to-all-start = ((bf16[8,16,16,256]{3,2,1,0:T(8,128)(2,1)}), bf16[8,16,16,256]{3,2,1,0:T(8,128)(2,1)S(1)}, u32[]{:S(2)}, u32[]{:S(2)}) async-start(bf16[8,16,16,256]{3,2,1,0:T(8,128)(2,1)} %bitcast.9), calls=%async_computation | async-start | bytes 2097152 | tf_op jit(solution)/shard_map/all_to_all | solution.py:378
  45.2 5.4 %collective-permute-start = (bf16[16,16,256]{2,1,0:T(8,128)(2,1)}, bf16[16,16,256]{2,1,0:T(8,128)(2,1)S(1)}, u32[]{:S(2)}, u32[]{:S(2)}) collective-permute-start(bf16[16,16,256]{2,1,0:T(8,128)(2,1)} %blend.1), channel_id=1, source_target_pairs={{0,24},{8,0},{16,8},{24,16},{1,25},{9,1},{17,9},{25,17},{2,26},{10... | collective-permute-start | bytes 393224 | tf_op jit(solution)/shard_map/ppermute | solution.py:413

commit v2 on v1

--- a/solution.py
+++ b/solution.py
@@ -1,4 +1,5 @@
 import functools
+import math
 
 import jax
 import jax.numpy as jnp
@@ -12,6 +13,7 @@
 COUPLING = 0.25
 LANES = 128
 ROWS = 8
+ANY = pl.BlockSpec(memory_space=pl.ANY)
 SMEM = pl.BlockSpec(memory_space=pltpu.SMEM)
 VMEM = pl.BlockSpec(memory_space=pltpu.VMEM)
 
@@ -55,39 +57,77 @@
     return (spots - (frame - 1) / 2.0) / (frame / 2.0)
 
 
-def render_kernel(sizes, zoom, frac, offset, owner, patch, outgoing, frames, named):
+def render_kernel(
+    sizes,
+    zoom_in,
+    frac_in,
+    offset_in,
+    owner_in,
+    patches_in,
+    outgoing,
+    frames_out,
+    zoom,
+    frac,
+    offset,
+    owner,
+    patches,
+    frames,
+    named,
+    small_sems,
+    patch_sems,
+    frame_sem,
+    band_sem,
+):
     tiles, bands, frame, source, capacity, devices = sizes
-    step = pl.program_id(0)
-    tile = lax.axis_index("tile") * tiles + step
-
-    @pl.when(step == 0)
-    def _():
-        for g in range(devices):
-            named[g] = 0
-        outgoing[...] = jnp.zeros_like(outgoing)
-
+    first = lax.axis_index("tile") * tiles
     ratio = frame / source
-    row_points = points_of(spots_along((frame, LANES), 0), zoom, frac, offset, 0, tile, ratio)
-    row_weights = jnp.concatenate(
-        [
-            hat_weight(row_points - spots_along((frame, LANES), 1, first)).astype(jnp.bfloat16)
-            for first in range(0, source, LANES)
-        ],
-        axis=1,
-    )
-    col_points = points_of(spots_along((ROWS, frame), 1), zoom, frac, offset, 1, tile, ratio)
-    col_points = jnp.broadcast_to(col_points[:1], (source, frame))
-    col_weights = hat_weight(col_points - spots_along((source, frame), 0)).astype(jnp.bfloat16)
-    halfway = jnp.dot(row_weights, patch[0], preferred_element_type=jnp.float32)
-    rendered = jnp.dot(
-        halfway.astype(jnp.bfloat16), col_weights, preferred_element_type=jnp.float32
-    ).astype(jnp.bfloat16)
-    frames[0] = rendered
-    for band in range(bands):
-        target = owner[band, 0, tile]
-        slot = named[target]
-        named[target] = slot + 1
-        outgoing[target * capacity + slot] = rendered[band * BAND : (band + 1) * BAND]
+    fetched = [
+        pltpu.make_async_copy(patches_in.at[j], patches.at[j], patch_sems.at[j])
+        for j in range(tiles)
+    ]
+    small = [
+        pltpu.make_async_copy(there, here, small_sems.at[k])
+        for k, (there, here) in enumerate(
+            ((zoom_in, zoom), (frac_in, frac), (offset_in, offset), (owner_in, owner))
+        )
+    ]
+    for copy in small + fetched:
+        copy.start()
+    for g in range(devices):
+        named[g] = 0
+    for copy in small:
+        copy.wait()
+    for j in range(tiles):
+        tile = first + j
+        row_points = points_of(spots_along((frame, LANES), 0), zoom, frac, offset, 0, tile, ratio)
+        row_weights = jnp.concatenate(
+            [
+                hat_weight(row_points - spots_along((frame, LANES), 1, p)).astype(jnp.bfloat16)
+                for p in range(0, source, LANES)
+            ],
+            axis=1,
+        )
+        col_points = points_of(spots_along((ROWS, frame), 1), zoom, frac, offset, 1, tile, ratio)
+        col_points = jnp.broadcast_to(col_points[:1], (source, frame))
+        col_weights = hat_weight(col_points - spots_along((source, frame), 0)).astype(jnp.bfloat16)
+        fetched[j].wait()
+        halfway = jnp.dot(row_weights, patches[j], preferred_element_type=jnp.float32)
+        rendered = jnp.dot(
+            halfway.astype(jnp.bfloat16), col_weights, preferred_element_type=jnp.float32
+        ).astype(jnp.bfloat16)
+        for band in range(bands):
+            row = j * bands + band
+            frames[row] = rendered[band * BAND : (band + 1) * BAND]
+            target = owner[band, 0, tile]
+            slot = named[target]
+            named[target] = slot + 1
+            pltpu.make_async_copy(
+                frames.at[row], outgoing.at[target * capacity + slot], band_sem
+            ).start()
+    kept = pltpu.make_async_copy(frames, frames_out, frame_sem)
+    kept.start()
+    pltpu.make_async_copy(frames, outgoing.at[pl.ds(0, tiles * bands)], band_sem).wait()
+    kept.wait()
 
 
 def feature_rows(frame, wanted):
@@ -112,8 +152,11 @@
     frames,
     base,
     cover_sum,
+    slot_cover,
+    slot_lines,
+    slot_bands,
+    codes,
     col_cover,
-    codes,
     parts,
 ):
     tiles, bands, frame, source, capacity, devices = sizes
@@ -148,12 +191,27 @@
 
     cover_sum[...] = jnp.zeros_like(cover_sum)
 
-    def add_cover(slot, carry):
+    def describe(slot, carry):
         code = codes[slot]
-
-        @pl.when(code >= 0)
+        used = code >= 0
+        code = jnp.maximum(code, 0)
+        tile, band = code // bands, code % bands
+        slot_bands[slot] = jnp.where(used, band, bands)
+        here = pl.ds(slot, 1)
+        row = jnp.zeros((1, LANES), jnp.float32)
+        start = (band * BAND).astype(jnp.float32)
+        scale = row + zoom[0, tile] * ratio
+        slot_lines[0, here, :] = 1.0 / scale
+        slot_lines[1, here, :] = (
+            row + start - offset[0, tile].astype(jnp.float32) - frac[0, tile]
+        ) / scale
+        slot_lines[2, here, :] = coords(row + start, frame)
+        place = jnp.where(used, sec * all_tiles + tile, -1)
+        slot_lines[3, here, :] = row + place.astype(jnp.float32)
+        slot_cover[here, :] = col_cover[pl.ds(tile, 1), :]
+
+        @pl.when(used)
         def _():
-            tile, band = code // bands, code % bands
             points = points_of(
                 spots_along((BAND, frame), 0, band * BAND), zoom, frac, offset, 0, tile, ratio
             )
@@ -161,7 +219,7 @@
 
         return carry
 
-    lax.fori_loop(0, devices * capacity, add_cover, 0)
+    lax.fori_loop(0, devices * capacity, describe, 0)
 
     parts[...] = jnp.zeros_like(parts)
     for j in range(tiles):
@@ -169,7 +227,7 @@
         spots = spots_along((frame, frame), 0)
         y = coords(spots, frame)
         cover = cover_of(points_of(spots, zoom, frac, offset, 0, tile, ratio), source)
-        level = frames[j].astype(jnp.float32)
+        level = frames[j * bands : (j + 1) * bands].reshape(frame, frame).astype(jnp.float32)
         columns = col_cover[pl.ds(tile, 1), :]
         weighted = (cover, cover * y, cover * y * y)
         for power, image in enumerate((None, level, level * level)):
@@ -184,21 +242,18 @@
     base[...] = total
 
 
-def blend_kernel(sizes, codes, incoming, cover_sum, grid, total):
+def blend_kernel(sizes, unroll, slot_bands, incoming, cover_sum, grid, total):
     tiles, bands, frame, source, capacity, devices = sizes
     total[...] = jnp.zeros_like(total)
 
-    def add(slot, carry):
-        code = codes[slot]
-
-        @pl.when(code >= 0)
-        def _():
-            total[code % bands] += incoming[slot].astype(jnp.float32)
-
+    def add(group, carry):
+        for k in range(unroll):
+            slot = group * unroll + k
+            total[slot_bands[slot]] += incoming[slot].astype(jnp.float32)
         return carry
 
-    lax.fori_loop(0, devices * capacity, add, 0)
-    grid[...] = (total[...] / (1.0 + cover_sum[...])).astype(jnp.bfloat16)
+    lax.fori_loop(0, devices * capacity // unroll, add, 0)
+    grid[...] = (total[:bands] / (1.0 + cover_sum[...])).astype(jnp.bfloat16)
 
 
 GRADIENT_ROWS = ({0: 0, 1: 1}, {2: 0}, {3: 0, 4: 1}, {5: 0})
@@ -206,61 +261,81 @@
 
 def gradient_kernel(
     sizes,
-    zoom,
-    frac,
-    offset,
-    codes,
+    unroll,
+    slot_bands,
     incoming,
     from_next,
     top_grid,
-    col_cover,
+    slot_cover,
+    slot_lines,
     base,
     payload,
     above,
-    parts,
+    sums,
 ):
     tiles, bands, frame, source, capacity, devices = sizes
     sec = lax.axis_index("sec")
-    sections = lax.axis_size("sec")
-    all_tiles = tiles * devices
-    ratio = frame / source
-
-    @pl.when(sec == sections - 1)
+    slots = devices * capacity
+    lanes = base.shape[1]
+
+    @pl.when(sec == lax.axis_size("sec") - 1)
     def _():
-        above[...] = top_grid[...].astype(jnp.float32)
-
-    @pl.when(sec != sections - 1)
+        above[:bands] = top_grid[...].astype(jnp.float32)
+
+    @pl.when(sec != lax.axis_size("sec") - 1)
     def _():
-        above[...] = from_next[...].astype(jnp.float32)
-
-    parts[...] = jnp.zeros_like(parts)
-
-    def add(slot, carry):
-        code = codes[slot]
-
-        @pl.when(code >= 0)
-        def _():
-            tile, band = code // bands, code % bands
-            spots = spots_along((BAND, frame), 0, band * BAND)
-            cover = cover_of(points_of(spots, zoom, frac, offset, 0, tile, ratio), source)
-            lifted = cover * coords(spots, frame)
+        above[:bands] = from_next[...].astype(jnp.float32)
+
+    above[bands] = jnp.zeros((BAND, frame), jnp.float32)
+    spots = spots_along((BAND, LANES), 0)
+    raised = spots * (2.0 / frame)
+
+    def add(group, carry):
+        for k in range(unroll):
+            slot = group * unroll + k
+            here = pl.ds(slot, 1)
+            points = spots * slot_lines[0, here, :] + slot_lines[1, here, :]
+            cover = cover_of(points, source)
+            lifted = cover * (raised + slot_lines[2, here, :])
             level = incoming[slot].astype(jnp.float32)
-            error = above[band] - level
+            error = above[slot_bands[slot]] - level
             product = error * level
-            place = sec * all_tiles + tile
-            for part, term in enumerate(
-                (cover * error, lifted * error, cover * product, lifted * product)
-            ):
-                parts[part, pl.ds(place, 1), :] += jnp.sum(term, axis=0, keepdims=True)
-
+            rows = pl.ds(pl.multiple_of(slot * ROWS, ROWS), ROWS)
+            for half in range(frame // LANES):
+                part = slice(half * LANES, (half + 1) * LANES)
+                for kind, (weight, value) in enumerate(
+                    ((cover, error), (lifted, error), (cover, product), (lifted, product))
+                ):
+                    term = weight * value[:, part]
+                    sums[kind, half, rows, :] = term[:ROWS] + term[ROWS:]
         return carry
 
-    lax.fori_loop(0, devices * capacity, add, 0)
-    first = pl.multiple_of(sec * all_tiles, all_tiles)
-    total = base[...]
-    for part, wanted in enumerate(GRADIENT_ROWS):
-        parts[part, pl.ds(first, all_tiles), :] *= col_cover[...]
-        total += exact_dot(feature_rows(frame, wanted), parts[part])
+    lax.fori_loop(0, slots // unroll, add, 0)
+    used = slot_lines[3] >= 0.0
+    by_slot = jnp.zeros((ROWS, slots), jnp.float32)
+    for kind, wanted in enumerate(GRADIENT_ROWS):
+        halves = []
+        for half in range(frame // LANES):
+            value = sums[kind, half, pl.ds(0, slots, stride=ROWS), :]
+            for r in range(1, ROWS):
+                value += sums[kind, half, pl.ds(r, slots, stride=ROWS), :]
+            columns = slot_cover[:, half * LANES : (half + 1) * LANES]
+            halves.append(jnp.where(used, value * columns, 0.0))
+        by_slot += exact_dot(feature_rows(frame, wanted), jnp.concatenate(halves, axis=1))
+    places = jnp.concatenate(
+        [
+            (slot_lines[3] == spots_along((slots, LANES), 1, p)).astype(jnp.float32)
+            for p in range(0, lanes, LANES)
+        ],
+        axis=1,
+    )
+    total = base[...] + lax.dot_general(
+        by_slot,
+        places,
+        (((1,), (0,)), ((), ())),
+        precision=lax.Precision.HIGHEST,
+        preferred_element_type=jnp.float32,
+    )
     payload[...] = jnp.broadcast_to(total[None], payload.shape)
 
 
@@ -356,22 +431,31 @@
     place = (zoom[0], frac[0], offset[0])
     routes = jnp.transpose(owner, (0, 2, 3, 1))[0]
 
-    whole = lambda *shape: pl.BlockSpec(shape, lambda i: (0,) * len(shape))
+    unroll = math.gcd(slots, 16)
+    rows = tiles * bands
     outgoing, frames = pl.pallas_call(
         functools.partial(render_kernel, sizes),
         name="render",
-        grid=(tiles,),
-        in_specs=[SMEM] * 4 + [pl.BlockSpec((1, source, source), lambda i: (i, 0, 0))],
-        out_specs=[
-            whole(slots, BAND, frame),
-            pl.BlockSpec((1, frame, frame), lambda i: (i, 0, 0)),
-        ],
+        in_specs=[ANY] * 5,
+        out_specs=[ANY] * 2,
         out_shape=[
             jax.ShapeDtypeStruct((slots, BAND, frame), jnp.bfloat16),
-            jax.ShapeDtypeStruct((tiles, frame, frame), jnp.bfloat16),
+            jax.ShapeDtypeStruct((rows, BAND, frame), jnp.bfloat16),
         ],
-        scratch_shapes=[pltpu.SMEM((devices,), jnp.int32)],
-        compiler_params=params(24),
+        scratch_shapes=[
+            pltpu.SMEM(place[0].shape, jnp.float32),
+            pltpu.SMEM(place[1].shape, jnp.float32),
+            pltpu.SMEM(place[2].shape, jnp.int32),
+            pltpu.SMEM(routes.shape, jnp.int32),
+            pltpu.VMEM((tiles, source, source), jnp.bfloat16),
+            pltpu.VMEM((rows, BAND, frame), jnp.bfloat16),
+            pltpu.SMEM((devices,), jnp.int32),
+            pltpu.SemaphoreType.DMA((4,)),
+            pltpu.SemaphoreType.DMA((tiles,)),
+            pltpu.SemaphoreType.DMA,
+            pltpu.SemaphoreType.DMA,
+        ],
+        compiler_params=params(58),
         cost_estimate=cost(800_000_000, 4 << 20),
     )(*place, routes, patches[0])
 
@@ -383,54 +467,59 @@
         tiled=True,
     ).reshape(slots, BAND, frame)
 
-    base, cover_sum, col_cover, codes = pl.pallas_call(
+    base, cover_sum, slot_cover, slot_lines, slot_bands = pl.pallas_call(
         functools.partial(moment_kernel, sizes),
         name="moments",
         in_specs=[SMEM] * 4 + [VMEM],
-        out_specs=[VMEM, VMEM, VMEM, SMEM],
+        out_specs=[VMEM, VMEM, VMEM, VMEM, SMEM],
         out_shape=[
             jax.ShapeDtypeStruct((ROWS, lanes), jnp.float32),
             jax.ShapeDtypeStruct((bands, BAND, frame), jnp.float32),
-            jax.ShapeDtypeStruct((all_tiles, frame), jnp.float32),
-            jax.ShapeDtypeStruct((slots + 1,), jnp.int32),
+            jax.ShapeDtypeStruct((slots, frame), jnp.float32),
+            jax.ShapeDtypeStruct((4, slots, LANES), jnp.float32),
+            jax.ShapeDtypeStruct((slots,), jnp.int32),
         ],
-        scratch_shapes=[pltpu.VMEM((3, lanes, frame), jnp.float32)],
+        scratch_shapes=[
+            pltpu.SMEM((slots + 1,), jnp.int32),
+            pltpu.VMEM((all_tiles, frame), jnp.float32),
+            pltpu.VMEM((3, lanes, frame), jnp.float32),
+        ],
         compiler_params=params(24),
         cost_estimate=cost(20_000_000, 1 << 20),
     )(*place, routes, frames)
 
     grid = pl.pallas_call(
-        functools.partial(blend_kernel, sizes),
+        functools.partial(blend_kernel, sizes, unroll),
         name="blend",
         in_specs=[SMEM, VMEM, VMEM],
         out_specs=VMEM,
         out_shape=jax.ShapeDtypeStruct((bands, BAND, frame), jnp.bfloat16),
-        scratch_shapes=[pltpu.VMEM((bands, BAND, frame), jnp.float32)],
+        scratch_shapes=[pltpu.VMEM((bands + 1, BAND, frame), jnp.float32)],
         compiler_params=params(24),
         cost_estimate=cost(1_000_000, 2 << 20),
-    )(codes, incoming, cover_sum)
+    )(slot_bands, incoming, cover_sum)
 
     from_next = lax.ppermute(grid, "sec", [(i, (i - 1) % sections) for i in range(sections)])
 
     payload = pl.pallas_call(
-        functools.partial(gradient_kernel, sizes),
+        functools.partial(gradient_kernel, sizes, unroll),
         name="gradient",
-        in_specs=[SMEM] * 4 + [VMEM] * 5,
+        in_specs=[SMEM] + [VMEM] * 6,
         out_specs=VMEM,
         out_shape=jax.ShapeDtypeStruct((sections * devices, ROWS, lanes), jnp.float32),
         scratch_shapes=[
-            pltpu.VMEM((bands, BAND, frame), jnp.float32),
-            pltpu.VMEM((4, lanes, frame), jnp.float32),
+            pltpu.VMEM((bands + 1, BAND, frame), jnp.float32),
+            pltpu.VMEM((4, frame // LANES, slots * ROWS, LANES), jnp.float32),
         ],
         compiler_params=params(24),
         cost_estimate=cost(8_000_000, 2 << 20),
     )(
-        *place,
-        codes,
+        slot_bands,
         incoming,
         from_next,
         top_grid.reshape(bands, BAND, frame),
-        col_cover,
+        slot_cover,
+        slot_lines,
         base,
     )
 

time: 70 us -> 62.2 us (0.89); the launches traced: 68.7 us -> 62 us
  local copies, waits for them, and re-layouts: 4.33 us -> 0.03 us
  Pallas kernels: 23.2 us -> 21.8 us
  waiting for transfers between devices: 19.2 us -> 17.9 us
    unnamed x20 -> x12, local copies, waits for them, and re-layouts: 4.33 us -> 0.03 us
    pallas_call x3, Pallas kernels: 11.6 us -> 9.11 us  [the longest x1 4.33 us: shards(): pl.pallas_call(functools.partial(render_kernel, sizes), name='render', in...]
    all_to_all x1, waiting for transfers between devices: 16.2 us -> 15.1 us  [shards(): lax.all_to_all(outgoing.reshape(devices, capacity, BAND, frame), 'tile',...]
    pallas_call x1, Pallas kernels: 10.3 us -> 11.5 us  [shards(): pl.pallas_call(functools.partial(moment_kernel, sizes), name='moments', i...]
  transfers between devices with their start and end apart: 2 -> 2, of which waited for: 2 -> 2; matrix products, arithmetic and copies ran while one was open for 0% -> 0% of each run, Pallas kernels for 15% -> 19%
where the time goes in v2:
time: 62.2 us; the launch traced here: 62 us
  Pallas kernels  21.8 us (35%)
  waiting for transfers between devices  17.9 us (29%)
  blocking collectives  12.6 us (20%)
  starting transfers between devices  8.93 us (14%)
  between operations  0.74 us (1%)
    all_to_all x1, waiting for transfers between devices, shards(): lax.all_to_all(outgoing.reshape(devices, capacity, BAND, frame), 'tile',...  15.1 us
    all_to_all x1, blocking collectives, shards(): lax.all_to_all(payload, ('sec', 'tile'), split_axis=0, concat_axis=0, til...  12.6 us
    pallas_call x1, Pallas kernels, shards(): pl.pallas_call(functools.partial(moment_kernel, sizes), name='moments', i...  11.5 us
    all_to_all x1, starting transfers between devices, shards(): lax.all_to_all(outgoing.reshape(devices, capacity, BAND, frame), 'tile',...  6.47 us
    pallas_call x1, Pallas kernels, shards(): pl.pallas_call(functools.partial(render_kernel, sizes), name='render', in...  4.33 us
    ppermute x1, waiting for transfers between devices, shards(): lax.ppermute(grid, 'sec', [(i, (i - 1) % sections) for i in range(section...  2.84 us
    pallas_call x1, Pallas kernels, shards(): pl.pallas_call(functools.partial(gradient_kernel, sizes, unroll), name='g...  2.79 us
    ppermute x1, starting transfers between devices, shards(): lax.ppermute(grid, 'sec', [(i, (i - 1) % sections) for i in range(section...  2.47 us
  transfers between devices with their start and end apart: 2, of which 2 were waited for; matrix products, arithmetic and copies ran while one was open for 0% of the time, Pallas kernels for 19%

profile of v2, /device:TPU:0, one launch (start us, length us, event | category | flops | bytes accessed | tf_op | source)
XLA Modules:
  0.0 62.0 jit_solution(13483951346540634934)
XLA Ops:
  0.6 0.0 copy-start.2
  0.6 0.0 copy-start.3
  0.7 0.0 copy-start.4
  0.7 0.0 copy-start.5
  0.7 4.3 %render.1 = (bf16[128,16,256]{2,1,0:T(8,128)(2,1)}, bf16[64,16,256]{2,1,0:T(8,128)(2,1)}) custom-call(f32[2,32]{1,0:T(2,128)} %bitcast.21, f32[2,32]{1,0:T(2,128)} %bitcast.23, s32[2,32]{1,0:T(2,128)} %bitcast.25, s32[16,1,32]{2,1,0:T(1,128)} %bitcast.19, bf16[4,512,512]{2,1,0:T(8,128)(2,1)} %bitcast.30), custom_call_target="tpu_custom_call" | custom-call | flops 800000000 | bytes 4194304 | tf_op jit(solution)/shard_map/render/pallas_call | solution.py:436
  5.0 0.0 copy-start
  5.0 0.0 copy-start.1
  5.0 6.5 %all-to-all-start = ((bf16[8,16,16,256]{3,2,1,0:T(8,128)(2,1)}), bf16[8,16,16,256]{3,2,1,0:T(8,128)(2,1)S(1)}, u32[]{:S(2)}, u32[]{:S(2)}) async-start(bf16[8,16,16,256]{3,2,1,0:T(8,128)(2,1)} %bitcast.27), calls=%async_computation | async-start | bytes 2097152 | tf_op jit(solution)/shard_map/all_to_all | solution.py:462
  11.5 0.0 copy-done.2
  11.5 0.0 copy-done.3
  11.5 0.0 copy-done.4
  11.5 0.0 copy-done.5
  11.5 0.0 copy-done
  11.5 11.5 %moments.1 = (f32[8,128]{1,0:T(8,128)S(1)}, f32[16,16,256]{2,1,0:T(8,128)S(1)}, f32[128,256]{1,0:T(8,128)S(1)}, f32[4,128,128]{2,1,0:T(8,128)S(1)}, s32[128]{0:T(128)S(1)}) custom-call(f32[2,32]{1,0:T(2,128)S(1)} %bitcast.22, f32[2,32]{1,0:T(2,128)S(1)} %bitcast.24, s32[2,32]{1,0:T(2,128)S(1)} %bitcast.26, s32[16,1,32]{2,1,0:T(1,128)S(1)} %bitcast.20, ...), custom_call_target="tpu_custom_call" | custom-call | flops 20000000 | bytes 1048576 | tf_op jit(solution)/shard_map/moments/pallas_call | solution.py:470
  23.0 15.1 %all-to-all-done = bf16[8,16,16,256]{3,2,1,0:T(8,128)(2,1)S(1)} async-done(((bf16[8,16,16,256]{3,2,1,0:T(8,128)(2,1)}), bf16[8,16,16,256]{3,2,1,0:T(8,128)(2,1)S(1)}, u32[]{:S(2)}, u32[]{:S(2)}) %all-to-all-start) | async-done | bytes 1048608 | tf_op jit(solution)/shard_map/all_to_all | solution.py:462
  38.1 2.0 %blend.1 = bf16[16,16,256]{2,1,0:T(8,128)(2,1)} custom-call(s32[128]{0:T(128)S(1)} %get-tuple-element.10.slot_bands, bf16[128,16,256]{2,1,0:T(8,128)(2,1)S(1)} %bitcast.16, f32[16,16,256]{2,1,0:T(8,128)S(1)} %get-tuple-element.12.cover_sum), custom_call_target="tpu_custom_call" | custom-call | flops 1000000 | bytes 2097152 | tf_op jit(solution)/shard_map/blend/pallas_call | solution.py:491
  40.1 2.5 %collective-permute-start = (bf16[16,16,256]{2,1,0:T(8,128)(2,1)}, bf16[16,16,256]{2,1,0:T(8,128)(2,1)S(1)}, u32[]{:S(2)}, u32[]{:S(2)}) collective-permute-start(bf16[16,16,256]{2,1,0:T(8,128)(2,1)} %blend.1), channel_id=1, source_target_pairs={{0,24},{8,0},{16,8},{24,16},{1,25},{9,1},{17,9},{25,17},{2,26},{10... | collective-permute-start | bytes 393224 | tf_op jit(solution)/shard_map/ppermute | solution.py:502
  42.6 2.8 %collective-permute-done.from_next = bf16[16,16,256]{2,1,0:T(8,128)(2,1)S(1)} collective-permute-done((bf16[16,16,256]{2,1,0:T(8,128)(2,1)}, bf16[16,16,256]{2,1,0:T(8,128)(2,1)S(1)}, u32[]{:S(2)}, u32[]{:S(2)}) %collective-permute-start) | collective-permute-done | bytes 131104 | tf_op jit(solution)/shard_map/ppermute | solution.py:502
  45.4 0.0 copy-done.1
  45.4 2.8 %gradient.1 = f32[32,8,128]{2,1,0:T(8,128)S(1)} custom-call(s32[128]{0:T(128)S(1)} %get-tuple-element.10.slot_bands, bf16[128,16,256]{2,1,0:T(8,128)(2,1)S(1)} %bitcast.17, bf16[16,16,256]{2,1,0:T(8,128)(2,1)S(1)} %collective-permute-done.from_next, bf16[16,16,256]{2,1,0:T(8,128)(2,1)S(1)} %bitcast.18, f32[128,256]{1,0:T(8,128)S(1)} %get-tuple-element.13.slot_cover, ...), custom_call_target="tpu_custom_call" | custom-call | flops 8000000 | bytes 2097152 | tf_op jit(solution)/shard_map/gradient/pallas_call | solution.py:504
  48.2 12.6 %all_to_all.10.received = f32[32,8,128]{2,1,0:T(8,128)S(1)} all-to-all(f32[32,8,128]{2,1,0:T(8,128)S(1)} %gradient.1), channel_id=1, replica_groups=mesh['sec'=4,'tile'=8] {'sec','tile'}, dimensions={0} | all-to-all | bytes 262144 | tf_op jit(solution)/shard_map/all_to_all | solution.py:526
  60.8 1.2 %solve.1 = f32[4,6]{1,0:T(4,128)} custom-call(f32[32,8,128]{2,1,0:T(8,128)S(1)} %all_to_all.10.received), custom_call_target="tpu_custom_call" | custom-call | flops 100000 | bytes 262144 | tf_op jit(solution)/shard_map/solve/pallas_call | solution.py:530
Async XLA Ops:
  0.6 10.9 %copy-start.2 = (s32[1,32,16,1]{1,3,2,0:T(1,128)S(1)}, s32[1,32,16,1]{1,3,2,0:T(1,128)}, u32[]{:S(2)}) copy-start(s32[1,32,16,1]{1,3,2,0:T(1,128)} %param.10) | copy-start | bytes 6148
  0.6 10.9 %copy-start.3 = (f32[1,2,32]{2,1,0:T(2,128)S(1)}, f32[1,2,32]{2,1,0:T(2,128)}, u32[]{:S(2)}) copy-start(f32[1,2,32]{2,1,0:T(2,128)} %param.7) | copy-start | bytes 772
  0.7 10.9 %copy-start.4 = (f32[1,2,32]{2,1,0:T(2,128)S(1)}, f32[1,2,32]{2,1,0:T(2,128)}, u32[]{:S(2)}) copy-start(f32[1,2,32]{2,1,0:T(2,128)} %param.8) | copy-start | bytes 772
  0.7 10.9 %copy-start.5 = (s32[1,2,32]{2,1,0:T(2,128)S(1)}, s32[1,2,32]{2,1,0:T(2,128)}, u32[]{:S(2)}) copy-start(s32[1,2,32]{2,1,0:T(2,128)} %param.9) | copy-start | bytes 772
  5.0 6.5 %copy-start = (bf16[64,16,256]{2,1,0:T(8,128)(2,1)S(1)}, bf16[64,16,256]{2,1,0:T(8,128)(2,1)}, u32[]{:S(2)}) copy-start(bf16[64,16,256]{2,1,0:T(8,128)(2,1)} %get-tuple-element.9.frames) | copy-start | bytes 1572868
  5.0 40.4 %copy-start.1 = (bf16[1,256,256]{2,1,0:T(8,128)(2,1)S(1)}, bf16[1,256,256]{2,1,0:T(8,128)(2,1)}, u32[]{:S(2)}) copy-start(bf16[1,256,256]{2,1,0:T(8,128)(2,1)} %param.11) | copy-start | bytes 393220
  5.0 33.1 %all-to-all-start = ((bf16[8,16,16,256]{3,2,1,0:T(8,128)(2,1)}), bf16[8,16,16,256]{3,2,1,0:T(8,128)(2,1)S(1)}, u32[]{:S(2)}, u32[]{:S(2)}) async-start(bf16[8,16,16,256]{3,2,1,0:T(8,128)(2,1)} %bitcast.27), calls=%async_computation | async-start | bytes 2097152 | tf_op jit(solution)/shard_map/all_to_all | solution.py:462
  40.1 5.3 %collective-permute-start = (bf16[16,16,256]{2,1,0:T(8,128)(2,1)}, bf16[16,16,256]{2,1,0:T(8,128)(2,1)S(1)}, u32[]{:S(2)}, u32[]{:S(2)}) collective-permute-start(bf16[16,16,256]{2,1,0:T(8,128)(2,1)} %blend.1), channel_id=1, source_target_pairs={{0,24},{8,0},{16,8},{24,16},{1,25},{9,1},{17,9},{25,17},{2,26},{10... | collective-permute-start | bytes 393224 | tf_op jit(solution)/shard_map/ppermute | solution.py:502

commit v3 on v2

--- a/solution.py
+++ b/solution.py
@@ -1,5 +1,4 @@
 import functools
-import math
 
 import jax
 import jax.numpy as jnp
@@ -13,7 +12,7 @@
 COUPLING = 0.25
 LANES = 128
 ROWS = 8
-ANY = pl.BlockSpec(memory_space=pl.ANY)
+HBM = pl.BlockSpec(memory_space=pltpu.HBM)
 SMEM = pl.BlockSpec(memory_space=pltpu.SMEM)
 VMEM = pl.BlockSpec(memory_space=pltpu.VMEM)
 
@@ -58,28 +57,15 @@
 
 
 def render_kernel(
-    sizes,
-    zoom_in,
-    frac_in,
-    offset_in,
-    owner_in,
-    patches_in,
-    outgoing,
-    frames_out,
-    zoom,
-    frac,
-    offset,
-    owner,
-    patches,
-    frames,
-    named,
-    small_sems,
-    patch_sems,
-    frame_sem,
-    band_sem,
+    sizes, zoom_in, frac_in, offset_in, owner_in, patches_in, frames, *outgoing_and_scratch
 ):
     tiles, bands, frame, source, capacity, devices = sizes
-    first = lax.axis_index("tile") * tiles
+    outgoing = outgoing_and_scratch[:devices]
+    zoom, frac, offset, owner, patches, named, rows, small_sems, patch_sems = (
+        outgoing_and_scratch[devices:]
+    )
+    me = lax.axis_index("tile")
+    first = me * tiles
     ratio = frame / source
     fetched = [
         pltpu.make_async_copy(patches_in.at[j], patches.at[j], patch_sems.at[j])
@@ -95,8 +81,16 @@
         copy.start()
     for g in range(devices):
         named[g] = 0
+    for slot in range(devices * capacity):
+        rows[slot] = 0
     for copy in small:
         copy.wait()
+    for j in range(tiles):
+        for band in range(bands):
+            target = owner[band, 0, first + j]
+            slot = named[target]
+            named[target] = slot + 1
+            rows[target * capacity + slot] = j * bands + band
     for j in range(tiles):
         tile = first + j
         row_points = points_of(spots_along((frame, LANES), 0), zoom, frac, offset, 0, tile, ratio)
@@ -115,19 +109,11 @@
         rendered = jnp.dot(
             halfway.astype(jnp.bfloat16), col_weights, preferred_element_type=jnp.float32
         ).astype(jnp.bfloat16)
-        for band in range(bands):
-            row = j * bands + band
-            frames[row] = rendered[band * BAND : (band + 1) * BAND]
-            target = owner[band, 0, tile]
-            slot = named[target]
-            named[target] = slot + 1
-            pltpu.make_async_copy(
-                frames.at[row], outgoing.at[target * capacity + slot], band_sem
-            ).start()
-    kept = pltpu.make_async_copy(frames, frames_out, frame_sem)
-    kept.start()
-    pltpu.make_async_copy(frames, outgoing.at[pl.ds(0, tiles * bands)], band_sem).wait()
-    kept.wait()
+        frames[j * bands : (j + 1) * bands] = rendered.reshape(bands, BAND, frame)
+    for distance in range(devices):
+        target = me ^ distance
+        for slot in range(capacity):
+            outgoing[distance][slot] = frames[rows[target * capacity + slot]]
 
 
 def feature_rows(frame, wanted):
@@ -166,18 +152,19 @@
     all_tiles = tiles * devices
     ratio = frame / source
 
-    for device in range(devices):
+    for distance in range(devices):
+        device = me ^ distance
 
         def note(position, count):
             tile = device * tiles + position // bands
             band = position % bands
-            codes[device * capacity + count] = tile * bands + band
+            codes[distance * capacity + count] = tile * bands + band
             return count + (owner[band, 0, tile] == me).astype(jnp.int32)
 
         count = lax.fori_loop(0, tiles * bands, note, 0, unroll=8)
 
         def blank(position, carry):
-            codes[device * capacity + position] = -1
+            codes[distance * capacity + position] = -1
             return carry
 
         lax.fori_loop(count, capacity, blank, 0)
@@ -242,17 +229,14 @@
     base[...] = total
 
 
-def blend_kernel(sizes, unroll, slot_bands, incoming, cover_sum, grid, total):
+def blend_kernel(sizes, slot_bands, cover_sum, *blocks_and_rest):
     tiles, bands, frame, source, capacity, devices = sizes
+    blocks = blocks_and_rest[:devices]
+    grid, total = blocks_and_rest[devices:]
     total[...] = jnp.zeros_like(total)
-
-    def add(group, carry):
-        for k in range(unroll):
-            slot = group * unroll + k
-            total[slot_bands[slot]] += incoming[slot].astype(jnp.float32)
-        return carry
-
-    lax.fori_loop(0, devices * capacity // unroll, add, 0)
+    for distance, block in enumerate(blocks):
+        for k in range(capacity):
+            total[slot_bands[distance * capacity + k]] += block[k].astype(jnp.float32)
     grid[...] = (total[:bands] / (1.0 + cover_sum[...])).astype(jnp.bfloat16)
 
 
@@ -260,19 +244,13 @@
 
 
 def gradient_kernel(
-    sizes,
-    unroll,
-    slot_bands,
-    incoming,
-    from_next,
-    top_grid,
-    slot_cover,
-    slot_lines,
-    base,
-    payload,
-    above,
-    sums,
+    sizes, slot_bands, from_next, top_grid, slot_cover, slot_lines, base, grid, *blocks_and_rest
 ):
+    devices = sizes[-1]
+    blocks = blocks_and_rest[:devices]
+    payload, grid_out, above, sums, grid_sem = blocks_and_rest[devices:]
+    written = pltpu.make_async_copy(grid, grid_out, grid_sem)
+    written.start()
     tiles, bands, frame, source, capacity, devices = sizes
     sec = lax.axis_index("sec")
     slots = devices * capacity
@@ -290,17 +268,17 @@
     spots = spots_along((BAND, LANES), 0)
     raised = spots * (2.0 / frame)
 
-    def add(group, carry):
-        for k in range(unroll):
-            slot = group * unroll + k
-            here = pl.ds(slot, 1)
-            points = spots * slot_lines[0, here, :] + slot_lines[1, here, :]
+    for distance, block in enumerate(blocks):
+        for k in range(capacity):
+            slot = distance * capacity + k
+            here = slice(slot, slot + 1)
+            points = spots * slot_lines[0, here] + slot_lines[1, here]
             cover = cover_of(points, source)
-            lifted = cover * (raised + slot_lines[2, here, :])
-            level = incoming[slot].astype(jnp.float32)
+            lifted = cover * (raised + slot_lines[2, here])
+            level = block[k].astype(jnp.float32)
             error = above[slot_bands[slot]] - level
             product = error * level
-            rows = pl.ds(pl.multiple_of(slot * ROWS, ROWS), ROWS)
+            rows = slice(slot * ROWS, (slot + 1) * ROWS)
             for half in range(frame // LANES):
                 part = slice(half * LANES, (half + 1) * LANES)
                 for kind, (weight, value) in enumerate(
@@ -308,9 +286,6 @@
                 ):
                     term = weight * value[:, part]
                     sums[kind, half, rows, :] = term[:ROWS] + term[ROWS:]
-        return carry
-
-    lax.fori_loop(0, slots // unroll, add, 0)
     used = slot_lines[3] >= 0.0
     by_slot = jnp.zeros((ROWS, slots), jnp.float32)
     for kind, wanted in enumerate(GRADIENT_ROWS):
@@ -337,6 +312,7 @@
         preferred_element_type=jnp.float32,
     )
     payload[...] = jnp.broadcast_to(total[None], payload.shape)
+    written.wait()
 
 
 def solve_kernel(sizes, received, corrections):
@@ -431,41 +407,34 @@
     place = (zoom[0], frac[0], offset[0])
     routes = jnp.transpose(owner, (0, 2, 3, 1))[0]
 
-    unroll = math.gcd(slots, 16)
     rows = tiles * bands
-    outgoing, frames = pl.pallas_call(
+    block = jax.ShapeDtypeStruct((capacity, BAND, frame), jnp.bfloat16)
+    frames, *outgoing = pl.pallas_call(
         functools.partial(render_kernel, sizes),
         name="render",
-        in_specs=[ANY] * 5,
-        out_specs=[ANY] * 2,
-        out_shape=[
-            jax.ShapeDtypeStruct((slots, BAND, frame), jnp.bfloat16),
-            jax.ShapeDtypeStruct((rows, BAND, frame), jnp.bfloat16),
-        ],
+        in_specs=[HBM] * 5,
+        out_specs=[VMEM] * (1 + devices),
+        out_shape=[jax.ShapeDtypeStruct((rows, BAND, frame), jnp.bfloat16)] + [block] * devices,
         scratch_shapes=[
             pltpu.SMEM(place[0].shape, jnp.float32),
             pltpu.SMEM(place[1].shape, jnp.float32),
             pltpu.SMEM(place[2].shape, jnp.int32),
             pltpu.SMEM(routes.shape, jnp.int32),
             pltpu.VMEM((tiles, source, source), jnp.bfloat16),
-            pltpu.VMEM((rows, BAND, frame), jnp.bfloat16),
             pltpu.SMEM((devices,), jnp.int32),
+            pltpu.SMEM((slots,), jnp.int32),
             pltpu.SemaphoreType.DMA((4,)),
             pltpu.SemaphoreType.DMA((tiles,)),
-            pltpu.SemaphoreType.DMA,
-            pltpu.SemaphoreType.DMA,
         ],
-        compiler_params=params(58),
+        compiler_params=params(24),
         cost_estimate=cost(800_000_000, 4 << 20),
-    )(*place, routes, patches[0])
-
-    incoming = lax.all_to_all(
-        outgoing.reshape(devices, capacity, BAND, frame),
-        "tile",
-        split_axis=0,
-        concat_axis=0,
-        tiled=True,
-    ).reshape(slots, BAND, frame)
+    )(*(pltpu.with_memory_space_constraint(x, pltpu.HBM) for x in (*place, routes, patches[0])))
+
+    incoming = [outgoing[0]] + [None] * (devices - 1)
+    for distance in sorted(range(1, devices), key=lambda d: (-(d.bit_length()), d)):
+        incoming[distance] = lax.ppermute(
+            outgoing[distance], "tile", [(i, i ^ distance) for i in range(devices)]
+        )
 
     base, cover_sum, slot_cover, slot_lines, slot_bands = pl.pallas_call(
         functools.partial(moment_kernel, sizes),
@@ -489,38 +458,43 @@
     )(*place, routes, frames)
 
     grid = pl.pallas_call(
-        functools.partial(blend_kernel, sizes, unroll),
+        functools.partial(blend_kernel, sizes),
         name="blend",
-        in_specs=[SMEM, VMEM, VMEM],
+        in_specs=[SMEM] + [VMEM] * (1 + devices),
         out_specs=VMEM,
         out_shape=jax.ShapeDtypeStruct((bands, BAND, frame), jnp.bfloat16),
         scratch_shapes=[pltpu.VMEM((bands + 1, BAND, frame), jnp.float32)],
         compiler_params=params(24),
         cost_estimate=cost(1_000_000, 2 << 20),
-    )(slot_bands, incoming, cover_sum)
+    )(slot_bands, cover_sum, *incoming)
 
     from_next = lax.ppermute(grid, "sec", [(i, (i - 1) % sections) for i in range(sections)])
 
-    payload = pl.pallas_call(
-        functools.partial(gradient_kernel, sizes, unroll),
+    payload, grid_out = pl.pallas_call(
+        functools.partial(gradient_kernel, sizes),
         name="gradient",
-        in_specs=[SMEM] + [VMEM] * 6,
-        out_specs=VMEM,
-        out_shape=jax.ShapeDtypeStruct((sections * devices, ROWS, lanes), jnp.float32),
+        in_specs=[SMEM] + [VMEM] * (6 + devices),
+        out_specs=[VMEM, HBM],
+        out_shape=[
+            jax.ShapeDtypeStruct((sections * devices, ROWS, lanes), jnp.float32),
+            jax.ShapeDtypeStruct((bands, BAND, frame), jnp.bfloat16),
+        ],
         scratch_shapes=[
             pltpu.VMEM((bands + 1, BAND, frame), jnp.float32),
             pltpu.VMEM((4, frame // LANES, slots * ROWS, LANES), jnp.float32),
+            pltpu.SemaphoreType.DMA,
         ],
         compiler_params=params(24),
         cost_estimate=cost(8_000_000, 2 << 20),
     )(
         slot_bands,
-        incoming,
         from_next,
         top_grid.reshape(bands, BAND, frame),
         slot_cover,
         slot_lines,
         base,
+        grid,
+        *incoming,
     )
 
     received = lax.all_to_all(
@@ -537,7 +511,7 @@
         cost_estimate=cost(100_000, 1 << 18),
     )(received)
     return (
-        grid.reshape(1, 1, frame, frame),
+        grid_out.reshape(1, 1, frame, frame),
         jnp.transpose(corrections[None], (2, 0, 1)),
     )
 

time: 62.2 us -> 59 us (0.949)
  waiting for transfers between devices: 17.9 us -> 6.47 us
  blocking collectives: 12.6 us -> 18.3 us
  starting transfers between devices: 8.93 us -> 12.6 us
  Pallas kernels: 21.8 us -> 20.8 us
    all_to_all x1 -> x0, waiting for transfers between devices: 15.1 us -> none  [shards(): lax.all_to_all(outgoing.reshape(devices, capacity, BAND, frame), 'tile',...]
    ppermute x0 -> x7, starting transfers between devices: none -> 9.58 us  [shards(): lax.ppermute(outgoing[distance], 'tile', [(i, i ^ distance) for i in rang...]
    all_to_all x1 -> x0, starting transfers between devices: 6.47 us -> none  [shards(): lax.all_to_all(outgoing.reshape(devices, capacity, BAND, frame), 'tile',...]
    all_to_all x1, blocking collectives: 12.6 us -> 18.3 us  [shards(): lax.all_to_all(payload, ('sec', 'tile'), split_axis=0, concat_axis=0, til...]
    ppermute x0 -> x7, waiting for transfers between devices: none -> 2.92 us  [shards(): lax.ppermute(outgoing[distance], 'tile', [(i, i ^ distance) for i in rang...]
    ppermute x1, waiting for transfers between devices: 2.84 us -> 3.55 us  [shards(): lax.ppermute(grid, 'sec', [(i, (i - 1) % sections) for i in range(section...]
  transfers between devices with their start and end apart: 2 -> 8, of which waited for: 2 -> 3; matrix products, arithmetic and copies ran while one was open for 0% -> 0% of each run, Pallas kernels for 19% -> 19%
where the time goes in v3:
time: 59 us; the launch traced here: 58.9 us
  Pallas kernels  20.8 us (35%)
  blocking collectives  18.3 us (31%)
  starting transfers between devices  12.6 us (21%)
  waiting for transfers between devices  6.47 us (11%)
  between operations  0.74 us (1%)
    all_to_all x1, blocking collectives, shards(): lax.all_to_all(payload, ('sec', 'tile'), split_axis=0, concat_axis=0, til...  18.3 us
    pallas_call x1, Pallas kernels, shards(): pl.pallas_call(functools.partial(moment_kernel, sizes), name='moments', i...  11.4 us
    ppermute x7, starting transfers between devices, shards(): lax.ppermute(outgoing[distance], 'tile', [(i, i ^ distance) for i in rang...  9.58 us
    pallas_call x1, Pallas kernels, shards(): pl.pallas_call(functools.partial(render_kernel, sizes), name='render', in...  3.77 us
    ppermute x1, waiting for transfers between devices, shards(): lax.ppermute(grid, 'sec', [(i, (i - 1) % sections) for i in range(section...  3.55 us
    pallas_call x1, Pallas kernels, shards(): pl.pallas_call(functools.partial(gradient_kernel, sizes), name='gradient'...  3.08 us
    ppermute x1, starting transfers between devices, shards(): lax.ppermute(grid, 'sec', [(i, (i - 1) % sections) for i in range(section...  3.03 us
    ppermute x7, waiting for transfers between devices, shards(): lax.ppermute(outgoing[distance], 'tile', [(i, i ^ distance) for i in rang...  2.92 us
  transfers between devices with their start and end apart: 8, of which 3 were waited for; matrix products, arithmetic and copies ran while one was open for 0% of the time, Pallas kernels for 19%

profile of v3, /device:TPU:0, one launch (start us, length us, event | category | flops | bytes accessed | tf_op | source)
XLA Modules:
  0.0 58.9 jit_solution(16386256015753458107)
XLA Ops:
  0.6 0.0 copy-start.1
  0.6 0.0 copy-start.4
  0.7 0.0 copy-start.3
  0.7 0.0 copy-start.2
  0.7 0.0 copy-start
  0.7 3.8 %render.1 = (bf16[64,16,256]{2,1,0:T(8,128)(2,1)S(1)}, bf16[16,16,256]{2,1,0:T(8,128)(2,1)S(1)}, bf16[16,16,256]{2,1,0:T(8,128)(2,1)S(1)}, bf16[16,16,256]{2,1,0...) custom-call(f32[2,32]{1,0:T(2,128)} %bitcast.17, ...), custom_call_target="tpu_custom_call" | custom-call | flops 800000000 | bytes 4194304 | tf_op jit(solution)/shard_map/render/pallas_call | solution.py:412
  4.5 0.5 collective-permute-start
  5.0 2.7 %collective-permute-start.1 = (bf16[16,16,256]{2,1,0:T(8,128)(2,1)S(1)}, bf16[16,16,256]{2,1,0:T(8,128)(2,1)S(1)}, u32[]{:S(2)}, u32[]{:S(2)}) collective-permute-start(bf16[16,16,256]{2,1,0:T(8,128)(2,1)S(1)} %get-tuple-element.23), channel_id=1, source_target_pairs={{0,2},{1,3},{2,0},{3,1},{4,6},{5,7},{6,4},{7,5},{8,10},{9,11},{10,... | collective-permute-start | bytes 393224 | tf_op jit(solution)/shard_map/ppermute | solution.py:435
  7.6 0.1 collective-permute-start.2
  7.7 2.8 %collective-permute-start.3 = (bf16[16,16,256]{2,1,0:T(8,128)(2,1)S(1)}, bf16[16,16,256]{2,1,0:T(8,128)(2,1)S(1)}, u32[]{:S(2)}, u32[]{:S(2)}) collective-permute-start(bf16[16,16,256]{2,1,0:T(8,128)(2,1)S(1)} %get-tuple-element.25), channel_id=1, source_target_pairs={{0,4},{1,5},{2,6},{3,7},{4,0},{5,1},{6,2},{7,3},{8,12},{9,13},{10,... | collective-permute-start | bytes 393224 | tf_op jit(solution)/shard_map/ppermute | solution.py:435
  10.5 0.0 collective-permute-start.4
  10.5 0.0 collective-permute-done.blocks_and_rest_1_
  10.5 3.6 %collective-permute-start.5 = (bf16[16,16,256]{2,1,0:T(8,128)(2,1)S(1)}, bf16[16,16,256]{2,1,0:T(8,128)(2,1)S(1)}, u32[]{:S(2)}, u32[]{:S(2)}) collective-permute-start(bf16[16,16,256]{2,1,0:T(8,128)(2,1)S(1)} %get-tuple-element.27), channel_id=1, source_target_pairs={{0,6},{1,7},{2,4},{3,5},{4,2},{5,3},{6,0},{7,1},{8,14},{9,15},{10,... | collective-permute-start | bytes 393224 | tf_op jit(solution)/shard_map/ppermute | solution.py:435
  14.0 2.8 %collective-permute-done.1.blocks_and_rest_2_ = bf16[16,16,256]{2,1,0:T(8,128)(2,1)S(1)} collective-permute-done((bf16[16,16,256]{2,1,0:T(8,128)(2,1)S(1)}, bf16[16,16,256]{2,1,0:T(8,128)(2,1)S(1)}, u32[]{:S(2)}, u32[]{:S(2)}) %collective-permute-start.1) | collective-permute-done | bytes 131104 | tf_op jit(solution)/shard_map/ppermute | solution.py:435
  16.9 0.0 collective-permute-start.6
  16.9 0.0 copy-done.1
  16.9 0.0 copy-done.4
  16.9 0.0 copy-done.3
  16.9 0.0 copy-done.2
  16.9 11.4 %moments.1 = (f32[8,128]{1,0:T(8,128)S(1)}, f32[16,16,256]{2,1,0:T(8,128)S(1)}, f32[128,256]{1,0:T(8,128)S(1)}, f32[4,128,128]{2,1,0:T(8,128)S(1)}, s32[128]{0:T(128)S(1)}) custom-call(f32[2,32]{1,0:T(2,128)S(1)} %bitcast.18, f32[2,32]{1,0:T(2,128)S(1)} %bitcast.20, s32[2,32]{1,0:T(2,128)S(1)} %bitcast.22, s32[16,1,32]{2,1,0:T(1,128)S(1)} %bitcast.16, ...), custom_call_target="tpu_custom_call" | custom-call | flops 20000000 | bytes 1048576 | tf_op jit(solution)/shard_map/moments/pallas_call | solution.py:439
  28.3 0.0 collective-permute-done.2.blocks_and_rest_3_
  28.3 0.0 collective-permute-done.3.blocks_and_rest_4_
  28.3 0.1 collective-permute-done.4.blocks_and_rest_5_
  28.4 0.0 collective-permute-done.5.blocks_and_rest_6_
  28.4 0.0 collective-permute-done.6.blocks_and_rest_7_
  28.5 1.3 %blend.1.grid = bf16[16,16,256]{2,1,0:T(8,128)(2,1)S(1)} custom-call(s32[128]{0:T(128)S(1)} %get-tuple-element.19.slot_bands, f32[16,16,256]{2,1,0:T(8,128)S(1)} %get-tuple-element.20.cover_sum, bf16[16,16,256]{2,1,0:T(8,128)(2,1)S(1)} %get-tuple-element.21.blocks_and_rest_0_, bf16[16,16,256]{2,1,0:T(8,128)(2,1)S(1)} %collective-permute-done.blocks_and_rest_1_, ...), custom_call_target="tpu_custom_call" | custom-call | flops 1000000 | bytes 2097152 | tf_op jit(solution)/shard_map/blend/pallas_call | solution.py:460
  29.8 3.0 %collective-permute-start.7 = (bf16[16,16,256]{2,1,0:T(8,128)(2,1)S(1)}, bf16[16,16,256]{2,1,0:T(8,128)(2,1)S(1)}, u32[]{:S(2)}, u32[]{:S(2)}) collective-permute-start(bf16[16,16,256]{2,1,0:T(8,128)(2,1)S(1)} %blend.1.grid), channel_id=1, source_target_pairs={{0,24},{8,0},{16,8},{24,16},{1,25},{9,1},{17,9},{25,17},{2,26},{10... | collective-permute-start | bytes 393224 | tf_op jit(solution)/shard_map/ppermute | solution.py:471
  32.8 3.5 %collective-permute-done.7.from_next = bf16[16,16,256]{2,1,0:T(8,128)(2,1)S(1)} collective-permute-done((bf16[16,16,256]{2,1,0:T(8,128)(2,1)S(1)}, bf16[16,16,256]{2,1,0:T(8,128)(2,1)S(1)}, u32[]{:S(2)}, u32[]{:S(2)}) %collective-permute-start.7) | collective-permute-done | bytes 131104 | tf_op jit(solution)/shard_map/ppermute | solution.py:471
  36.3 0.0 copy-done
  36.3 3.1 %gradient.1 = (f32[32,8,128]{2,1,0:T(8,128)S(1)}, bf16[16,16,256]{2,1,0:T(8,128)(2,1)}) custom-call(s32[128]{0:T(128)S(1)} %get-tuple-element.19.slot_bands, bf16[16,16,256]{2,1,0:T(8,128)(2,1)S(1)} %collective-permute-done.7.from_next, bf16[16,16,256]{2,1,0:T(8,128)(2,1)S(1)} %bitcast.14, f32[128,256]{1,0:T(8,128)S(1)} %get-tuple-element.29.slot_cover, ...), custom_call_target="tpu_custom_call" | custom-call | flops 8000000 | bytes 2097152 | tf_op jit(solution)/shard_map/gradient/pallas_call | solution.py:473
  39.4 18.3 %all_to_all.5.received = f32[32,8,128]{2,1,0:T(8,128)S(1)} all-to-all(f32[32,8,128]{2,1,0:T(8,128)S(1)} %get-tuple-element.33), channel_id=1, replica_groups=mesh['sec'=4,'tile'=8] {'sec','tile'}, dimensions={0} | all-to-all | bytes 262144 | tf_op jit(solution)/shard_map/all_to_all | solution.py:500
  57.7 1.2 %solve.1 = f32[4,6]{1,0:T(4,128)} custom-call(f32[32,8,128]{2,1,0:T(8,128)S(1)} %all_to_all.5.received), custom_call_target="tpu_custom_call" | custom-call | flops 100000 | bytes 262144 | tf_op jit(solution)/shard_map/solve/pallas_call | solution.py:504
Async XLA Ops:
  0.6 16.2 %copy-start.1 = (s32[1,32,16,1]{1,3,2,0:T(1,128)S(1)}, s32[1,32,16,1]{1,3,2,0:T(1,128)}, u32[]{:S(2)}) copy-start(s32[1,32,16,1]{1,3,2,0:T(1,128)} %param.10) | copy-start | bytes 6148
  0.6 16.2 %copy-start.4 = (s32[1,2,32]{2,1,0:T(2,128)S(1)}, s32[1,2,32]{2,1,0:T(2,128)}, u32[]{:S(2)}) copy-start(s32[1,2,32]{2,1,0:T(2,128)} %param.9) | copy-start | bytes 772
  0.7 16.2 %copy-start.3 = (f32[1,2,32]{2,1,0:T(2,128)S(1)}, f32[1,2,32]{2,1,0:T(2,128)}, u32[]{:S(2)}) copy-start(f32[1,2,32]{2,1,0:T(2,128)} %param.8) | copy-start | bytes 772
  0.7 16.2 %copy-start.2 = (f32[1,2,32]{2,1,0:T(2,128)S(1)}, f32[1,2,32]{2,1,0:T(2,128)}, u32[]{:S(2)}) copy-start(f32[1,2,32]{2,1,0:T(2,128)} %param.7) | copy-start | bytes 772
  0.7 35.7 %copy-start = (bf16[1,256,256]{2,1,0:T(8,128)(2,1)S(1)}, bf16[1,256,256]{2,1,0:T(8,128)(2,1)}, u32[]{:S(2)}) copy-start(bf16[1,256,256]{2,1,0:T(8,128)(2,1)} %param.11) | copy-start | bytes 393220
  4.5 6.0 %collective-permute-start = (bf16[16,16,256]{2,1,0:T(8,128)(2,1)S(1)}, bf16[16,16,256]{2,1,0:T(8,128)(2,1)S(1)}, u32[]{:S(2)}, u32[]{:S(2)}) collective-permute-start(bf16[16,16,256]{2,1,0:T(8,128)(2,1)S(1)} %get-tuple-element.22), channel_id=1, source_target_pairs={{0,1},{1,0},{2,3},{3,2},{4,5},{5,4},{6,7},{7,6},{8,9},{9,8},{10,11... | collective-permute-start | bytes 393224 | tf_op jit(solution)/shard_map/ppermute | solution.py:435
  5.0 11.9 %collective-permute-start.1 = (bf16[16,16,256]{2,1,0:T(8,128)(2,1)S(1)}, bf16[16,16,256]{2,1,0:T(8,128)(2,1)S(1)}, u32[]{:S(2)}, u32[]{:S(2)}) collective-permute-start(bf16[16,16,256]{2,1,0:T(8,128)(2,1)S(1)} %get-tuple-element.23), channel_id=1, source_target_pairs={{0,2},{1,3},{2,0},{3,1},{4,6},{5,7},{6,4},{7,5},{8,10},{9,11},{10,... | collective-permute-start | bytes 393224 | tf_op jit(solution)/shard_map/ppermute | solution.py:435
  7.6 20.7 %collective-permute-start.2 = (bf16[16,16,256]{2,1,0:T(8,128)(2,1)S(1)}, bf16[16,16,256]{2,1,0:T(8,128)(2,1)S(1)}, u32[]{:S(2)}, u32[]{:S(2)}) collective-permute-start(bf16[16,16,256]{2,1,0:T(8,128)(2,1)S(1)} %get-tuple-element.24), channel_id=1, source_target_pairs={{0,3},{1,2},{2,1},{3,0},{4,7},{5,6},{6,5},{7,4},{8,11},{9,10},{10,... | collective-permute-start | bytes 393224 | tf_op jit(solution)/shard_map/ppermute | solution.py:435
  7.7 20.7 %collective-permute-start.3 = (bf16[16,16,256]{2,1,0:T(8,128)(2,1)S(1)}, bf16[16,16,256]{2,1,0:T(8,128)(2,1)S(1)}, u32[]{:S(2)}, u32[]{:S(2)}) collective-permute-start(bf16[16,16,256]{2,1,0:T(8,128)(2,1)S(1)} %get-tuple-element.25), channel_id=1, source_target_pairs={{0,4},{1,5},{2,6},{3,7},{4,0},{5,1},{6,2},{7,3},{8,12},{9,13},{10,... | collective-permute-start | bytes 393224 | tf_op jit(solution)/shard_map/ppermute | solution.py:435
  10.5 18.0 %collective-permute-start.4 = (bf16[16,16,256]{2,1,0:T(8,128)(2,1)S(1)}, bf16[16,16,256]{2,1,0:T(8,128)(2,1)S(1)}, u32[]{:S(2)}, u32[]{:S(2)}) collective-permute-start(bf16[16,16,256]{2,1,0:T(8,128)(2,1)S(1)} %get-tuple-element.26), channel_id=1, source_target_pairs={{0,5},{1,4},{2,7},{3,6},{4,1},{5,0},{6,3},{7,2},{8,13},{9,12},{10,... | collective-permute-start | bytes 393224 | tf_op jit(solution)/shard_map/ppermute | solution.py:435
  10.5 18.0 %collective-permute-start.5 = (bf16[16,16,256]{2,1,0:T(8,128)(2,1)S(1)}, bf16[16,16,256]{2,1,0:T(8,128)(2,1)S(1)}, u32[]{:S(2)}, u32[]{:S(2)}) collective-permute-start(bf16[16,16,256]{2,1,0:T(8,128)(2,1)S(1)} %get-tuple-element.27), channel_id=1, source_target_pairs={{0,6},{1,7},{2,4},{3,5},{4,2},{5,3},{6,0},{7,1},{8,14},{9,15},{10,... | collective-permute-start | bytes 393224 | tf_op jit(solution)/shard_map/ppermute | solution.py:435
  16.9 11.6 %collective-permute-start.6 = (bf16[16,16,256]{2,1,0:T(8,128)(2,1)S(1)}, bf16[16,16,256]{2,1,0:T(8,128)(2,1)S(1)}, u32[]{:S(2)}, u32[]{:S(2)}) collective-permute-start(bf16[16,16,256]{2,1,0:T(8,128)(2,1)S(1)} %get-tuple-element.28), channel_id=1, source_target_pairs={{0,7},{1,6},{2,5},{3,4},{4,3},{5,2},{6,1},{7,0},{8,15},{9,14},{10,... | collective-permute-start | bytes 393224 | tf_op jit(solution)/shard_map/ppermute | solution.py:435
  29.8 6.6 %collective-permute-start.7 = (bf16[16,16,256]{2,1,0:T(8,128)(2,1)S(1)}, bf16[16,16,256]{2,1,0:T(8,128)(2,1)S(1)}, u32[]{:S(2)}, u32[]{:S(2)}) collective-permute-start(bf16[16,16,256]{2,1,0:T(8,128)(2,1)S(1)} %blend.1.grid), channel_id=1, source_target_pairs={{0,24},{8,0},{16,8},{24,16},{1,25},{9,1},{17,9},{25,17},{2,26},{10... | collective-permute-start | bytes 393224 | tf_op jit(solution)/shard_map/ppermute | solution.py:471

commit v4 on v3

--- a/solution.py
+++ b/solution.py
@@ -1,4 +1,5 @@
 import functools
+import math
 
 import jax
 import jax.numpy as jnp
@@ -56,13 +57,21 @@
     return (spots - (frame - 1) / 2.0) / (frame / 2.0)
 
 
+def exchange_plan(devices):
+    if devices == 8:
+        outgoing = [[0], [2, 3], [4], [5], [6], [7], [1]]
+        return outgoing, [(0, 0), (1, 2), (2, 4), (3, 5), (4, 6), (5, 7), (6, 1), (7, 3)]
+    return [[d] for d in range(devices)], [(d, d) for d in range(devices)]
+
+
 def render_kernel(
     sizes, zoom_in, frac_in, offset_in, owner_in, patches_in, frames, *outgoing_and_scratch
 ):
     tiles, bands, frame, source, capacity, devices = sizes
-    outgoing = outgoing_and_scratch[:devices]
+    plan, _ = exchange_plan(devices)
+    outgoing = outgoing_and_scratch[: len(plan)]
     zoom, frac, offset, owner, patches, named, rows, small_sems, patch_sems = (
-        outgoing_and_scratch[devices:]
+        outgoing_and_scratch[len(plan) :]
     )
     me = lax.axis_index("tile")
     first = me * tiles
@@ -86,12 +95,6 @@
     for copy in small:
         copy.wait()
     for j in range(tiles):
-        for band in range(bands):
-            target = owner[band, 0, first + j]
-            slot = named[target]
-            named[target] = slot + 1
-            rows[target * capacity + slot] = j * bands + band
-    for j in range(tiles):
         tile = first + j
         row_points = points_of(spots_along((frame, LANES), 0), zoom, frac, offset, 0, tile, ratio)
         row_weights = jnp.concatenate(
@@ -105,15 +108,34 @@
         col_points = jnp.broadcast_to(col_points[:1], (source, frame))
         col_weights = hat_weight(col_points - spots_along((source, frame), 0)).astype(jnp.bfloat16)
         fetched[j].wait()
-        halfway = jnp.dot(row_weights, patches[j], preferred_element_type=jnp.float32)
+        half, quarter = source // 2, frame // 4
+        upper = jnp.dot(
+            row_weights[: 3 * quarter, :half],
+            patches[j, :half],
+            preferred_element_type=jnp.float32,
+        )
+        lower = jnp.dot(
+            row_weights[quarter:, half:],
+            patches[j, half:],
+            preferred_element_type=jnp.float32,
+        )
+        halfway = jnp.concatenate(
+            [upper[:quarter], upper[quarter:] + lower[: 2 * quarter], lower[2 * quarter :]]
+        )
         rendered = jnp.dot(
             halfway.astype(jnp.bfloat16), col_weights, preferred_element_type=jnp.float32
         ).astype(jnp.bfloat16)
         frames[j * bands : (j + 1) * bands] = rendered.reshape(bands, BAND, frame)
-    for distance in range(devices):
-        target = me ^ distance
-        for slot in range(capacity):
-            outgoing[distance][slot] = frames[rows[target * capacity + slot]]
+        for band in range(bands):
+            target = owner[band, 0, tile]
+            slot = named[target]
+            named[target] = slot + 1
+            rows[target * capacity + slot] = j * bands + band
+    for there, group in zip(outgoing, plan):
+        for position, distance in enumerate(group):
+            target = me ^ distance
+            for slot in range(capacity):
+                there[position * capacity + slot] = frames[rows[target * capacity + slot]]
 
 
 def feature_rows(frame, wanted):
@@ -129,85 +151,87 @@
 MOMENT_ROWS = ({0: 0, 1: 1, 3: 2}, {2: 0, 4: 1}, {5: 0})
 
 
-def moment_kernel(
-    sizes,
-    zoom,
-    frac,
-    offset,
-    owner,
-    frames,
-    base,
-    cover_sum,
-    slot_cover,
-    slot_lines,
-    slot_bands,
-    codes,
-    col_cover,
-    parts,
+def scan_kernel(sizes, owner, codes):
+    tiles, bands, frame, source, capacity, devices = sizes
+    me = lax.axis_index("tile")
+
+    def scan(block, distance):
+        count = 0
+        for j in range(tiles):
+            tile = (me ^ distance) * tiles + j
+            named = [owner[band, 0, tile] for band in range(bands)]
+            for band in range(bands):
+                codes[block * capacity + count] = tile * bands + band
+                count += (named[band] == me).astype(jnp.int32)
+
+        def blank(position, carry):
+            codes[block * capacity + position] = -1
+            return carry
+
+        lax.fori_loop(count, capacity, blank, 0)
+
+    arriving = exchange_plan(devices)[1]
+    if devices == 8:
+        for block, (_, distance) in enumerate(arriving):
+            scan(block, distance)
+    else:
+        pl.loop(0, devices)(lambda block: scan(block, block))
+
+
+def slot_kernel(
+    sizes, zoom, frac, offset, codes, cover_sum, col_cover, slot_lines, slot_bands
 ):
+    tiles, bands, frame, source, capacity, devices = sizes
+    slots = devices * capacity
+    all_tiles = tiles * devices
+    ratio = frame / source
+
+    @pl.loop(0, all_tiles // ROWS)
+    def _(group):
+        for k in range(ROWS):
+            tile = group * ROWS + k
+            points = points_of(spots_along((1, frame), 1), zoom, frac, offset, 1, tile, ratio)
+            col_cover[pl.ds(tile, 1), :] = cover_of(points, source)
+
+    cover_sum[...] = jnp.zeros_like(cover_sum)
+    unroll = math.gcd(slots, ROWS)
+
+    @pl.loop(0, slots // unroll)
+    def _(group):
+        for k in range(unroll):
+            slot = group * unroll + k
+            used = codes[slot] >= 0
+            code = jnp.maximum(codes[slot], 0)
+            tile, band = code // bands, code % bands
+            before = jnp.maximum(codes[jnp.maximum(slot - 1, 0)], 0) // bands
+            place = jnp.where(used, band, bands)
+            slot_bands[0, slot] = place
+            slot_bands[1, slot] = jnp.where(used, tile, all_tiles)
+            slot_bands[2, slot] = (used & (before == tile)).astype(jnp.int32)
+            here = pl.ds(slot, 1)
+            row = jnp.zeros((1, LANES), jnp.float32)
+            start = row + (band * BAND).astype(jnp.float32)
+            shift = row + (offset[0, tile].astype(jnp.float32) + frac[0, tile])
+            inverse = 1.0 / (row + zoom[0, tile] * ratio)
+            slope = jnp.broadcast_to(inverse, (BAND, LANES))
+            first = (start - shift) * inverse
+            slot_lines[0, here, :] = inverse
+            slot_lines[1, here, :] = first
+            slot_lines[2, here, :] = coords(start, frame)
+            cover = cover_of(spots_along((BAND, LANES), 0) * slope + first, source)
+            columns = col_cover[pl.ds(tile, 1), :]
+            for half in range(frame // LANES):
+                part = slice(half * LANES, (half + 1) * LANES)
+                cover_sum[place, :, part] += cover * columns[:, part]
+
+
+def moment_kernel(sizes, zoom, frac, offset, frames, base, parts):
     tiles, bands, frame, source, capacity, devices = sizes
     me = lax.axis_index("tile")
     sec = lax.axis_index("sec")
     sections = lax.axis_size("sec")
     all_tiles = tiles * devices
     ratio = frame / source
-
-    for distance in range(devices):
-        device = me ^ distance
-
-        def note(position, count):
-            tile = device * tiles + position // bands
-            band = position % bands
-            codes[distance * capacity + count] = tile * bands + band
-            return count + (owner[band, 0, tile] == me).astype(jnp.int32)
-
-        count = lax.fori_loop(0, tiles * bands, note, 0, unroll=8)
-
-        def blank(position, carry):
-            codes[distance * capacity + position] = -1
-            return carry
-
-        lax.fori_loop(count, capacity, blank, 0)
-
-    def cover_row(tile, carry):
-        points = points_of(spots_along((1, frame), 1), zoom, frac, offset, 1, tile, ratio)
-        col_cover[pl.ds(tile, 1), :] = cover_of(points, source)
-        return carry
-
-    lax.fori_loop(0, all_tiles, cover_row, 0, unroll=8)
-
-    cover_sum[...] = jnp.zeros_like(cover_sum)
-
-    def describe(slot, carry):
-        code = codes[slot]
-        used = code >= 0
-        code = jnp.maximum(code, 0)
-        tile, band = code // bands, code % bands
-        slot_bands[slot] = jnp.where(used, band, bands)
-        here = pl.ds(slot, 1)
-        row = jnp.zeros((1, LANES), jnp.float32)
-        start = (band * BAND).astype(jnp.float32)
-        scale = row + zoom[0, tile] * ratio
-        slot_lines[0, here, :] = 1.0 / scale
-        slot_lines[1, here, :] = (
-            row + start - offset[0, tile].astype(jnp.float32) - frac[0, tile]
-        ) / scale
-        slot_lines[2, here, :] = coords(row + start, frame)
-        place = jnp.where(used, sec * all_tiles + tile, -1)
-        slot_lines[3, here, :] = row + place.astype(jnp.float32)
-        slot_cover[here, :] = col_cover[pl.ds(tile, 1), :]
-
-        @pl.when(used)
-        def _():
-            points = points_of(
-                spots_along((BAND, frame), 0, band * BAND), zoom, frac, offset, 0, tile, ratio
-            )
-            cover_sum[band] += cover_of(points, source) * col_cover[pl.ds(tile, 1), :]
-
-        return carry
-
-    lax.fori_loop(0, devices * capacity, describe, 0)
-
     parts[...] = jnp.zeros_like(parts)
     for j in range(tiles):
         tile = me * tiles + j
@@ -215,7 +239,8 @@
         y = coords(spots, frame)
         cover = cover_of(points_of(spots, zoom, frac, offset, 0, tile, ratio), source)
         level = frames[j * bands : (j + 1) * bands].reshape(frame, frame).astype(jnp.float32)
-        columns = col_cover[pl.ds(tile, 1), :]
+        columns = points_of(spots_along((1, frame), 1), zoom, frac, offset, 1, tile, ratio)
+        columns = cover_of(columns, source)
         weighted = (cover, cover * y, cover * y * y)
         for power, image in enumerate((None, level, level * level)):
             block = (sec + 1 + power) % sections
@@ -231,29 +256,27 @@
 
 def blend_kernel(sizes, slot_bands, cover_sum, *blocks_and_rest):
     tiles, bands, frame, source, capacity, devices = sizes
-    blocks = blocks_and_rest[:devices]
-    grid, total = blocks_and_rest[devices:]
+    *blocks, grid, total = blocks_and_rest
     total[...] = jnp.zeros_like(total)
-    for distance, block in enumerate(blocks):
+    for block, (array, _) in enumerate(exchange_plan(devices)[1]):
         for k in range(capacity):
-            total[slot_bands[distance * capacity + k]] += block[k].astype(jnp.float32)
-    grid[...] = (total[:bands] / (1.0 + cover_sum[...])).astype(jnp.bfloat16)
+            level = blocks[array][k].astype(jnp.float32)
+            total[slot_bands[0, block * capacity + k]] += level
+    grid[...] = (total[:bands] / (1.0 + cover_sum[:bands])).astype(jnp.bfloat16)
 
 
 GRADIENT_ROWS = ({0: 0, 1: 1}, {2: 0}, {3: 0, 4: 1}, {5: 0})
 
 
 def gradient_kernel(
-    sizes, slot_bands, from_next, top_grid, slot_cover, slot_lines, base, grid, *blocks_and_rest
+    sizes, slot_bands, from_next, top_grid, col_cover, slot_lines, base, grid, *blocks_and_rest
 ):
-    devices = sizes[-1]
-    blocks = blocks_and_rest[:devices]
-    payload, grid_out, above, sums, grid_sem = blocks_and_rest[devices:]
+    tiles, bands, frame, source, capacity, devices = sizes
+    *blocks, payload, grid_out, above, sums, grid_sem = blocks_and_rest
     written = pltpu.make_async_copy(grid, grid_out, grid_sem)
     written.start()
-    tiles, bands, frame, source, capacity, devices = sizes
     sec = lax.axis_index("sec")
-    slots = devices * capacity
+    all_tiles = tiles * devices
     lanes = base.shape[1]
 
     @pl.when(sec == lax.axis_size("sec") - 1)
@@ -265,52 +288,64 @@
         above[:bands] = from_next[...].astype(jnp.float32)
 
     above[bands] = jnp.zeros((BAND, frame), jnp.float32)
+    sums[...] = jnp.zeros_like(sums)
     spots = spots_along((BAND, LANES), 0)
     raised = spots * (2.0 / frame)
-
-    for distance, block in enumerate(blocks):
+    halves = range(frame // LANES)
+
+    for block, (array, _) in enumerate(exchange_plan(devices)[1]):
+        running = None
         for k in range(capacity):
-            slot = distance * capacity + k
+            slot = block * capacity + k
             here = slice(slot, slot + 1)
             points = spots * slot_lines[0, here] + slot_lines[1, here]
             cover = cover_of(points, source)
             lifted = cover * (raised + slot_lines[2, here])
-            level = block[k].astype(jnp.float32)
-            error = above[slot_bands[slot]] - level
+            level = blocks[array][k].astype(jnp.float32)
+            error = above[slot_bands[0, slot]] - level
             product = error * level
-            rows = slice(slot * ROWS, (slot + 1) * ROWS)
-            for half in range(frame // LANES):
+            terms = []
+            for half in halves:
                 part = slice(half * LANES, (half + 1) * LANES)
-                for kind, (weight, value) in enumerate(
-                    ((cover, error), (lifted, error), (cover, product), (lifted, product))
+                for weight, value in (
+                    (cover, error),
+                    (lifted, error),
+                    (cover, product),
+                    (lifted, product),
                 ):
                     term = weight * value[:, part]
-                    sums[kind, half, rows, :] = term[:ROWS] + term[ROWS:]
-    used = slot_lines[3] >= 0.0
-    by_slot = jnp.zeros((ROWS, slots), jnp.float32)
-    for kind, wanted in enumerate(GRADIENT_ROWS):
-        halves = []
-        for half in range(frame // LANES):
-            value = sums[kind, half, pl.ds(0, slots, stride=ROWS), :]
+                    terms.append(term[:ROWS] + term[ROWS:])
+            if running is not None:
+                same = slot_bands[2, slot] == 1
+                terms = [
+                    term + jnp.where(same, before, 0.0) for term, before in zip(terms, running)
+                ]
+            running = terms
+            rows = pl.ds(pl.multiple_of(slot_bands[1, slot] * ROWS, ROWS), ROWS)
+            for index, term in enumerate(terms):
+                sums[index, rows, :] = term
+
+    values = [jnp.zeros((all_tiles, 1), jnp.float32)] * 6
+    for half in halves:
+        columns = col_cover[:, half * LANES : (half + 1) * LANES]
+        x = coords(spots_along((all_tiles, LANES), 1, half * LANES), frame)
+        for kind, wanted in enumerate(GRADIENT_ROWS):
+            index = half * len(GRADIENT_ROWS) + kind
+            value = sums[index, pl.ds(0, all_tiles, stride=ROWS), :]
             for r in range(1, ROWS):
-                value += sums[kind, half, pl.ds(r, slots, stride=ROWS), :]
-            columns = slot_cover[:, half * LANES : (half + 1) * LANES]
-            halves.append(jnp.where(used, value * columns, 0.0))
-        by_slot += exact_dot(feature_rows(frame, wanted), jnp.concatenate(halves, axis=1))
-    places = jnp.concatenate(
-        [
-            (slot_lines[3] == spots_along((slots, LANES), 1, p)).astype(jnp.float32)
-            for p in range(0, lanes, LANES)
-        ],
-        axis=1,
-    )
-    total = base[...] + lax.dot_general(
-        by_slot,
-        places,
-        (((1,), (0,)), ((), ())),
-        precision=lax.Precision.HIGHEST,
-        preferred_element_type=jnp.float32,
-    )
+                value += sums[index, pl.ds(r, all_tiles, stride=ROWS), :]
+            value = value * columns
+            for row, power in wanted.items():
+                term = value * x if power else value
+                values[row] += jnp.sum(term, axis=1, keepdims=True)
+    total = []
+    tile = lax.broadcasted_iota(jnp.int32, (all_tiles, LANES), 0) + sec * all_tiles
+    for first in range(0, lanes, LANES):
+        lane = lax.broadcasted_iota(jnp.int32, (all_tiles, LANES), 1) + first
+        places = (tile == lane).astype(jnp.float32)
+        rows = [jnp.sum(places * value, axis=0, keepdims=True) for value in values]
+        total.append(jnp.concatenate(rows + [jnp.zeros_like(rows[0])] * (ROWS - 6), axis=0))
+    total = base[...] + jnp.concatenate(total, axis=1)
     payload[...] = jnp.broadcast_to(total[None], payload.shape)
     written.wait()
 
@@ -389,8 +424,12 @@
             current = following
 
     first = sec * all_tiles + me * tiles
-    chosen = lax.broadcasted_iota(jnp.int32, (ROWS, lanes), 0) + first == lane
-    own = exact_dot(chosen.astype(jnp.float32), answer)
+    chosen = (row + first == lane).astype(jnp.float32)
+    place = lax.broadcasted_iota(jnp.int32, (ROWS, LANES), 1)
+    own = jnp.zeros((ROWS, LANES), jnp.float32)
+    for f in range(6):
+        value = jnp.sum(chosen * answer[f : f + 1], axis=1, keepdims=True)
+        own = jnp.where(place == f, value, own)
     corrections[...] = own[:tiles, :6]
 
 
@@ -408,13 +447,17 @@
     routes = jnp.transpose(owner, (0, 2, 3, 1))[0]
 
     rows = tiles * bands
-    block = jax.ShapeDtypeStruct((capacity, BAND, frame), jnp.bfloat16)
+    plan, arriving = exchange_plan(devices)
+    blocks = [
+        jax.ShapeDtypeStruct((len(group) * capacity, BAND, frame), jnp.bfloat16)
+        for group in plan
+    ]
     frames, *outgoing = pl.pallas_call(
         functools.partial(render_kernel, sizes),
         name="render",
         in_specs=[HBM] * 5,
-        out_specs=[VMEM] * (1 + devices),
-        out_shape=[jax.ShapeDtypeStruct((rows, BAND, frame), jnp.bfloat16)] + [block] * devices,
+        out_specs=[VMEM] * (1 + len(plan)),
+        out_shape=[jax.ShapeDtypeStruct((rows, BAND, frame), jnp.bfloat16)] + blocks,
         scratch_shapes=[
             pltpu.SMEM(place[0].shape, jnp.float32),
             pltpu.SMEM(place[1].shape, jnp.float32),
@@ -430,37 +473,57 @@
         cost_estimate=cost(800_000_000, 4 << 20),
     )(*(pltpu.with_memory_space_constraint(x, pltpu.HBM) for x in (*place, routes, patches[0])))
 
-    incoming = [outgoing[0]] + [None] * (devices - 1)
-    for distance in sorted(range(1, devices), key=lambda d: (-(d.bit_length()), d)):
-        incoming[distance] = lax.ppermute(
-            outgoing[distance], "tile", [(i, i ^ distance) for i in range(devices)]
-        )
-
-    base, cover_sum, slot_cover, slot_lines, slot_bands = pl.pallas_call(
+    base = pl.pallas_call(
         functools.partial(moment_kernel, sizes),
         name="moments",
-        in_specs=[SMEM] * 4 + [VMEM],
-        out_specs=[VMEM, VMEM, VMEM, VMEM, SMEM],
+        in_specs=[SMEM] * 3 + [VMEM],
+        out_specs=VMEM,
+        out_shape=jax.ShapeDtypeStruct((ROWS, lanes), jnp.float32),
+        scratch_shapes=[pltpu.VMEM((3, lanes, frame), jnp.float32)],
+        compiler_params=params(24),
+        cost_estimate=cost(20_000_000, 1 << 20),
+    )(*place, frames)
+
+    codes = pl.pallas_call(
+        functools.partial(scan_kernel, sizes),
+        name="scan",
+        in_specs=[SMEM],
+        out_specs=SMEM,
+        out_shape=jax.ShapeDtypeStruct((slots + 1,), jnp.int32),
+        compiler_params=params(24),
+        cost_estimate=cost(20_000_000, 1 << 20),
+    )(routes)
+
+    cover_sum, col_cover, slot_lines, slot_bands = pl.pallas_call(
+        functools.partial(slot_kernel, sizes),
+        name="slots",
+        in_specs=[SMEM] * 4,
+        out_specs=[VMEM] * 3 + [SMEM],
         out_shape=[
-            jax.ShapeDtypeStruct((ROWS, lanes), jnp.float32),
-            jax.ShapeDtypeStruct((bands, BAND, frame), jnp.float32),
-            jax.ShapeDtypeStruct((slots, frame), jnp.float32),
-            jax.ShapeDtypeStruct((4, slots, LANES), jnp.float32),
-            jax.ShapeDtypeStruct((slots,), jnp.int32),
+            jax.ShapeDtypeStruct((bands + 1, BAND, frame), jnp.float32),
+            jax.ShapeDtypeStruct((all_tiles, frame), jnp.float32),
+            jax.ShapeDtypeStruct((3, slots, LANES), jnp.float32),
+            jax.ShapeDtypeStruct((3, slots), jnp.int32),
         ],
-        scratch_shapes=[
-            pltpu.SMEM((slots + 1,), jnp.int32),
-            pltpu.VMEM((all_tiles, frame), jnp.float32),
-            pltpu.VMEM((3, lanes, frame), jnp.float32),
-        ],
         compiler_params=params(24),
         cost_estimate=cost(20_000_000, 1 << 20),
-    )(*place, routes, frames)
+    )(*place, codes)
+
+    def swapped(block, distance):
+        return lax.ppermute(block, "tile", [(i, i ^ distance) for i in range(devices)])
+
+    incoming = [outgoing[0]]
+    for block, group in zip(outgoing[1:], plan[1:]):
+        incoming.append(swapped(block, group[0]))
+        if len(group) == 2:
+            passed_on = incoming[-1][capacity:]
+    if devices == 8:
+        incoming.append(swapped(passed_on, 1))
 
     grid = pl.pallas_call(
         functools.partial(blend_kernel, sizes),
         name="blend",
-        in_specs=[SMEM] + [VMEM] * (1 + devices),
+        in_specs=[SMEM] + [VMEM] * (1 + len(incoming)),
         out_specs=VMEM,
         out_shape=jax.ShapeDtypeStruct((bands, BAND, frame), jnp.bfloat16),
         scratch_shapes=[pltpu.VMEM((bands + 1, BAND, frame), jnp.float32)],
@@ -473,7 +536,7 @@
     payload, grid_out = pl.pallas_call(
         functools.partial(gradient_kernel, sizes),
         name="gradient",
-        in_specs=[SMEM] + [VMEM] * (6 + devices),
+        in_specs=[SMEM] + [VMEM] * (6 + len(incoming)),
         out_specs=[VMEM, HBM],
         out_shape=[
             jax.ShapeDtypeStruct((sections * devices, ROWS, lanes), jnp.float32),
@@ -481,7 +544,7 @@
         ],
         scratch_shapes=[
             pltpu.VMEM((bands + 1, BAND, frame), jnp.float32),
-            pltpu.VMEM((4, frame // LANES, slots * ROWS, LANES), jnp.float32),
+            pltpu.VMEM((4 * frame // LANES, (all_tiles + 1) * ROWS, LANES), jnp.float32),
             pltpu.SemaphoreType.DMA,
         ],
         compiler_params=params(24),
@@ -490,7 +553,7 @@
         slot_bands,
         from_next,
         top_grid.reshape(bands, BAND, frame),
-        slot_cover,
+        col_cover,
         slot_lines,
         base,
         grid,

time: 59 us -> 54.9 us (0.931)
  Pallas kernels: 20.8 us -> 16.7 us
  waiting for transfers between devices: 6.47 us -> 7.48 us
  blocking collectives: 18.3 us -> 17.3 us
    pallas_call x1, Pallas kernels: 11.4 us -> 1.88 us  [shards(): pl.pallas_call(functools.partial(moment_kernel, sizes), name='moments', i...]
    pallas_call x0 -> x2, Pallas kernels: none -> 6.83 us  [the longest x1 3.59 us: shards(): pl.pallas_call(functools.partial(slot_kernel, sizes), name='slots', in_sp...]
    ppermute x7, waiting for transfers between devices: 2.92 us -> 6.79 us  [swapped(): lax.ppermute(block, 'tile', [(i, i ^ distance) for i in range(devices)])]
    ppermute x1, waiting for transfers between devices: 3.55 us -> 0.69 us  [shards(): lax.ppermute(grid, 'sec', [(i, (i - 1) % sections) for i in range(section...]
    pallas_call x1, Pallas kernels: 3.08 us -> 2.08 us  [shards(): pl.pallas_call(functools.partial(gradient_kernel, sizes), name='gradient'...]
    all_to_all x1, blocking collectives: 18.3 us -> 17.3 us  [shards(): lax.all_to_all(payload, ('sec', 'tile'), split_axis=0, concat_axis=0, til...]
  transfers between devices with their start and end apart: 8 -> 8, of which waited for: 3 -> 3; matrix products, arithmetic and copies ran while one was open for 0% -> 0% of each run, Pallas kernels for 19% -> 16%
where the time goes in v4:
time: 54.9 us; the launch traced here: 54.5 us
  blocking collectives  17.3 us (32%)
  Pallas kernels  16.7 us (30%)
  starting transfers between devices  12.3 us (22%)
  waiting for transfers between devices  7.48 us (14%)
  between operations  0.76 us (1%)
    all_to_all x1, blocking collectives, shards(): lax.all_to_all(payload, ('sec', 'tile'), split_axis=0, concat_axis=0, til...  17.3 us
    ppermute x7, starting transfers between devices, swapped(): lax.ppermute(block, 'tile', [(i, i ^ distance) for i in range(devices)])  9.85 us
    ppermute x7, waiting for transfers between devices, swapped(): lax.ppermute(block, 'tile', [(i, i ^ distance) for i in range(devices)])  6.79 us
    pallas_call x1, Pallas kernels, shards(): pl.pallas_call(functools.partial(slot_kernel, sizes), name='slots', in_sp...  3.59 us
    pallas_call x1, Pallas kernels, shards(): pl.pallas_call(functools.partial(render_kernel, sizes), name='render', in...  3.33 us
    pallas_call x1, Pallas kernels, shards(): pl.pallas_call(functools.partial(scan_kernel, sizes), name='scan', in_spe...  3.25 us
    ppermute x1, starting transfers between devices, shards(): lax.ppermute(grid, 'sec', [(i, (i - 1) % sections) for i in range(section...  2.45 us
    pallas_call x1, Pallas kernels, shards(): pl.pallas_call(functools.partial(gradient_kernel, sizes), name='gradient'...  2.08 us
  transfers between devices with their start and end apart: 8, of which 3 were waited for; matrix products, arithmetic and copies ran while one was open for 0% of the time, Pallas kernels for 16%

profile of v4, /device:TPU:0, one launch (start us, length us, event | category | flops | bytes accessed | tf_op | source)
XLA Modules:
  0.0 54.5 jit_solution(1784205380387656026)
XLA Ops:
  0.6 0.0 copy-start.4
  0.6 0.0 copy-start.3
  0.7 0.0 copy-start.2
  0.7 0.0 copy-start.1
  0.7 0.0 copy-start
  0.7 3.3 %render.1 = (bf16[64,16,256]{2,1,0:T(8,128)(2,1)S(1)}, bf16[16,16,256]{2,1,0:T(8,128)(2,1)S(1)}, bf16[32,16,256]{2,1,0:T(8,128)(2,1)S(1)}, bf16[16,16,256]{2,1,0...) custom-call(f32[2,32]{1,0:T(2,128)} %bitcast.15, ...), custom_call_target="tpu_custom_call" | custom-call | flops 800000000 | bytes 4194304 | tf_op jit(solution)/shard_map/render/pallas_call | solution.py:455
  4.0 3.1 %collective-permute-start = (bf16[32,16,256]{2,1,0:T(8,128)(2,1)S(1)}, bf16[32,16,256]{2,1,0:T(8,128)(2,1)S(1)}, u32[]{:S(2)}, u32[]{:S(2)}) collective-permute-start(bf16[32,16,256]{2,1,0:T(8,128)(2,1)S(1)} %get-tuple-element.19), channel_id=1, source_target_pairs={{0,2},{1,3},{2,0},{3,1},{4,6},{5,7},{6,4},{7,5},{8,10},{9,11},{10,... | collective-permute-start | bytes 786440 | tf_op jit(solution)/shard_map/ppermute | solution.py:513
  7.1 2.6 %collective-permute-start.1 = (bf16[16,16,256]{2,1,0:T(8,128)(2,1)S(1)}, bf16[16,16,256]{2,1,0:T(8,128)(2,1)S(1)}, u32[]{:S(2)}, u32[]{:S(2)}) collective-permute-start(bf16[16,16,256]{2,1,0:T(8,128)(2,1)S(1)} %get-tuple-element.20), channel_id=1, source_target_pairs={{0,4},{1,5},{2,6},{3,7},{4,0},{5,1},{6,2},{7,3},{8,12},{9,13},{10,... | collective-permute-start | bytes 393224 | tf_op jit(solution)/shard_map/ppermute | solution.py:513
  9.7 0.0 collective-permute-start.2
  9.7 1.7 %collective-permute-start.3 = (bf16[16,16,256]{2,1,0:T(8,128)(2,1)S(1)}, bf16[16,16,256]{2,1,0:T(8,128)(2,1)S(1)}, u32[]{:S(2)}, u32[]{:S(2)}) collective-permute-start(bf16[16,16,256]{2,1,0:T(8,128)(2,1)S(1)} %get-tuple-element.22), channel_id=1, source_target_pairs={{0,6},{1,7},{2,4},{3,5},{4,2},{5,3},{6,0},{7,1},{8,14},{9,15},{10,... | collective-permute-start | bytes 393224 | tf_op jit(solution)/shard_map/ppermute | solution.py:513
  11.4 1.9 %collective-permute-start.4 = (bf16[16,16,256]{2,1,0:T(8,128)(2,1)S(1)}, bf16[16,16,256]{2,1,0:T(8,128)(2,1)S(1)}, u32[]{:S(2)}, u32[]{:S(2)}) collective-permute-start(bf16[16,16,256]{2,1,0:T(8,128)(2,1)S(1)} %get-tuple-element.23), channel_id=1, source_target_pairs={{0,7},{1,6},{2,5},{3,4},{4,3},{5,2},{6,1},{7,0},{8,15},{9,14},{10,... | collective-permute-start | bytes 393224 | tf_op jit(solution)/shard_map/ppermute | solution.py:513
  13.3 5.4 %collective-permute-done.blocks_and_rest_1_ = bf16[32,16,256]{2,1,0:T(8,128)(2,1)S(1)} collective-permute-done((bf16[32,16,256]{2,1,0:T(8,128)(2,1)S(1)}, bf16[32,16,256]{2,1,0:T(8,128)(2,1)S(1)}, u32[]{:S(2)}, u32[]{:S(2)}) %collective-permute-start) | collective-permute-done | bytes 262176 | tf_op jit(solution)/shard_map/ppermute | solution.py:513
  18.7 0.0 collective-permute-start.5
  18.7 0.0 collective-permute-done.1.blocks_and_rest_2_
  18.7 0.6 %collective-permute-start.6 = (bf16[16,16,256]{2,1,0:T(8,128)(2,1)S(1)}, bf16[16,16,256]{2,1,0:T(8,128)(2,1)S(1)}, u32[]{:S(2)}, u32[]{:S(2)}) collective-permute-start(bf16[16,16,256]{2,1,0:T(8,128)(2,1)S(1)} %slice.4), channel_id=1, source_target_pairs={{0,1},{1,0},{2,3},{3,2},{4,5},{5,4},{6,7},{7,6},{8,9},{9,8},{10,11... | collective-permute-start | bytes 393224 | tf_op jit(solution)/shard_map/ppermute | solution.py:513
  19.3 0.0 copy-done.4
  19.3 3.2 %scan.1.codes = s32[129]{0:T(256)S(1)} custom-call(s32[16,1,32]{2,1,0:T(1,128)S(1)} %bitcast.25), custom_call_target="tpu_custom_call" | custom-call | flops 20000000 | bytes 1048576 | tf_op jit(solution)/shard_map/scan/pallas_call | solution.py:487
  22.6 0.0 copy-done.3
  22.6 0.0 copy-done.2
  22.6 0.0 copy-done.1
  22.6 3.6 %slots.1 = (f32[17,16,256]{2,1,0:T(8,128)S(1)}, f32[32,256]{1,0:T(8,128)S(1)}, f32[3,128,128]{2,1,0:T(8,128)S(1)}, s32[3,128]{1,0:T(4,128)S(1)}) custom-call(f32[2,32]{1,0:T(2,128)S(1)} %bitcast.16, f32[2,32]{1,0:T(2,128)S(1)} %bitcast.19, s32[2,32]{1,0:T(2,128)S(1)} %bitcast.22, s32[129]{0:T(256)S(1)} %scan.1.codes), custom_call_target="tpu_custom_call" | custom-call | flops 20000000 | bytes 1048576 | tf_op jit(solution)/shard_map/slots/pallas_call | solution.py:497
  26.2 1.4 %collective-permute-done.2.blocks_and_rest_3_ = bf16[16,16,256]{2,1,0:T(8,128)(2,1)S(1)} collective-permute-done((bf16[16,16,256]{2,1,0:T(8,128)(2,1)S(1)}, bf16[16,16,256]{2,1,0:T(8,128)(2,1)S(1)}, u32[]{:S(2)}, u32[]{:S(2)}) %collective-permute-start.2) | collective-permute-done | bytes 131104 | tf_op jit(solution)/shard_map/ppermute | solution.py:513
  27.6 0.0 collective-permute-done.3.blocks_and_rest_4_
  27.6 0.0 collective-permute-done.4.blocks_and_rest_5_
  27.6 0.0 collective-permute-done.5.blocks_and_rest_6_
  27.6 0.0 collective-permute-done.6.blocks_and_rest_7_
  27.6 1.3 %blend.1.grid = bf16[16,16,256]{2,1,0:T(8,128)(2,1)S(1)} custom-call(s32[3,128]{1,0:T(4,128)S(1)} %get-tuple-element.16.slot_bands, f32[17,16,256]{2,1,0:T(8,128)S(1)} %get-tuple-element.17.cover_sum, bf16[16,16,256]{2,1,0:T(8,128)(2,1)S(1)} %get-tuple-element.18.blocks_and_rest_0_, bf16[32,16,256]{2,1,0:T(8,128)(2,1)S(1)} %collective-permute-done.blocks_and_rest_1_, ...), custom_call_target="tpu_custom_call" | custom-call | flops 1000000 | bytes 2097152 | tf_op jit(solution)/shard_map/blend/pallas_call | solution.py:523
  28.9 2.4 %collective-permute-start.7 = (bf16[16,16,256]{2,1,0:T(8,128)(2,1)S(1)}, bf16[16,16,256]{2,1,0:T(8,128)(2,1)S(1)}, u32[]{:S(2)}, u32[]{:S(2)}) collective-permute-start(bf16[16,16,256]{2,1,0:T(8,128)(2,1)S(1)} %blend.1.grid), channel_id=1, source_target_pairs={{0,24},{8,0},{16,8},{24,16},{1,25},{9,1},{17,9},{25,17},{2,26},{10... | collective-permute-start | bytes 393224 | tf_op jit(solution)/shard_map/ppermute | solution.py:534
  31.4 1.9 %moments.1.base = f32[8,128]{1,0:T(8,128)S(1)} custom-call(f32[2,32]{1,0:T(2,128)S(1)} %bitcast.17, f32[2,32]{1,0:T(2,128)S(1)} %bitcast.20, s32[2,32]{1,0:T(2,128)S(1)} %bitcast.23, bf16[64,16,256]{2,1,0:T(8,128)(2,1)S(1)} %get-tuple-element.27.frames), custom_call_target="tpu_custom_call" | custom-call | flops 20000000 | bytes 1048576 | tf_op jit(solution)/shard_map/moments/pallas_call | solution.py:476
  33.3 0.7 %collective-permute-done.7.from_next = bf16[16,16,256]{2,1,0:T(8,128)(2,1)S(1)} collective-permute-done((bf16[16,16,256]{2,1,0:T(8,128)(2,1)S(1)}, bf16[16,16,256]{2,1,0:T(8,128)(2,1)S(1)}, u32[]{:S(2)}, u32[]{:S(2)}) %collective-permute-start.7) | collective-permute-done | bytes 131104 | tf_op jit(solution)/shard_map/ppermute | solution.py:534
  34.0 0.0 copy-done
  34.0 2.1 %gradient.1 = (f32[32,8,128]{2,1,0:T(8,128)S(1)}, bf16[16,16,256]{2,1,0:T(8,128)(2,1)}) custom-call(s32[3,128]{1,0:T(4,128)S(1)} %get-tuple-element.16.slot_bands, bf16[16,16,256]{2,1,0:T(8,128)(2,1)S(1)} %collective-permute-done.7.from_next, bf16[16,16,256]{2,1,0:T(8,128)(2,1)S(1)} %bitcast.14, f32[32,256]{1,0:T(8,128)S(1)} %get-tuple-element.25.col_cover, ...), custom_call_target="tpu_custom_call" | custom-call | flops 8000000 | bytes 2097152 | tf_op jit(solution)/shard_map/gradient/pallas_call | solution.py:536
  36.0 17.3 %all_to_all.5.received = f32[32,8,128]{2,1,0:T(8,128)S(1)} all-to-all(f32[32,8,128]{2,1,0:T(8,128)S(1)} %get-tuple-element.29), channel_id=1, replica_groups=mesh['sec'=4,'tile'=8] {'sec','tile'}, dimensions={0} | all-to-all | bytes 262144 | tf_op jit(solution)/shard_map/all_to_all | solution.py:563
  53.3 1.2 %solve.1 = f32[4,6]{1,0:T(4,128)} custom-call(f32[32,8,128]{2,1,0:T(8,128)S(1)} %all_to_all.5.received), custom_call_target="tpu_custom_call" | custom-call | flops 100000 | bytes 262144 | tf_op jit(solution)/shard_map/solve/pallas_call | solution.py:567
  (1 shorter events, 0.0 us)
Async XLA Ops:
  0.6 18.7 %copy-start.4 = (s32[1,32,16,1]{1,3,2,0:T(1,128)S(1)}, s32[1,32,16,1]{1,3,2,0:T(1,128)}, u32[]{:S(2)}) copy-start(s32[1,32,16,1]{1,3,2,0:T(1,128)} %param.10) | copy-start | bytes 6148
  0.6 21.9 %copy-start.3 = (s32[1,2,32]{2,1,0:T(2,128)S(1)}, s32[1,2,32]{2,1,0:T(2,128)}, u32[]{:S(2)}) copy-start(s32[1,2,32]{2,1,0:T(2,128)} %param.9) | copy-start | bytes 772
  0.7 21.9 %copy-start.2 = (f32[1,2,32]{2,1,0:T(2,128)S(1)}, f32[1,2,32]{2,1,0:T(2,128)}, u32[]{:S(2)}) copy-start(f32[1,2,32]{2,1,0:T(2,128)} %param.8) | copy-start | bytes 772
  0.7 21.9 %copy-start.1 = (f32[1,2,32]{2,1,0:T(2,128)S(1)}, f32[1,2,32]{2,1,0:T(2,128)}, u32[]{:S(2)}) copy-start(f32[1,2,32]{2,1,0:T(2,128)} %param.7) | copy-start | bytes 772
  0.7 33.3 %copy-start = (bf16[1,256,256]{2,1,0:T(8,128)(2,1)S(1)}, bf16[1,256,256]{2,1,0:T(8,128)(2,1)}, u32[]{:S(2)}) copy-start(bf16[1,256,256]{2,1,0:T(8,128)(2,1)} %param.11) | copy-start | bytes 393220
  4.0 14.7 %collective-permute-start = (bf16[32,16,256]{2,1,0:T(8,128)(2,1)S(1)}, bf16[32,16,256]{2,1,0:T(8,128)(2,1)S(1)}, u32[]{:S(2)}, u32[]{:S(2)}) collective-permute-start(bf16[32,16,256]{2,1,0:T(8,128)(2,1)S(1)} %get-tuple-element.19), channel_id=1, source_target_pairs={{0,2},{1,3},{2,0},{3,1},{4,6},{5,7},{6,4},{7,5},{8,10},{9,11},{10,... | collective-permute-start | bytes 786440 | tf_op jit(solution)/shard_map/ppermute | solution.py:513
  7.1 11.6 %collective-permute-start.1 = (bf16[16,16,256]{2,1,0:T(8,128)(2,1)S(1)}, bf16[16,16,256]{2,1,0:T(8,128)(2,1)S(1)}, u32[]{:S(2)}, u32[]{:S(2)}) collective-permute-start(bf16[16,16,256]{2,1,0:T(8,128)(2,1)S(1)} %get-tuple-element.20), channel_id=1, source_target_pairs={{0,4},{1,5},{2,6},{3,7},{4,0},{5,1},{6,2},{7,3},{8,12},{9,13},{10,... | collective-permute-start | bytes 393224 | tf_op jit(solution)/shard_map/ppermute | solution.py:513
  9.7 17.9 %collective-permute-start.2 = (bf16[16,16,256]{2,1,0:T(8,128)(2,1)S(1)}, bf16[16,16,256]{2,1,0:T(8,128)(2,1)S(1)}, u32[]{:S(2)}, u32[]{:S(2)}) collective-permute-start(bf16[16,16,256]{2,1,0:T(8,128)(2,1)S(1)} %get-tuple-element.21), channel_id=1, source_target_pairs={{0,5},{1,4},{2,7},{3,6},{4,1},{5,0},{6,3},{7,2},{8,13},{9,12},{10,... | collective-permute-start | bytes 393224 | tf_op jit(solution)/shard_map/ppermute | solution.py:513
  9.7 17.9 %collective-permute-start.3 = (bf16[16,16,256]{2,1,0:T(8,128)(2,1)S(1)}, bf16[16,16,256]{2,1,0:T(8,128)(2,1)S(1)}, u32[]{:S(2)}, u32[]{:S(2)}) collective-permute-start(bf16[16,16,256]{2,1,0:T(8,128)(2,1)S(1)} %get-tuple-element.22), channel_id=1, source_target_pairs={{0,6},{1,7},{2,4},{3,5},{4,2},{5,3},{6,0},{7,1},{8,14},{9,15},{10,... | collective-permute-start | bytes 393224 | tf_op jit(solution)/shard_map/ppermute | solution.py:513
  11.4 16.2 %collective-permute-start.4 = (bf16[16,16,256]{2,1,0:T(8,128)(2,1)S(1)}, bf16[16,16,256]{2,1,0:T(8,128)(2,1)S(1)}, u32[]{:S(2)}, u32[]{:S(2)}) collective-permute-start(bf16[16,16,256]{2,1,0:T(8,128)(2,1)S(1)} %get-tuple-element.23), channel_id=1, source_target_pairs={{0,7},{1,6},{2,5},{3,4},{4,3},{5,2},{6,1},{7,0},{8,15},{9,14},{10,... | collective-permute-start | bytes 393224 | tf_op jit(solution)/shard_map/ppermute | solution.py:513
  18.7 8.9 %collective-permute-start.5 = (bf16[16,16,256]{2,1,0:T(8,128)(2,1)S(1)}, bf16[16,16,256]{2,1,0:T(8,128)(2,1)S(1)}, u32[]{:S(2)}, u32[]{:S(2)}) collective-permute-start(bf16[16,16,256]{2,1,0:T(8,128)(2,1)S(1)} %get-tuple-element.24), channel_id=1, source_target_pairs={{0,1},{1,0},{2,3},{3,2},{4,5},{5,4},{6,7},{7,6},{8,9},{9,8},{10,11... | collective-permute-start | bytes 393224 | tf_op jit(solution)/shard_map/ppermute | solution.py:513
  18.7 8.8 %collective-permute-start.6 = (bf16[16,16,256]{2,1,0:T(8,128)(2,1)S(1)}, bf16[16,16,256]{2,1,0:T(8,128)(2,1)S(1)}, u32[]{:S(2)}, u32[]{:S(2)}) collective-permute-start(bf16[16,16,256]{2,1,0:T(8,128)(2,1)S(1)} %slice.4), channel_id=1, source_target_pairs={{0,1},{1,0},{2,3},{3,2},{4,5},{5,4},{6,7},{7,6},{8,9},{9,8},{10,11... | collective-permute-start | bytes 393224 | tf_op jit(solution)/shard_map/ppermute | solution.py:513
  28.9 5.0 %collective-permute-start.7 = (bf16[16,16,256]{2,1,0:T(8,128)(2,1)S(1)}, bf16[16,16,256]{2,1,0:T(8,128)(2,1)S(1)}, u32[]{:S(2)}, u32[]{:S(2)}) collective-permute-start(bf16[16,16,256]{2,1,0:T(8,128)(2,1)S(1)} %blend.1.grid), channel_id=1, source_target_pairs={{0,24},{8,0},{16,8},{24,16},{1,25},{9,1},{17,9},{25,17},{2,26},{10... | collective-permute-start | bytes 393224 | tf_op jit(solution)/shard_map/ppermute | solution.py:534

commit v5 on v4

--- a/solution.py
+++ b/solution.py
@@ -503,7 +503,7 @@
             jax.ShapeDtypeStruct((bands + 1, BAND, frame), jnp.float32),
             jax.ShapeDtypeStruct((all_tiles, frame), jnp.float32),
             jax.ShapeDtypeStruct((3, slots, LANES), jnp.float32),
-            jax.ShapeDtypeStruct((3, slots), jnp.int32),
+            pltpu.SMEM((3, slots), jnp.int32),
         ],
         compiler_params=params(24),
         cost_estimate=cost(20_000_000, 1 << 20),
@@ -529,7 +529,7 @@
         scratch_shapes=[pltpu.VMEM((bands + 1, BAND, frame), jnp.float32)],
         compiler_params=params(24),
         cost_estimate=cost(1_000_000, 2 << 20),
-    )(slot_bands, cover_sum, *incoming)
+    )(pltpu.with_memory_space_constraint(slot_bands, pltpu.SMEM), cover_sum, *incoming)
 
     from_next = lax.ppermute(grid, "sec", [(i, (i - 1) % sections) for i in range(sections)])
 
@@ -550,7 +550,7 @@
         compiler_params=params(24),
         cost_estimate=cost(8_000_000, 2 << 20),
     )(
-        slot_bands,
+        pltpu.with_memory_space_constraint(slot_bands, pltpu.SMEM),
         from_next,
         top_grid.reshape(bands, BAND, frame),
         col_cover,

time: 54.9 us -> 53.6 us (0.976)
  Pallas kernels: 16.7 us -> 15 us
    pallas_call x1, Pallas kernels: 3.59 us -> 2.97 us  [shards(): pl.pallas_call(functools.partial(slot_kernel, sizes), name='slots', in_sp...]
    ppermute x7, waiting for transfers between devices: 6.79 us -> 7.38 us  [swapped(): lax.ppermute(block, 'tile', [(i, i ^ distance) for i in range(devices)])]
    pallas_call x1, Pallas kernels: 2.08 us -> 1.5 us  [shards(): pl.pallas_call(functools.partial(gradient_kernel, sizes), name='gradient'...]
  transfers between devices with their start and end apart: 8 -> 8, of which waited for: 3 -> 3; matrix products, arithmetic and copies ran while one was open for 0% -> 0% of each run, Pallas kernels for 16% -> 15%
where the time goes in v5:
time: 53.6 us; the launch traced here: 53.4 us
  blocking collectives  17.3 us (32%)
  Pallas kernels  15 us (28%)
  starting transfers between devices  12.4 us (23%)
  waiting for transfers between devices  8.02 us (15%)
  between operations  0.76 us (1%)
    all_to_all x1, blocking collectives, shards(): lax.all_to_all(payload, ('sec', 'tile'), split_axis=0, concat_axis=0, til...  17.3 us
    ppermute x7, starting transfers between devices, swapped(): lax.ppermute(block, 'tile', [(i, i ^ distance) for i in range(devices)])  9.85 us
    ppermute x7, waiting for transfers between devices, swapped(): lax.ppermute(block, 'tile', [(i, i ^ distance) for i in range(devices)])  7.38 us
    pallas_call x1, Pallas kernels, shards(): pl.pallas_call(functools.partial(render_kernel, sizes), name='render', in...  3.33 us
    pallas_call x1, Pallas kernels, shards(): pl.pallas_call(functools.partial(scan_kernel, sizes), name='scan', in_spe...  3.29 us
    pallas_call x1, Pallas kernels, shards(): pl.pallas_call(functools.partial(slot_kernel, sizes), name='slots', in_sp...  2.97 us
    ppermute x1, starting transfers between devices, shards(): lax.ppermute(grid, 'sec', [(i, (i - 1) % sections) for i in range(section...  2.51 us
    pallas_call x1, Pallas kernels, shards(): pl.pallas_call(functools.partial(moment_kernel, sizes), name='moments', i...  1.88 us
  transfers between devices with their start and end apart: 8, of which 3 were waited for; matrix products, arithmetic and copies ran while one was open for 0% of the time, Pallas kernels for 15%

profile of v5, /device:TPU:0, one launch (start us, length us, event | category | flops | bytes accessed | tf_op | source)
XLA Modules:
  0.0 53.4 jit_solution(15086709817486256030)
XLA Ops:
  0.6 0.0 copy-start.4
  0.6 0.0 copy-start.3
  0.7 0.0 copy-start.2
  0.7 0.0 copy-start.1
  0.7 0.0 copy-start
  0.7 3.3 %render.1 = (bf16[64,16,256]{2,1,0:T(8,128)(2,1)S(1)}, bf16[16,16,256]{2,1,0:T(8,128)(2,1)S(1)}, bf16[32,16,256]{2,1,0:T(8,128)(2,1)S(1)}, bf16[16,16,256]{2,1,0...) custom-call(f32[2,32]{1,0:T(2,128)} %bitcast.15, ...), custom_call_target="tpu_custom_call" | custom-call | flops 800000000 | bytes 4194304 | tf_op jit(solution)/shard_map/render/pallas_call | solution.py:455
  4.0 3.1 %collective-permute-start = (bf16[32,16,256]{2,1,0:T(8,128)(2,1)S(1)}, bf16[32,16,256]{2,1,0:T(8,128)(2,1)S(1)}, u32[]{:S(2)}, u32[]{:S(2)}) collective-permute-start(bf16[32,16,256]{2,1,0:T(8,128)(2,1)S(1)} %get-tuple-element.19), channel_id=1, source_target_pairs={{0,2},{1,3},{2,0},{3,1},{4,6},{5,7},{6,4},{7,5},{8,10},{9,11},{10,... | collective-permute-start | bytes 786440 | tf_op jit(solution)/shard_map/ppermute | solution.py:513
  7.1 2.6 %collective-permute-start.1 = (bf16[16,16,256]{2,1,0:T(8,128)(2,1)S(1)}, bf16[16,16,256]{2,1,0:T(8,128)(2,1)S(1)}, u32[]{:S(2)}, u32[]{:S(2)}) collective-permute-start(bf16[16,16,256]{2,1,0:T(8,128)(2,1)S(1)} %get-tuple-element.20), channel_id=1, source_target_pairs={{0,4},{1,5},{2,6},{3,7},{4,0},{5,1},{6,2},{7,3},{8,12},{9,13},{10,... | collective-permute-start | bytes 393224 | tf_op jit(solution)/shard_map/ppermute | solution.py:513
  9.7 0.0 collective-permute-start.2
  9.7 1.7 %collective-permute-start.3 = (bf16[16,16,256]{2,1,0:T(8,128)(2,1)S(1)}, bf16[16,16,256]{2,1,0:T(8,128)(2,1)S(1)}, u32[]{:S(2)}, u32[]{:S(2)}) collective-permute-start(bf16[16,16,256]{2,1,0:T(8,128)(2,1)S(1)} %get-tuple-element.22), channel_id=1, source_target_pairs={{0,6},{1,7},{2,4},{3,5},{4,2},{5,3},{6,0},{7,1},{8,14},{9,15},{10,... | collective-permute-start | bytes 393224 | tf_op jit(solution)/shard_map/ppermute | solution.py:513
  11.4 1.9 %collective-permute-start.4 = (bf16[16,16,256]{2,1,0:T(8,128)(2,1)S(1)}, bf16[16,16,256]{2,1,0:T(8,128)(2,1)S(1)}, u32[]{:S(2)}, u32[]{:S(2)}) collective-permute-start(bf16[16,16,256]{2,1,0:T(8,128)(2,1)S(1)} %get-tuple-element.23), channel_id=1, source_target_pairs={{0,7},{1,6},{2,5},{3,4},{4,3},{5,2},{6,1},{7,0},{8,15},{9,14},{10,... | collective-permute-start | bytes 393224 | tf_op jit(solution)/shard_map/ppermute | solution.py:513
  13.3 5.4 %collective-permute-done.blocks_and_rest_1_ = bf16[32,16,256]{2,1,0:T(8,128)(2,1)S(1)} collective-permute-done((bf16[32,16,256]{2,1,0:T(8,128)(2,1)S(1)}, bf16[32,16,256]{2,1,0:T(8,128)(2,1)S(1)}, u32[]{:S(2)}, u32[]{:S(2)}) %collective-permute-start) | collective-permute-done | bytes 262176 | tf_op jit(solution)/shard_map/ppermute | solution.py:513
  18.7 0.0 collective-permute-start.5
  18.7 0.0 collective-permute-done.1.blocks_and_rest_2_
  18.7 0.6 %collective-permute-start.6 = (bf16[16,16,256]{2,1,0:T(8,128)(2,1)S(1)}, bf16[16,16,256]{2,1,0:T(8,128)(2,1)S(1)}, u32[]{:S(2)}, u32[]{:S(2)}) collective-permute-start(bf16[16,16,256]{2,1,0:T(8,128)(2,1)S(1)} %slice.4), channel_id=1, source_target_pairs={{0,1},{1,0},{2,3},{3,2},{4,5},{5,4},{6,7},{7,6},{8,9},{9,8},{10,11... | collective-permute-start | bytes 393224 | tf_op jit(solution)/shard_map/ppermute | solution.py:513
  19.3 0.0 copy-done.4
  19.3 3.3 %scan.1.codes = s32[129]{0:T(256)S(1)} custom-call(s32[16,1,32]{2,1,0:T(1,128)S(1)} %bitcast.25), custom_call_target="tpu_custom_call" | custom-call | flops 20000000 | bytes 1048576 | tf_op jit(solution)/shard_map/scan/pallas_call | solution.py:487
  22.6 0.0 copy-done.3
  22.6 0.0 copy-done.2
  22.6 0.0 copy-done.1
  22.6 3.0 %slots.1 = (f32[17,16,256]{2,1,0:T(8,128)S(1)}, f32[32,256]{1,0:T(8,128)S(1)}, f32[3,128,128]{2,1,0:T(8,128)S(1)}, s32[3,128]{1,0:T(4,128)S(4)}) custom-call(f32[2,32]{1,0:T(2,128)S(1)} %bitcast.16, f32[2,32]{1,0:T(2,128)S(1)} %bitcast.19, s32[2,32]{1,0:T(2,128)S(1)} %bitcast.22, s32[129]{0:T(256)S(1)} %scan.1.codes), custom_call_target="tpu_custom_call" | custom-call | flops 20000000 | bytes 1048576 | tf_op jit(solution)/shard_map/slots/pallas_call | solution.py:497
  25.6 1.9 %collective-permute-done.2.blocks_and_rest_3_ = bf16[16,16,256]{2,1,0:T(8,128)(2,1)S(1)} collective-permute-done((bf16[16,16,256]{2,1,0:T(8,128)(2,1)S(1)}, bf16[16,16,256]{2,1,0:T(8,128)(2,1)S(1)}, u32[]{:S(2)}, u32[]{:S(2)}) %collective-permute-start.2) | collective-permute-done | bytes 131104 | tf_op jit(solution)/shard_map/ppermute | solution.py:513
  27.6 0.0 collective-permute-done.3.blocks_and_rest_4_
  27.6 0.0 collective-permute-done.4.blocks_and_rest_5_
  27.6 0.0 collective-permute-done.5.blocks_and_rest_6_
  27.6 0.0 collective-permute-done.6.blocks_and_rest_7_
  27.6 0.8 %blend.1.grid = bf16[16,16,256]{2,1,0:T(8,128)(2,1)S(1)} custom-call(s32[3,128]{1,0:T(4,128)S(4)} %get-tuple-element.16.slot_bands, f32[17,16,256]{2,1,0:T(8,128)S(1)} %get-tuple-element.17.cover_sum, bf16[16,16,256]{2,1,0:T(8,128)(2,1)S(1)} %get-tuple-element.18.blocks_and_rest_0_, bf16[32,16,256]{2,1,0:T(8,128)(2,1)S(1)} %collective-permute-done.blocks_and_rest_1_, ...), custom_call_target="tpu_custom_call" | custom-call | flops 1000000 | bytes 2097152 | tf_op jit(solution)/shard_map/blend/pallas_call | solution.py:523
  28.4 2.5 %collective-permute-start.7 = (bf16[16,16,256]{2,1,0:T(8,128)(2,1)S(1)}, bf16[16,16,256]{2,1,0:T(8,128)(2,1)S(1)}, u32[]{:S(2)}, u32[]{:S(2)}) collective-permute-start(bf16[16,16,256]{2,1,0:T(8,128)(2,1)S(1)} %blend.1.grid), channel_id=1, source_target_pairs={{0,24},{8,0},{16,8},{24,16},{1,25},{9,1},{17,9},{25,17},{2,26},{10... | collective-permute-start | bytes 393224 | tf_op jit(solution)/shard_map/ppermute | solution.py:534
  30.9 1.9 %moments.1.base = f32[8,128]{1,0:T(8,128)S(1)} custom-call(f32[2,32]{1,0:T(2,128)S(1)} %bitcast.17, f32[2,32]{1,0:T(2,128)S(1)} %bitcast.20, s32[2,32]{1,0:T(2,128)S(1)} %bitcast.23, bf16[64,16,256]{2,1,0:T(8,128)(2,1)S(1)} %get-tuple-element.27.frames), custom_call_target="tpu_custom_call" | custom-call | flops 20000000 | bytes 1048576 | tf_op jit(solution)/shard_map/moments/pallas_call | solution.py:476
  32.8 0.6 %collective-permute-done.7.from_next = bf16[16,16,256]{2,1,0:T(8,128)(2,1)S(1)} collective-permute-done((bf16[16,16,256]{2,1,0:T(8,128)(2,1)S(1)}, bf16[16,16,256]{2,1,0:T(8,128)(2,1)S(1)}, u32[]{:S(2)}, u32[]{:S(2)}) %collective-permute-start.7) | collective-permute-done | bytes 131104 | tf_op jit(solution)/shard_map/ppermute | solution.py:534
  33.4 0.0 copy-done
  33.4 1.5 %gradient.1 = (f32[32,8,128]{2,1,0:T(8,128)S(1)}, bf16[16,16,256]{2,1,0:T(8,128)(2,1)}) custom-call(s32[3,128]{1,0:T(4,128)S(4)} %get-tuple-element.16.slot_bands, bf16[16,16,256]{2,1,0:T(8,128)(2,1)S(1)} %collective-permute-done.7.from_next, bf16[16,16,256]{2,1,0:T(8,128)(2,1)S(1)} %bitcast.14, f32[32,256]{1,0:T(8,128)S(1)} %get-tuple-element.25.col_cover, ...), custom_call_target="tpu_custom_call" | custom-call | flops 8000000 | bytes 2097152 | tf_op jit(solution)/shard_map/gradient/pallas_call | solution.py:536
  34.9 17.3 %all_to_all.5.received = f32[32,8,128]{2,1,0:T(8,128)S(1)} all-to-all(f32[32,8,128]{2,1,0:T(8,128)S(1)} %get-tuple-element.29), channel_id=1, replica_groups=mesh['sec'=4,'tile'=8] {'sec','tile'}, dimensions={0} | all-to-all | bytes 262144 | tf_op jit(solution)/shard_map/all_to_all | solution.py:563
  52.3 1.2 %solve.1 = f32[4,6]{1,0:T(4,128)} custom-call(f32[32,8,128]{2,1,0:T(8,128)S(1)} %all_to_all.5.received), custom_call_target="tpu_custom_call" | custom-call | flops 100000 | bytes 262144 | tf_op jit(solution)/shard_map/solve/pallas_call | solution.py:567
  (1 shorter events, 0.0 us)
Async XLA Ops:
  0.6 18.7 %copy-start.4 = (s32[1,32,16,1]{1,3,2,0:T(1,128)S(1)}, s32[1,32,16,1]{1,3,2,0:T(1,128)}, u32[]{:S(2)}) copy-start(s32[1,32,16,1]{1,3,2,0:T(1,128)} %param.10) | copy-start | bytes 6148
  0.6 22.0 %copy-start.3 = (s32[1,2,32]{2,1,0:T(2,128)S(1)}, s32[1,2,32]{2,1,0:T(2,128)}, u32[]{:S(2)}) copy-start(s32[1,2,32]{2,1,0:T(2,128)} %param.9) | copy-start | bytes 772
  0.7 22.0 %copy-start.2 = (f32[1,2,32]{2,1,0:T(2,128)S(1)}, f32[1,2,32]{2,1,0:T(2,128)}, u32[]{:S(2)}) copy-start(f32[1,2,32]{2,1,0:T(2,128)} %param.8) | copy-start | bytes 772
  0.7 22.0 %copy-start.1 = (f32[1,2,32]{2,1,0:T(2,128)S(1)}, f32[1,2,32]{2,1,0:T(2,128)}, u32[]{:S(2)}) copy-start(f32[1,2,32]{2,1,0:T(2,128)} %param.7) | copy-start | bytes 772
  0.7 32.8 %copy-start = (bf16[1,256,256]{2,1,0:T(8,128)(2,1)S(1)}, bf16[1,256,256]{2,1,0:T(8,128)(2,1)}, u32[]{:S(2)}) copy-start(bf16[1,256,256]{2,1,0:T(8,128)(2,1)} %param.11) | copy-start | bytes 393220
  4.0 14.7 %collective-permute-start = (bf16[32,16,256]{2,1,0:T(8,128)(2,1)S(1)}, bf16[32,16,256]{2,1,0:T(8,128)(2,1)S(1)}, u32[]{:S(2)}, u32[]{:S(2)}) collective-permute-start(bf16[32,16,256]{2,1,0:T(8,128)(2,1)S(1)} %get-tuple-element.19), channel_id=1, source_target_pairs={{0,2},{1,3},{2,0},{3,1},{4,6},{5,7},{6,4},{7,5},{8,10},{9,11},{10,... | collective-permute-start | bytes 786440 | tf_op jit(solution)/shard_map/ppermute | solution.py:513
  7.1 11.6 %collective-permute-start.1 = (bf16[16,16,256]{2,1,0:T(8,128)(2,1)S(1)}, bf16[16,16,256]{2,1,0:T(8,128)(2,1)S(1)}, u32[]{:S(2)}, u32[]{:S(2)}) collective-permute-start(bf16[16,16,256]{2,1,0:T(8,128)(2,1)S(1)} %get-tuple-element.20), channel_id=1, source_target_pairs={{0,4},{1,5},{2,6},{3,7},{4,0},{5,1},{6,2},{7,3},{8,12},{9,13},{10,... | collective-permute-start | bytes 393224 | tf_op jit(solution)/shard_map/ppermute | solution.py:513
  9.7 17.9 %collective-permute-start.2 = (bf16[16,16,256]{2,1,0:T(8,128)(2,1)S(1)}, bf16[16,16,256]{2,1,0:T(8,128)(2,1)S(1)}, u32[]{:S(2)}, u32[]{:S(2)}) collective-permute-start(bf16[16,16,256]{2,1,0:T(8,128)(2,1)S(1)} %get-tuple-element.21), channel_id=1, source_target_pairs={{0,5},{1,4},{2,7},{3,6},{4,1},{5,0},{6,3},{7,2},{8,13},{9,12},{10,... | collective-permute-start | bytes 393224 | tf_op jit(solution)/shard_map/ppermute | solution.py:513
  9.7 17.9 %collective-permute-start.3 = (bf16[16,16,256]{2,1,0:T(8,128)(2,1)S(1)}, bf16[16,16,256]{2,1,0:T(8,128)(2,1)S(1)}, u32[]{:S(2)}, u32[]{:S(2)}) collective-permute-start(bf16[16,16,256]{2,1,0:T(8,128)(2,1)S(1)} %get-tuple-element.22), channel_id=1, source_target_pairs={{0,6},{1,7},{2,4},{3,5},{4,2},{5,3},{6,0},{7,1},{8,14},{9,15},{10,... | collective-permute-start | bytes 393224 | tf_op jit(solution)/shard_map/ppermute | solution.py:513
  11.4 16.2 %collective-permute-start.4 = (bf16[16,16,256]{2,1,0:T(8,128)(2,1)S(1)}, bf16[16,16,256]{2,1,0:T(8,128)(2,1)S(1)}, u32[]{:S(2)}, u32[]{:S(2)}) collective-permute-start(bf16[16,16,256]{2,1,0:T(8,128)(2,1)S(1)} %get-tuple-element.23), channel_id=1, source_target_pairs={{0,7},{1,6},{2,5},{3,4},{4,3},{5,2},{6,1},{7,0},{8,15},{9,14},{10,... | collective-permute-start | bytes 393224 | tf_op jit(solution)/shard_map/ppermute | solution.py:513
  18.7 8.9 %collective-permute-start.5 = (bf16[16,16,256]{2,1,0:T(8,128)(2,1)S(1)}, bf16[16,16,256]{2,1,0:T(8,128)(2,1)S(1)}, u32[]{:S(2)}, u32[]{:S(2)}) collective-permute-start(bf16[16,16,256]{2,1,0:T(8,128)(2,1)S(1)} %get-tuple-element.24), channel_id=1, source_target_pairs={{0,1},{1,0},{2,3},{3,2},{4,5},{5,4},{6,7},{7,6},{8,9},{9,8},{10,11... | collective-permute-start | bytes 393224 | tf_op jit(solution)/shard_map/ppermute | solution.py:513
  18.7 8.8 %collective-permute-start.6 = (bf16[16,16,256]{2,1,0:T(8,128)(2,1)S(1)}, bf16[16,16,256]{2,1,0:T(8,128)(2,1)S(1)}, u32[]{:S(2)}, u32[]{:S(2)}) collective-permute-start(bf16[16,16,256]{2,1,0:T(8,128)(2,1)S(1)} %slice.4), channel_id=1, source_target_pairs={{0,1},{1,0},{2,3},{3,2},{4,5},{5,4},{6,7},{7,6},{8,9},{9,8},{10,11... | collective-permute-start | bytes 393224 | tf_op jit(solution)/shard_map/ppermute | solution.py:513
  28.4 5.0 %collective-permute-start.7 = (bf16[16,16,256]{2,1,0:T(8,128)(2,1)S(1)}, bf16[16,16,256]{2,1,0:T(8,128)(2,1)S(1)}, u32[]{:S(2)}, u32[]{:S(2)}) collective-permute-start(bf16[16,16,256]{2,1,0:T(8,128)(2,1)S(1)} %blend.1.grid), channel_id=1, source_target_pairs={{0,24},{8,0},{16,8},{24,16},{1,25},{9,1},{17,9},{25,17},{2,26},{10... | collective-permute-start | bytes 393224 | tf_op jit(solution)/shard_map/ppermute | solution.py:534

commit v6 on v5

--- a/solution.py
+++ b/solution.py
@@ -13,6 +13,8 @@
 COUPLING = 0.25
 LANES = 128
 ROWS = 8
+SPARE = 24
+PACKED = 29
 HBM = pl.BlockSpec(memory_space=pltpu.HBM)
 SMEM = pl.BlockSpec(memory_space=pltpu.SMEM)
 VMEM = pl.BlockSpec(memory_space=pltpu.VMEM)
@@ -62,6 +64,54 @@
         outgoing = [[0], [2, 3], [4], [5], [6], [7], [1]]
         return outgoing, [(0, 0), (1, 2), (2, 4), (3, 5), (4, 6), (5, 7), (6, 1), (7, 3)]
     return [[d] for d in range(devices)], [(d, d) for d in range(devices)]
+
+
+def is_packed(capacity, devices, distance):
+    return devices == 8 and capacity == 16 and distance > 0
+
+
+def spare_pieces():
+    kept = LANES - SPARE
+    pieces = [(4 * i + c, kept, 13 + i, SPARE * c, SPARE) for i in range(3) for c in range(4)]
+    return pieces + [(12, kept + 8 * i, 13 + i, 4 * SPARE, 8) for i in range(3)]
+
+
+def moved(value, start, goal):
+    shift = (goal - start) % LANES
+    return pltpu.roll(value, shift, 1) if shift else value
+
+
+def lane_window(start, count):
+    lane = lax.broadcasted_iota(jnp.int32, (BAND, LANES), 1)
+    return (lane >= start) & (lane < start + count)
+
+
+def pack_block(there, start, firsts, seconds):
+    for k in range(16):
+        there[start + k] = firsts(k)
+    values = [seconds(k).astype(jnp.float32) for k in range(16)]
+    for slot, lane, donor, goal, count in spare_pieces():
+        values[slot] = jnp.where(
+            lane_window(lane, count), moved(values[donor], goal, lane), values[slot]
+        )
+    for k in range(13):
+        there[start + 16 + k] = values[k].astype(jnp.bfloat16)
+
+
+def unpack_block(block):
+    firsts = [block[k].astype(jnp.float32) for k in range(16)]
+    seconds = [block[16 + k].astype(jnp.float32) for k in range(13)]
+    seconds += [jnp.zeros((BAND, LANES), jnp.float32)] * 3
+    for slot, lane, donor, start, count in spare_pieces():
+        seconds[donor] = jnp.where(
+            lane_window(start, count), moved(seconds[slot], lane, start), seconds[donor]
+        )
+    kept = lane_window(0, LANES - SPARE)
+    seconds = [
+        jnp.where(kept, second, moved(first, 0, LANES - SPARE))
+        for first, second in zip(firsts, seconds)
+    ]
+    return list(zip(firsts, seconds))
 
 
 def render_kernel(
@@ -74,7 +124,7 @@
         outgoing_and_scratch[len(plan) :]
     )
     me = lax.axis_index("tile")
-    first = me * tiles
+    first_tile = me * tiles
     ratio = frame / source
     fetched = [
         pltpu.make_async_copy(patches_in.at[j], patches.at[j], patch_sems.at[j])
@@ -95,7 +145,7 @@
     for copy in small:
         copy.wait()
     for j in range(tiles):
-        tile = first + j
+        tile = first_tile + j
         row_points = points_of(spots_along((frame, LANES), 0), zoom, frac, offset, 0, tile, ratio)
         row_weights = jnp.concatenate(
             [
@@ -105,6 +155,12 @@
             axis=1,
         )
         col_points = points_of(spots_along((ROWS, frame), 1), zoom, frac, offset, 1, tile, ratio)
+        over = moved(col_points[:, frame - LANES :], LANES - SPARE, 0)
+        lane = lax.broadcasted_iota(jnp.int32, over.shape, 1)
+        folded = (lane < SPARE) & (cover_of(over, source) > 0.0)
+        col_points = jnp.concatenate(
+            [jnp.where(folded, over, col_points[:, :LANES]), col_points[:, LANES:]], axis=1
+        )
         col_points = jnp.broadcast_to(col_points[:1], (source, frame))
         col_weights = hat_weight(col_points - spots_along((source, frame), 0)).astype(jnp.bfloat16)
         fetched[j].wait()
@@ -134,6 +190,15 @@
     for there, group in zip(outgoing, plan):
         for position, distance in enumerate(group):
             target = me ^ distance
+            if is_packed(capacity, devices, distance):
+                taken = [rows[target * capacity + slot] for slot in range(capacity)]
+                pack_block(
+                    there,
+                    PACKED * position,
+                    lambda k: frames[taken[k], :, :LANES],
+                    lambda k: frames[taken[k], :, LANES:],
+                )
+                continue
             for slot in range(capacity):
                 there[position * capacity + slot] = frames[rows[target * capacity + slot]]
 
@@ -193,6 +258,7 @@
             points = points_of(spots_along((1, frame), 1), zoom, frac, offset, 1, tile, ratio)
             col_cover[pl.ds(tile, 1), :] = cover_of(points, source)
 
+    col_cover[all_tiles:] = jnp.zeros((ROWS, frame), jnp.float32)
     cover_sum[...] = jnp.zeros_like(cover_sum)
     unroll = math.gcd(slots, ROWS)
 
@@ -254,14 +320,37 @@
     base[...] = total
 
 
-def blend_kernel(sizes, slot_bands, cover_sum, *blocks_and_rest):
+def add_blocks(sizes, chosen, slot_bands, col_cover, blocks, whole, total):
     tiles, bands, frame, source, capacity, devices = sizes
-    *blocks, grid, total = blocks_and_rest
+    whole = iter(whole)
+    for (block, distance), values in zip(chosen, blocks):
+        packed = is_packed(capacity, devices, distance)
+        if packed:
+            unpacked, levels = next(whole), unpack_block(values)
+        for k in range(capacity):
+            slot = block * capacity + k
+            columns = col_cover[pl.ds(slot_bands[1, slot], 1), :]
+            for half in range(frame // LANES):
+                part = slice(half * LANES, (half + 1) * LANES)
+                level = levels[k][half] if packed else values[k, :, part].astype(jnp.float32)
+                if packed or half == 0:
+                    level = jnp.where(columns[:, part] > 0.0, level, 0.0)
+                total[slot_bands[0, slot], :, part] += level
+                if packed:
+                    unpacked[k, :, part] = level.astype(jnp.bfloat16)
+
+
+def first_blend_kernel(sizes, chosen, slot_bands, col_cover, *refs):
+    blocks, (total, *whole) = refs[: len(chosen)], refs[len(chosen) :]
     total[...] = jnp.zeros_like(total)
-    for block, (array, _) in enumerate(exchange_plan(devices)[1]):
-        for k in range(capacity):
-            level = blocks[array][k].astype(jnp.float32)
-            total[slot_bands[0, block * capacity + k]] += level
+    add_blocks(sizes, chosen, slot_bands, col_cover, blocks, whole, total)
+
+
+def last_blend_kernel(sizes, chosen, slot_bands, col_cover, cover_sum, before, *refs):
+    bands = sizes[1]
+    blocks, (grid, *whole, total) = refs[: len(chosen)], refs[len(chosen) :]
+    total[...] = before[...]
+    add_blocks(sizes, chosen, slot_bands, col_cover, blocks, whole, total)
     grid[...] = (total[:bands] / (1.0 + cover_sum[:bands])).astype(jnp.bfloat16)
 
 
@@ -327,7 +416,7 @@
 
     values = [jnp.zeros((all_tiles, 1), jnp.float32)] * 6
     for half in halves:
-        columns = col_cover[:, half * LANES : (half + 1) * LANES]
+        columns = col_cover[:all_tiles, half * LANES : (half + 1) * LANES]
         x = coords(spots_along((all_tiles, LANES), 1, half * LANES), frame)
         for kind, wanted in enumerate(GRADIENT_ROWS):
             index = half * len(GRADIENT_ROWS) + kind
@@ -449,7 +538,12 @@
     rows = tiles * bands
     plan, arriving = exchange_plan(devices)
     blocks = [
-        jax.ShapeDtypeStruct((len(group) * capacity, BAND, frame), jnp.bfloat16)
+        jax.ShapeDtypeStruct(
+            (len(group) * PACKED, BAND, LANES)
+            if is_packed(capacity, devices, group[0])
+            else (len(group) * capacity, BAND, frame),
+            jnp.bfloat16,
+        )
         for group in plan
     ]
     frames, *outgoing = pl.pallas_call(
@@ -501,7 +595,7 @@
         out_specs=[VMEM] * 3 + [SMEM],
         out_shape=[
             jax.ShapeDtypeStruct((bands + 1, BAND, frame), jnp.float32),
-            jax.ShapeDtypeStruct((all_tiles, frame), jnp.float32),
+            jax.ShapeDtypeStruct((all_tiles + ROWS, frame), jnp.float32),
             jax.ShapeDtypeStruct((3, slots, LANES), jnp.float32),
             pltpu.SMEM((3, slots), jnp.int32),
         ],
@@ -516,20 +610,49 @@
     for block, group in zip(outgoing[1:], plan[1:]):
         incoming.append(swapped(block, group[0]))
         if len(group) == 2:
-            passed_on = incoming[-1][capacity:]
+            passed_on = incoming[-1][incoming[-1].shape[0] // 2 :]
     if devices == 8:
         incoming.append(swapped(passed_on, 1))
 
-    grid = pl.pallas_call(
-        functools.partial(blend_kernel, sizes),
-        name="blend",
-        in_specs=[SMEM] + [VMEM] * (1 + len(incoming)),
-        out_specs=VMEM,
-        out_shape=jax.ShapeDtypeStruct((bands, BAND, frame), jnp.bfloat16),
-        scratch_shapes=[pltpu.VMEM((bands + 1, BAND, frame), jnp.float32)],
-        compiler_params=params(24),
-        cost_estimate=cost(1_000_000, 2 << 20),
-    )(pltpu.with_memory_space_constraint(slot_bands, pltpu.SMEM), cover_sum, *incoming)
+    slot_bands = pltpu.with_memory_space_constraint(slot_bands, pltpu.SMEM)
+    total = jax.ShapeDtypeStruct((bands + 1, BAND, frame), jnp.float32)
+
+    def blend(kernel, name, chosen, results, scratch, *operands):
+        distances = [(block, arriving[block][1]) for block in chosen]
+        arrays = [arriving[block][0] for block in chosen]
+        packed = [
+            array
+            for array, (_, distance) in zip(arrays, distances)
+            if is_packed(capacity, devices, distance)
+        ]
+        whole = jax.ShapeDtypeStruct((capacity, BAND, frame), jnp.bfloat16)
+        result, *unpacked = pl.pallas_call(
+            functools.partial(kernel, sizes, distances),
+            name=name,
+            in_specs=[SMEM] + [VMEM] * (len(operands) + len(chosen)),
+            out_specs=[VMEM] * (1 + len(packed)),
+            out_shape=[results] + [whole] * len(packed),
+            scratch_shapes=scratch,
+            compiler_params=params(24),
+            cost_estimate=cost(1_000_000, 2 << 20),
+        )(slot_bands, *operands, *(incoming[array] for array in arrays))
+        for array, block in zip(packed, unpacked):
+            incoming[array] = block
+        return result
+
+    last = (4, 5) if devices == 8 else range(devices - devices // 4, devices)
+    early = [block for block in range(devices) if block not in last]
+    before = blend(first_blend_kernel, "first_blend", early, total, [], col_cover)
+    grid = blend(
+        last_blend_kernel,
+        "last_blend",
+        last,
+        jax.ShapeDtypeStruct((bands, BAND, frame), jnp.bfloat16),
+        [pltpu.VMEM(total.shape, total.dtype)],
+        col_cover,
+        cover_sum,
+        before,
+    )
 
     from_next = lax.ppermute(grid, "sec", [(i, (i - 1) % sections) for i in range(sections)])
 
@@ -550,7 +673,7 @@
         compiler_params=params(24),
         cost_estimate=cost(8_000_000, 2 << 20),
     )(
-        pltpu.with_memory_space_constraint(slot_bands, pltpu.SMEM),
+        slot_bands,
         from_next,
         top_grid.reshape(bands, BAND, frame),
         col_cover,

time: 53.6 us -> 52 us (0.970)
  blocking collectives: 17.3 us -> 13.9 us
  waiting for transfers between devices: 8.02 us -> 9.42 us
    all_to_all x1, blocking collectives: 17.3 us -> 13.9 us  [shards(): lax.all_to_all(payload, ('sec', 'tile'), split_axis=0, concat_axis=0, til...]
    ppermute x1, waiting for transfers between devices: 0.64 us -> 1.98 us  [shards(): lax.ppermute(grid, 'sec', [(i, (i - 1) % sections) for i in range(section...]
    pallas_call x1 -> x2, Pallas kernels: 0.81 us -> 1.39 us  [blend(): pl.pallas_call(functools.partial(kernel, sizes, distances), name=name, in...]
  transfers between devices with their start and end apart: 8 -> 8, of which waited for: 3 -> 2; matrix products, arithmetic and copies ran while one was open for 0% -> 0% of each run, Pallas kernels for 15% -> 17%
where the time goes in v6:
time: 52 us; the launch traced here: 51.8 us
  Pallas kernels  15.2 us (29%)
  blocking collectives  13.9 us (27%)
  starting transfers between devices  12.5 us (24%)
  waiting for transfers between devices  9.42 us (18%)
  between operations  0.79 us (2%)
    all_to_all x1, blocking collectives, shards(): lax.all_to_all(payload, ('sec', 'tile'), split_axis=0, concat_axis=0, til...  13.9 us
    ppermute x7, starting transfers between devices, swapped(): lax.ppermute(block, 'tile', [(i, i ^ distance) for i in range(devices)])  9.86 us
    ppermute x7, waiting for transfers between devices, swapped(): lax.ppermute(block, 'tile', [(i, i ^ distance) for i in range(devices)])  7.45 us
    pallas_call x1, Pallas kernels, shards(): pl.pallas_call(functools.partial(render_kernel, sizes), name='render', in...  3.46 us
    pallas_call x1, Pallas kernels, shards(): pl.pallas_call(functools.partial(slot_kernel, sizes), name='slots', in_sp...  2.96 us
    pallas_call x1, Pallas kernels, shards(): pl.pallas_call(functools.partial(scan_kernel, sizes), name='scan', in_spe...  2.8 us
    ppermute x1, starting transfers between devices, shards(): lax.ppermute(grid, 'sec', [(i, (i - 1) % sections) for i in range(section...  2.64 us
    ppermute x1, waiting for transfers between devices, shards(): lax.ppermute(grid, 'sec', [(i, (i - 1) % sections) for i in range(section...  1.98 us
  transfers between devices with their start and end apart: 8, of which 2 were waited for; matrix products, arithmetic and copies ran while one was open for 0% of the time, Pallas kernels for 17%

profile of v6, /device:TPU:0, one launch (start us, length us, event | category | flops | bytes accessed | tf_op | source)
XLA Modules:
  0.0 51.8 jit_solution(1469415593665317210)
XLA Ops:
  0.6 0.0 copy-start.4
  0.6 0.0 copy-start.3
  0.7 0.0 copy-start.2
  0.7 0.0 copy-start.1
  0.7 0.0 copy-start
  0.7 3.5 %render.1 = (bf16[64,16,256]{2,1,0:T(8,128)(2,1)S(1)}, bf16[16,16,256]{2,1,0:T(8,128)(2,1)S(1)}, bf16[58,16,128]{2,1,0:T(8,128)(2,1)S(1)}, bf16[29,16,128]{2,1,0...) custom-call(f32[2,32]{1,0:T(2,128)} %bitcast.15, ...), custom_call_target="tpu_custom_call" | custom-call | flops 800000000 | bytes 4194304 | tf_op jit(solution)/shard_map/render/pallas_call | solution.py:549
  4.1 3.1 %collective-permute-start = (bf16[58,16,128]{2,1,0:T(8,128)(2,1)S(1)}, bf16[58,16,128]{2,1,0:T(8,128)(2,1)S(1)}, u32[]{:S(2)}, u32[]{:S(2)}) collective-permute-start(bf16[58,16,128]{2,1,0:T(8,128)(2,1)S(1)} %get-tuple-element.29), channel_id=1, source_target_pairs={{0,2},{1,3},{2,0},{3,1},{4,6},{5,7},{6,4},{7,5},{8,10},{9,11},{10,... | collective-permute-start | bytes 712712 | tf_op jit(solution)/shard_map/ppermute | solution.py:607
  7.2 2.6 %collective-permute-start.1 = (bf16[29,16,128]{2,1,0:T(8,128)(2,1)S(1)}, bf16[29,16,128]{2,1,0:T(8,128)(2,1)S(1)}, u32[]{:S(2)}, u32[]{:S(2)}) collective-permute-start(bf16[29,16,128]{2,1,0:T(8,128)(2,1)S(1)} %get-tuple-element.30), channel_id=1, source_target_pairs={{0,4},{1,5},{2,6},{3,7},{4,0},{5,1},{6,2},{7,3},{8,12},{9,13},{10,... | collective-permute-start | bytes 356360 | tf_op jit(solution)/shard_map/ppermute | solution.py:607
  9.8 0.0 collective-permute-start.2
  9.8 0.4 collective-permute-start.3
  10.3 7.4 %collective-permute-done.refs_1_ = bf16[58,16,128]{2,1,0:T(8,128)(2,1)S(1)} collective-permute-done((bf16[58,16,128]{2,1,0:T(8,128)(2,1)S(1)}, bf16[58,16,128]{2,1,0:T(8,128)(2,1)S(1)}, u32[]{:S(2)}, u32[]{:S(2)}) %collective-permute-start) | collective-permute-done | bytes 237600 | tf_op jit(solution)/shard_map/ppermute | solution.py:607
  17.7 0.1 collective-permute-start.4
  17.8 3.0 %collective-permute-start.5 = (bf16[29,16,128]{2,1,0:T(8,128)(2,1)S(1)}, bf16[29,16,128]{2,1,0:T(8,128)(2,1)S(1)}, u32[]{:S(2)}, u32[]{:S(2)}) collective-permute-start(bf16[29,16,128]{2,1,0:T(8,128)(2,1)S(1)} %get-tuple-element.34), channel_id=1, source_target_pairs={{0,6},{1,7},{2,4},{3,5},{4,2},{5,3},{6,0},{7,1},{8,14},{9,15},{10,... | collective-permute-start | bytes 356360 | tf_op jit(solution)/shard_map/ppermute | solution.py:607
  20.8 0.0 collective-permute-done.1.refs_2_
  20.8 0.7 %collective-permute-start.6 = (bf16[29,16,128]{2,1,0:T(8,128)(2,1)S(1)}, bf16[29,16,128]{2,1,0:T(8,128)(2,1)S(1)}, u32[]{:S(2)}, u32[]{:S(2)}) collective-permute-start(bf16[29,16,128]{2,1,0:T(8,128)(2,1)S(1)} %get-tuple-element.35), channel_id=1, source_target_pairs={{0,7},{1,6},{2,5},{3,4},{4,3},{5,2},{6,1},{7,0},{8,15},{9,14},{10,... | collective-permute-start | bytes 356360 | tf_op jit(solution)/shard_map/ppermute | solution.py:607
  21.5 0.0 copy-done.4
  21.5 2.8 %scan.1.codes = s32[129]{0:T(256)S(1)} custom-call(s32[16,1,32]{2,1,0:T(1,128)S(1)} %bitcast.25), custom_call_target="tpu_custom_call" | custom-call | flops 20000000 | bytes 1048576 | tf_op jit(solution)/shard_map/scan/pallas_call | solution.py:581
  24.3 0.0 copy-done.3
  24.3 0.0 copy-done.2
  24.3 0.0 copy-done.1
  24.3 3.0 %slots.1 = (f32[17,16,256]{2,1,0:T(8,128)S(1)}, f32[40,256]{1,0:T(8,128)S(1)}, f32[3,128,128]{2,1,0:T(8,128)S(1)}, s32[3,128]{1,0:T(4,128)S(4)}) custom-call(f32[2,32]{1,0:T(2,128)S(1)} %bitcast.16, f32[2,32]{1,0:T(2,128)S(1)} %bitcast.19, s32[2,32]{1,0:T(2,128)S(1)} %bitcast.22, s32[129]{0:T(256)S(1)} %scan.1.codes), custom_call_target="tpu_custom_call" | custom-call | flops 20000000 | bytes 1048576 | tf_op jit(solution)/shard_map/slots/pallas_call | solution.py:591
  27.3 0.0 collective-permute-done.2.refs_3_
  27.3 0.0 collective-permute-done.3.refs_4_
  27.3 0.0 collective-permute-done.4.refs_5_
  27.3 1.0 %first_blend.1 = (f32[17,16,256]{2,1,0:T(8,128)S(1)}, bf16[16,16,256]{2,1,0:T(8,128)(2,1)S(1)}, bf16[16,16,256]{2,1,0:T(8,128)(2,1)S(1)}, bf16[16,16,256]{2,1,0:...) custom-call(s32[3,128]{1,0:T(4,128)S(4)} %get-tuple-element.25.slot_bands, ...), custom_call_target="tpu_custom_call" | custom-call | flops 1000000 | bytes 2097152 | tf_op jit(solution)/shard_map/first_blend/pallas_call | solution.py:629
  28.3 0.0 collective-permute-done.5.refs_0_
  28.3 0.0 collective-permute-done.6.refs_1_
  28.3 0.4 last_blend.1
  28.7 2.6 %collective-permute-start.7 = (bf16[16,16,256]{2,1,0:T(8,128)(2,1)S(1)}, bf16[16,16,256]{2,1,0:T(8,128)(2,1)S(1)}, u32[]{:S(2)}, u32[]{:S(2)}) collective-permute-start(bf16[16,16,256]{2,1,0:T(8,128)(2,1)S(1)} %get-tuple-element.36.grid), channel_id=1, source_target_pairs={{0,24},{8,0},{16,8},{24,16},{1,25},{9,1},{17,9},{25,17},{2,26},{10... | collective-permute-start | bytes 393224 | tf_op jit(solution)/shard_map/ppermute | solution.py:657
  31.4 1.9 %moments.1.base = f32[8,128]{1,0:T(8,128)S(1)} custom-call(f32[2,32]{1,0:T(2,128)S(1)} %bitcast.17, f32[2,32]{1,0:T(2,128)S(1)} %bitcast.20, s32[2,32]{1,0:T(2,128)S(1)} %bitcast.23, bf16[64,16,256]{2,1,0:T(8,128)(2,1)S(1)} %get-tuple-element.38.frames), custom_call_target="tpu_custom_call" | custom-call | flops 20000000 | bytes 1048576 | tf_op jit(solution)/shard_map/moments/pallas_call | solution.py:570
  33.2 2.0 %collective-permute-done.7.from_next = bf16[16,16,256]{2,1,0:T(8,128)(2,1)S(1)} collective-permute-done((bf16[16,16,256]{2,1,0:T(8,128)(2,1)S(1)}, bf16[16,16,256]{2,1,0:T(8,128)(2,1)S(1)}, u32[]{:S(2)}, u32[]{:S(2)}) %collective-permute-start.7) | collective-permute-done | bytes 131104 | tf_op jit(solution)/shard_map/ppermute | solution.py:657
  35.2 0.0 copy-done
  35.2 1.5 %gradient.1 = (f32[32,8,128]{2,1,0:T(8,128)S(1)}, bf16[16,16,256]{2,1,0:T(8,128)(2,1)}) custom-call(s32[3,128]{1,0:T(4,128)S(4)} %get-tuple-element.25.slot_bands, bf16[16,16,256]{2,1,0:T(8,128)(2,1)S(1)} %collective-permute-done.7.from_next, bf16[16,16,256]{2,1,0:T(8,128)(2,1)S(1)} %bitcast.14, f32[40,256]{1,0:T(8,128)S(1)} %get-tuple-element.26.col_cover, ...), custom_call_target="tpu_custom_call" | custom-call | flops 8000000 | bytes 2097152 | tf_op jit(solution)/shard_map/gradient/pallas_call | solution.py:659
  36.7 13.9 %all_to_all.5.received = f32[32,8,128]{2,1,0:T(8,128)S(1)} all-to-all(f32[32,8,128]{2,1,0:T(8,128)S(1)} %get-tuple-element.47), channel_id=1, replica_groups=mesh['sec'=4,'tile'=8] {'sec','tile'}, dimensions={0} | all-to-all | bytes 262144 | tf_op jit(solution)/shard_map/all_to_all | solution.py:686
  50.6 1.2 %solve.1 = f32[4,6]{1,0:T(4,128)} custom-call(f32[32,8,128]{2,1,0:T(8,128)S(1)} %all_to_all.5.received), custom_call_target="tpu_custom_call" | custom-call | flops 100000 | bytes 262144 | tf_op jit(solution)/shard_map/solve/pallas_call | solution.py:690
  (1 shorter events, 0.0 us)
Async XLA Ops:
  0.6 20.8 %copy-start.4 = (s32[1,32,16,1]{1,3,2,0:T(1,128)S(1)}, s32[1,32,16,1]{1,3,2,0:T(1,128)}, u32[]{:S(2)}) copy-start(s32[1,32,16,1]{1,3,2,0:T(1,128)} %param.10) | copy-start | bytes 6148
  0.6 23.6 %copy-start.3 = (s32[1,2,32]{2,1,0:T(2,128)S(1)}, s32[1,2,32]{2,1,0:T(2,128)}, u32[]{:S(2)}) copy-start(s32[1,2,32]{2,1,0:T(2,128)} %param.9) | copy-start | bytes 772
  0.7 23.6 %copy-start.2 = (f32[1,2,32]{2,1,0:T(2,128)S(1)}, f32[1,2,32]{2,1,0:T(2,128)}, u32[]{:S(2)}) copy-start(f32[1,2,32]{2,1,0:T(2,128)} %param.8) | copy-start | bytes 772
  0.7 23.6 %copy-start.1 = (f32[1,2,32]{2,1,0:T(2,128)S(1)}, f32[1,2,32]{2,1,0:T(2,128)}, u32[]{:S(2)}) copy-start(f32[1,2,32]{2,1,0:T(2,128)} %param.7) | copy-start | bytes 772
  0.7 34.6 %copy-start = (bf16[1,256,256]{2,1,0:T(8,128)(2,1)S(1)}, bf16[1,256,256]{2,1,0:T(8,128)(2,1)}, u32[]{:S(2)}) copy-start(bf16[1,256,256]{2,1,0:T(8,128)(2,1)} %param.11) | copy-start | bytes 393220
  4.1 13.6 %collective-permute-start = (bf16[58,16,128]{2,1,0:T(8,128)(2,1)S(1)}, bf16[58,16,128]{2,1,0:T(8,128)(2,1)S(1)}, u32[]{:S(2)}, u32[]{:S(2)}) collective-permute-start(bf16[58,16,128]{2,1,0:T(8,128)(2,1)S(1)} %get-tuple-element.29), channel_id=1, source_target_pairs={{0,2},{1,3},{2,0},{3,1},{4,6},{5,7},{6,4},{7,5},{8,10},{9,11},{10,... | collective-permute-start | bytes 712712 | tf_op jit(solution)/shard_map/ppermute | solution.py:607
  7.2 13.5 %collective-permute-start.1 = (bf16[29,16,128]{2,1,0:T(8,128)(2,1)S(1)}, bf16[29,16,128]{2,1,0:T(8,128)(2,1)S(1)}, u32[]{:S(2)}, u32[]{:S(2)}) collective-permute-start(bf16[29,16,128]{2,1,0:T(8,128)(2,1)S(1)} %get-tuple-element.30), channel_id=1, source_target_pairs={{0,4},{1,5},{2,6},{3,7},{4,0},{5,1},{6,2},{7,3},{8,12},{9,13},{10,... | collective-permute-start | bytes 356360 | tf_op jit(solution)/shard_map/ppermute | solution.py:607
  9.8 17.5 %collective-permute-start.2 = (bf16[29,16,128]{2,1,0:T(8,128)(2,1)S(1)}, bf16[29,16,128]{2,1,0:T(8,128)(2,1)S(1)}, u32[]{:S(2)}, u32[]{:S(2)}) collective-permute-start(bf16[29,16,128]{2,1,0:T(8,128)(2,1)S(1)} %get-tuple-element.31), channel_id=1, source_target_pairs={{0,5},{1,4},{2,7},{3,6},{4,1},{5,0},{6,3},{7,2},{8,13},{9,12},{10,... | collective-permute-start | bytes 356360 | tf_op jit(solution)/shard_map/ppermute | solution.py:607
  9.8 17.5 %collective-permute-start.3 = (bf16[29,16,128]{2,1,0:T(8,128)(2,1)S(1)}, bf16[29,16,128]{2,1,0:T(8,128)(2,1)S(1)}, u32[]{:S(2)}, u32[]{:S(2)}) collective-permute-start(bf16[29,16,128]{2,1,0:T(8,128)(2,1)S(1)} %get-tuple-element.32), channel_id=1, source_target_pairs={{0,1},{1,0},{2,3},{3,2},{4,5},{5,4},{6,7},{7,6},{8,9},{9,8},{10,11... | collective-permute-start | bytes 356360 | tf_op jit(solution)/shard_map/ppermute | solution.py:607
  17.7 9.6 %collective-permute-start.4 = (bf16[29,16,128]{2,1,0:T(8,128)(2,1)S(1)}, bf16[29,16,128]{2,1,0:T(8,128)(2,1)S(1)}, u32[]{:S(2)}, u32[]{:S(2)}) collective-permute-start(bf16[29,16,128]{2,1,0:T(8,128)(2,1)S(1)} %slice.4), channel_id=1, source_target_pairs={{0,1},{1,0},{2,3},{3,2},{4,5},{5,4},{6,7},{7,6},{8,9},{9,8},{10,11... | collective-permute-start | bytes 356360 | tf_op jit(solution)/shard_map/ppermute | solution.py:607
  17.8 10.5 %collective-permute-start.5 = (bf16[29,16,128]{2,1,0:T(8,128)(2,1)S(1)}, bf16[29,16,128]{2,1,0:T(8,128)(2,1)S(1)}, u32[]{:S(2)}, u32[]{:S(2)}) collective-permute-start(bf16[29,16,128]{2,1,0:T(8,128)(2,1)S(1)} %get-tuple-element.34), channel_id=1, source_target_pairs={{0,6},{1,7},{2,4},{3,5},{4,2},{5,3},{6,0},{7,1},{8,14},{9,15},{10,... | collective-permute-start | bytes 356360 | tf_op jit(solution)/shard_map/ppermute | solution.py:607
  20.8 7.5 %collective-permute-start.6 = (bf16[29,16,128]{2,1,0:T(8,128)(2,1)S(1)}, bf16[29,16,128]{2,1,0:T(8,128)(2,1)S(1)}, u32[]{:S(2)}, u32[]{:S(2)}) collective-permute-start(bf16[29,16,128]{2,1,0:T(8,128)(2,1)S(1)} %get-tuple-element.35), channel_id=1, source_target_pairs={{0,7},{1,6},{2,5},{3,4},{4,3},{5,2},{6,1},{7,0},{8,15},{9,14},{10,... | collective-permute-start | bytes 356360 | tf_op jit(solution)/shard_map/ppermute | solution.py:607
  28.7 6.5 %collective-permute-start.7 = (bf16[16,16,256]{2,1,0:T(8,128)(2,1)S(1)}, bf16[16,16,256]{2,1,0:T(8,128)(2,1)S(1)}, u32[]{:S(2)}, u32[]{:S(2)}) collective-permute-start(bf16[16,16,256]{2,1,0:T(8,128)(2,1)S(1)} %get-tuple-element.36.grid), channel_id=1, source_target_pairs={{0,24},{8,0},{16,8},{24,16},{1,25},{9,1},{17,9},{25,17},{2,26},{10... | collective-permute-start | bytes 393224 | tf_op jit(solution)/shard_map/ppermute | solution.py:657

commit v7 on v6

--- a/solution.py
+++ b/solution.py
@@ -213,7 +213,8 @@
     return rows
 
 
-MOMENT_ROWS = ({0: 0, 1: 1, 3: 2}, {2: 0, 4: 1}, {5: 0})
+MOMENT_ROWS = ((0, 0, {0: 0, 1: 1}), (0, 1, {2: 0}), (1, 0, {0: 2}), (1, 1, {1: 1}), (1, 2, {2: 0}))
+PAYLOAD_ROWS = 4
 
 
 def scan_kernel(sizes, owner, codes):
@@ -291,11 +292,13 @@
                 cover_sum[place, :, part] += cover * columns[:, part]
 
 
+def payload_lanes(tiles, devices):
+    return pl.cdiv(2 * tiles * devices + 6 * tiles, LANES) * LANES
+
+
 def moment_kernel(sizes, zoom, frac, offset, frames, base, parts):
     tiles, bands, frame, source, capacity, devices = sizes
     me = lax.axis_index("tile")
-    sec = lax.axis_index("sec")
-    sections = lax.axis_size("sec")
     all_tiles = tiles * devices
     ratio = frame / source
     parts[...] = jnp.zeros_like(parts)
@@ -309,15 +312,17 @@
         columns = cover_of(columns, source)
         weighted = (cover, cover * y, cover * y * y)
         for power, image in enumerate((None, level, level * level)):
-            block = (sec + 1 + power) % sections
-            place = block * all_tiles + tile
-            for a, rows in enumerate(weighted):
-                total = rows if image is None else rows * image
-                parts[a, pl.ds(place, 1), :] = columns * jnp.sum(total, axis=0, keepdims=True)
-    total = exact_dot(feature_rows(frame, MOMENT_ROWS[0]), parts[0])
-    for a in (1, 2):
-        total += exact_dot(feature_rows(frame, MOMENT_ROWS[a]), parts[a])
-    base[...] = total
+            sums = [
+                columns * jnp.sum(rows if image is None else rows * image, axis=0, keepdims=True)
+                for rows in weighted
+            ]
+            for k, (half, a, _) in enumerate(MOMENT_ROWS):
+                place = 2 * all_tiles + tiles * (2 * power + half) + j
+                parts[k, place : place + 1, :] = sums[a]
+    total = 0.0
+    for k, (_, _, wanted) in enumerate(MOMENT_ROWS):
+        total += exact_dot(feature_rows(frame, wanted), parts[k])
+    base[...] = total[:PAYLOAD_ROWS]
 
 
 def add_blocks(sizes, chosen, slot_bands, col_cover, blocks, whole, total):
@@ -366,7 +371,6 @@
     written.start()
     sec = lax.axis_index("sec")
     all_tiles = tiles * devices
-    lanes = base.shape[1]
 
     @pl.when(sec == lax.axis_size("sec") - 1)
     def _():
@@ -428,12 +432,15 @@
                 term = value * x if power else value
                 values[row] += jnp.sum(term, axis=1, keepdims=True)
     total = []
-    tile = lax.broadcasted_iota(jnp.int32, (all_tiles, LANES), 0) + sec * all_tiles
-    for first in range(0, lanes, LANES):
-        lane = lax.broadcasted_iota(jnp.int32, (all_tiles, LANES), 1) + first
-        places = (tile == lane).astype(jnp.float32)
-        rows = [jnp.sum(places * value, axis=0, keepdims=True) for value in values]
-        total.append(jnp.concatenate(rows + [jnp.zeros_like(rows[0])] * (ROWS - 6), axis=0))
+    tile = lax.broadcasted_iota(jnp.int32, (all_tiles, LANES), 0)
+    for start in range(0, base.shape[1], LANES):
+        lane = lax.broadcasted_iota(jnp.int32, (all_tiles, LANES), 1) + start
+        placed = [
+            sum(jnp.where(lane == tile + k * all_tiles, values[3 * k + r], 0.0) for k in range(2))
+            for r in range(3)
+        ]
+        rows = [jnp.sum(value, axis=0, keepdims=True) for value in placed]
+        total.append(jnp.concatenate(rows + [jnp.zeros_like(rows[0])], axis=0))
     total = base[...] + jnp.concatenate(total, axis=1)
     payload[...] = jnp.broadcast_to(total[None], payload.shape)
     written.wait()
@@ -449,22 +456,48 @@
     within = lane % all_tiles
     area = frame * frame
 
-    gradients = jnp.zeros((ROWS, lanes), jnp.float32)
-    moments = [jnp.zeros((ROWS, lanes), jnp.float32) for _ in range(3)]
+    width = max(lanes, received.shape[2])
+
+    def rolled(value, shift):
+        return pltpu.roll(value, shift % width, 1)
+
+    def fetched(source):
+        value = received[source]
+        if value.shape[1] < width:
+            value = jnp.pad(value, ((0, 0), (0, width - value.shape[1])))
+        return jnp.concatenate([value, rolled(value, width - tiles)], axis=0)
+
+    wide = lax.broadcasted_iota(jnp.int32, (ROWS, width), 1)
+    gradients = [jnp.zeros((ROWS, width), jnp.float32)] * 2
+    moments = [jnp.zeros((ROWS, width), jnp.float32)] * 3
     for s in range(sections):
-        own = received[s * devices]
-        for t in range(1, devices):
-            own += received[s * devices + t]
-        here = lane // all_tiles == s
-        gradients = jnp.where(here, own, gradients)
-        for power in range(3):
-            shift = ((sections - 1 - power) * all_tiles) % lanes
-            moved = pltpu.roll(own, shift, 1) if shift else own
-            moments[power] = jnp.where(here, moved, moments[power])
-    gradients = gradients * (1.0 / area)
-    moments = [m * (1.0 / area) for m in moments]
-
-    where = ((0, 1, 2), (1, 3, 4), (2, 4, 5))
+
+        def gather(t, carry):
+            own, *moments = carry
+            value = fetched(s * devices + t)
+            place = s * all_tiles + t * tiles
+            here = (wide >= place) & (wide < place + tiles)
+            for power in range(3):
+                start = 2 * all_tiles + 2 * power * tiles
+                moment = rolled(value, place - start + 2 * width)
+                moments[power] = jnp.where(here, moment, moments[power])
+            return (own + value, *moments)
+
+        carry = (jnp.zeros((ROWS, width), jnp.float32), *moments)
+        if devices <= 8:
+            for t in range(devices):
+                carry = gather(t, carry)
+        else:
+            carry = lax.fori_loop(0, devices, gather, carry)
+        own, *moments = carry
+        here = wide // all_tiles == s
+        for k in range(2):
+            part = rolled(own, (s - k) * all_tiles)
+            gradients[k] = jnp.where(here, part, gradients[k])
+    gradients = [value[:, :lanes] * (1.0 / area) for value in gradients]
+    moments = [value[:, :lanes] * (1.0 / area) for value in moments]
+
+    where = ((0, 1, 2), (1, 4, 5), (2, 5, 6))
     row = lax.broadcasted_iota(jnp.int32, (ROWS, lanes), 0)
 
     def entry(f, g):
@@ -480,6 +513,7 @@
 
     normal = [stacked([entry(f, g) for f in range(6)]) for g in range(6)]
     diagonal = stacked([entry(f, f) for f in range(6)])
+    gradients = stacked([gradients[f // 3][f % 3 : f % 3 + 1] for f in range(6)])
     precond = 1.0 / (diagonal + 4.0 * COUPLING)
 
     def total(values):
@@ -530,7 +564,7 @@
     capacity = max(2, 2 * tiles * bands // devices)
     slots = devices * capacity
     all_tiles = tiles * devices
-    lanes = sections * all_tiles
+    width = payload_lanes(tiles, devices)
     sizes = (tiles, bands, frame, source, capacity, devices)
     place = (zoom[0], frac[0], offset[0])
     routes = jnp.transpose(owner, (0, 2, 3, 1))[0]
@@ -572,8 +606,8 @@
         name="moments",
         in_specs=[SMEM] * 3 + [VMEM],
         out_specs=VMEM,
-        out_shape=jax.ShapeDtypeStruct((ROWS, lanes), jnp.float32),
-        scratch_shapes=[pltpu.VMEM((3, lanes, frame), jnp.float32)],
+        out_shape=jax.ShapeDtypeStruct((PAYLOAD_ROWS, width), jnp.float32),
+        scratch_shapes=[pltpu.VMEM((len(MOMENT_ROWS), width, frame), jnp.float32)],
         compiler_params=params(24),
         cost_estimate=cost(20_000_000, 1 << 20),
     )(*place, frames)
@@ -640,7 +674,7 @@
             incoming[array] = block
         return result
 
-    last = (4, 5) if devices == 8 else range(devices - devices // 4, devices)
+    last = [5] if devices == 8 else range(devices - devices // 4, devices)
     early = [block for block in range(devices) if block not in last]
     before = blend(first_blend_kernel, "first_blend", early, total, [], col_cover)
     grid = blend(
@@ -662,7 +696,7 @@
         in_specs=[SMEM] + [VMEM] * (6 + len(incoming)),
         out_specs=[VMEM, HBM],
         out_shape=[
-            jax.ShapeDtypeStruct((sections * devices, ROWS, lanes), jnp.float32),
+            jax.ShapeDtypeStruct((sections * devices, PAYLOAD_ROWS, width), jnp.float32),
             jax.ShapeDtypeStruct((bands, BAND, frame), jnp.bfloat16),
         ],
         scratch_shapes=[

time: 52 us -> 51.1 us (0.983)
  waiting for transfers between devices: 9.42 us -> 5.83 us
  starting transfers between devices: 12.5 us -> 13.9 us
  Pallas kernels: 15.2 us -> 15.9 us
  blocking collectives: 13.9 us -> 14.5 us
    ppermute x7, waiting for transfers between devices: 7.45 us -> 5.2 us  [swapped(): lax.ppermute(block, 'tile', [(i, i ^ distance) for i in range(devices)])]
    ppermute x7, starting transfers between devices: 9.86 us -> 11.4 us  [swapped(): lax.ppermute(block, 'tile', [(i, i ^ distance) for i in range(devices)])]
    ppermute x1, waiting for transfers between devices: 1.98 us -> 0.62 us  [shards(): lax.ppermute(grid, 'sec', [(i, (i - 1) % sections) for i in range(section...]
    all_to_all x1, blocking collectives: 13.9 us -> 14.5 us  [shards(): lax.all_to_all(payload, ('sec', 'tile'), split_axis=0, concat_axis=0, til...]
    pallas_call x1, Pallas kernels: 2.8 us -> 3.36 us  [shards(): pl.pallas_call(functools.partial(scan_kernel, sizes), name='scan', in_spe...]
  transfers between devices with their start and end apart: 8 -> 8, of which waited for: 2 -> 2; matrix products, arithmetic and copies ran while one was open for 0% -> 0% of each run, Pallas kernels for 17% -> 18%
where the time goes in v7:
time: 51.1 us; the launch traced here: 51 us
  Pallas kernels  15.9 us (31%)
  blocking collectives  14.5 us (28%)
  starting transfers between devices  13.9 us (27%)
  waiting for transfers between devices  5.83 us (11%)
  between operations  0.79 us (2%)
    all_to_all x1, blocking collectives, shards(): lax.all_to_all(payload, ('sec', 'tile'), split_axis=0, concat_axis=0, til...  14.5 us
    ppermute x7, starting transfers between devices, swapped(): lax.ppermute(block, 'tile', [(i, i ^ distance) for i in range(devices)])  11.4 us
    ppermute x7, waiting for transfers between devices, swapped(): lax.ppermute(block, 'tile', [(i, i ^ distance) for i in range(devices)])  5.2 us
    pallas_call x1, Pallas kernels, shards(): pl.pallas_call(functools.partial(render_kernel, sizes), name='render', in...  3.46 us
    pallas_call x1, Pallas kernels, shards(): pl.pallas_call(functools.partial(scan_kernel, sizes), name='scan', in_spe...  3.36 us
    pallas_call x1, Pallas kernels, shards(): pl.pallas_call(functools.partial(slot_kernel, sizes), name='slots', in_sp...  2.96 us
    ppermute x1, starting transfers between devices, shards(): lax.ppermute(grid, 'sec', [(i, (i - 1) % sections) for i in range(section...  2.51 us
    pallas_call x1, Pallas kernels, shards(): pl.pallas_call(functools.partial(moment_kernel, sizes), name='moments', i...  1.9 us
  transfers between devices with their start and end apart: 8, of which 2 were waited for; matrix products, arithmetic and copies ran while one was open for 0% of the time, Pallas kernels for 18%

profile of v7, /device:TPU:0, one launch (start us, length us, event | category | flops | bytes accessed | tf_op | source)
XLA Modules:
  0.0 51.0 jit_solution(14939324678164406112)
XLA Ops:
  0.6 0.0 copy-start.4
  0.6 0.0 copy-start.3
  0.7 0.0 copy-start.2
  0.7 0.0 copy-start.1
  0.7 0.0 copy-start
  0.7 3.5 %render.1 = (bf16[64,16,256]{2,1,0:T(8,128)(2,1)S(1)}, bf16[16,16,256]{2,1,0:T(8,128)(2,1)S(1)}, bf16[58,16,128]{2,1,0:T(8,128)(2,1)S(1)}, bf16[29,16,128]{2,1,0...) custom-call(f32[2,32]{1,0:T(2,128)} %bitcast.15, ...), custom_call_target="tpu_custom_call" | custom-call | flops 800000000 | bytes 4194304 | tf_op jit(solution)/shard_map/render/pallas_call | solution.py:583
  4.1 3.1 %collective-permute-start = (bf16[58,16,128]{2,1,0:T(8,128)(2,1)S(1)}, bf16[58,16,128]{2,1,0:T(8,128)(2,1)S(1)}, u32[]{:S(2)}, u32[]{:S(2)}) collective-permute-start(bf16[58,16,128]{2,1,0:T(8,128)(2,1)S(1)} %get-tuple-element.29), channel_id=1, source_target_pairs={{0,2},{1,3},{2,0},{3,1},{4,6},{5,7},{6,4},{7,5},{8,10},{9,11},{10,... | collective-permute-start | bytes 712712 | tf_op jit(solution)/shard_map/ppermute | solution.py:641
  7.2 2.6 %collective-permute-start.1 = (bf16[29,16,128]{2,1,0:T(8,128)(2,1)S(1)}, bf16[29,16,128]{2,1,0:T(8,128)(2,1)S(1)}, u32[]{:S(2)}, u32[]{:S(2)}) collective-permute-start(bf16[29,16,128]{2,1,0:T(8,128)(2,1)S(1)} %get-tuple-element.30), channel_id=1, source_target_pairs={{0,4},{1,5},{2,6},{3,7},{4,0},{5,1},{6,2},{7,3},{8,12},{9,13},{10,... | collective-permute-start | bytes 356360 | tf_op jit(solution)/shard_map/ppermute | solution.py:641
  9.8 0.0 collective-permute-start.2
  9.8 1.7 %collective-permute-start.3 = (bf16[29,16,128]{2,1,0:T(8,128)(2,1)S(1)}, bf16[29,16,128]{2,1,0:T(8,128)(2,1)S(1)}, u32[]{:S(2)}, u32[]{:S(2)}) collective-permute-start(bf16[29,16,128]{2,1,0:T(8,128)(2,1)S(1)} %get-tuple-element.32), channel_id=1, source_target_pairs={{0,6},{1,7},{2,4},{3,5},{4,2},{5,3},{6,0},{7,1},{8,14},{9,15},{10,... | collective-permute-start | bytes 356360 | tf_op jit(solution)/shard_map/ppermute | solution.py:641
  11.5 1.0 %collective-permute-start.4 = (bf16[29,16,128]{2,1,0:T(8,128)(2,1)S(1)}, bf16[29,16,128]{2,1,0:T(8,128)(2,1)S(1)}, u32[]{:S(2)}, u32[]{:S(2)}) collective-permute-start(bf16[29,16,128]{2,1,0:T(8,128)(2,1)S(1)} %get-tuple-element.33), channel_id=1, source_target_pairs={{0,1},{1,0},{2,3},{3,2},{4,5},{5,4},{6,7},{7,6},{8,9},{9,8},{10,11... | collective-permute-start | bytes 356360 | tf_op jit(solution)/shard_map/ppermute | solution.py:641
  12.5 5.2 %collective-permute-done.refs_1_ = bf16[58,16,128]{2,1,0:T(8,128)(2,1)S(1)} collective-permute-done((bf16[58,16,128]{2,1,0:T(8,128)(2,1)S(1)}, bf16[58,16,128]{2,1,0:T(8,128)(2,1)S(1)}, u32[]{:S(2)}, u32[]{:S(2)}) %collective-permute-start) | collective-permute-done | bytes 237600 | tf_op jit(solution)/shard_map/ppermute | solution.py:641
  17.7 0.1 collective-permute-start.5
  17.8 0.0 collective-permute-done.1.refs_2_
  17.8 3.0 %collective-permute-start.6 = (bf16[29,16,128]{2,1,0:T(8,128)(2,1)S(1)}, bf16[29,16,128]{2,1,0:T(8,128)(2,1)S(1)}, u32[]{:S(2)}, u32[]{:S(2)}) collective-permute-start(bf16[29,16,128]{2,1,0:T(8,128)(2,1)S(1)} %get-tuple-element.35), channel_id=1, source_target_pairs={{0,7},{1,6},{2,5},{3,4},{4,3},{5,2},{6,1},{7,0},{8,15},{9,14},{10,... | collective-permute-start | bytes 356360 | tf_op jit(solution)/shard_map/ppermute | solution.py:641
  20.7 0.0 copy-done.4
  20.7 3.4 %scan.1.codes = s32[129]{0:T(256)S(1)} custom-call(s32[16,1,32]{2,1,0:T(1,128)S(1)} %bitcast.25), custom_call_target="tpu_custom_call" | custom-call | flops 20000000 | bytes 1048576 | tf_op jit(solution)/shard_map/scan/pallas_call | solution.py:615
  24.1 0.0 copy-done.3
  24.1 0.0 copy-done.2
  24.1 0.0 copy-done.1
  24.1 3.0 %slots.1 = (f32[17,16,256]{2,1,0:T(8,128)S(1)}, f32[40,256]{1,0:T(8,128)S(1)}, f32[3,128,128]{2,1,0:T(8,128)S(1)}, s32[3,128]{1,0:T(4,128)S(4)}) custom-call(f32[2,32]{1,0:T(2,128)S(1)} %bitcast.16, f32[2,32]{1,0:T(2,128)S(1)} %bitcast.19, s32[2,32]{1,0:T(2,128)S(1)} %bitcast.22, s32[129]{0:T(256)S(1)} %scan.1.codes), custom_call_target="tpu_custom_call" | custom-call | flops 20000000 | bytes 1048576 | tf_op jit(solution)/shard_map/slots/pallas_call | solution.py:625
  27.1 0.0 collective-permute-done.2.refs_3_
  27.1 0.0 collective-permute-done.3.refs_4_
  27.1 0.0 collective-permute-done.4.refs_5_
  27.1 0.0 collective-permute-done.5.refs_6_
  27.1 1.2 %first_blend.1 = (f32[17,16,256]{2,1,0:T(8,128)S(1)}, bf16[16,16,256]{2,1,0:T(8,128)(2,1)S(1)}, bf16[16,16,256]{2,1,0:T(8,128)(2,1)S(1)}, bf16[16,16,256]{2,1,0:...) custom-call(s32[3,128]{1,0:T(4,128)S(4)} %get-tuple-element.25.slot_, ...), custom_call_target="tpu_custom_call" | custom-call | flops 1000000 | bytes 2097152 | tf_op jit(solution)/shard_map/first_blend/pallas_call | solution.py:663
  28.3 0.0 collective-permute-done.6.refs_0_
  28.3 0.3 last_blend.1
  28.6 2.5 %collective-permute-start.7 = (bf16[16,16,256]{2,1,0:T(8,128)(2,1)S(1)}, bf16[16,16,256]{2,1,0:T(8,128)(2,1)S(1)}, u32[]{:S(2)}, u32[]{:S(2)}) collective-permute-start(bf16[16,16,256]{2,1,0:T(8,128)(2,1)S(1)} %get-tuple-element.36.grid), channel_id=1, source_target_pairs={{0,24},{8,0},{16,8},{24,16},{1,25},{9,1},{17,9},{25,17},{2,26},{10... | collective-permute-start | bytes 393224 | tf_op jit(solution)/shard_map/ppermute | solution.py:691
  31.1 1.9 %moments.1.base = f32[4,128]{1,0:T(4,128)S(1)} custom-call(f32[2,32]{1,0:T(2,128)S(1)} %bitcast.17, f32[2,32]{1,0:T(2,128)S(1)} %bitcast.20, s32[2,32]{1,0:T(2,128)S(1)} %bitcast.23, bf16[64,16,256]{2,1,0:T(8,128)(2,1)S(1)} %get-tuple-element.38.frames), custom_call_target="tpu_custom_call" | custom-call | flops 20000000 | bytes 1048576 | tf_op jit(solution)/shard_map/moments/pallas_call | solution.py:604
  33.0 0.6 %collective-permute-done.7.from_next = bf16[16,16,256]{2,1,0:T(8,128)(2,1)S(1)} collective-permute-done((bf16[16,16,256]{2,1,0:T(8,128)(2,1)S(1)}, bf16[16,16,256]{2,1,0:T(8,128)(2,1)S(1)}, u32[]{:S(2)}, u32[]{:S(2)}) %collective-permute-start.7) | collective-permute-done | bytes 131104 | tf_op jit(solution)/shard_map/ppermute | solution.py:691
  33.6 0.0 copy-done
  33.6 1.5 %gradient.1 = (f32[32,4,128]{2,1,0:T(4,128)S(1)}, bf16[16,16,256]{2,1,0:T(8,128)(2,1)}) custom-call(s32[3,128]{1,0:T(4,128)S(4)} %get-tuple-element.25.slot_bands, bf16[16,16,256]{2,1,0:T(8,128)(2,1)S(1)} %collective-permute-done.7.from_next, bf16[16,16,256]{2,1,0:T(8,128)(2,1)S(1)} %bitcast.14, f32[40,256]{1,0:T(8,128)S(1)} %get-tuple-element.26.col_cover, ...), custom_call_target="tpu_custom_call" | custom-call | flops 8000000 | bytes 2097152 | tf_op jit(solution)/shard_map/gradient/pallas_call | solution.py:693
  35.1 14.5 %all_to_all.5.received = f32[32,4,128]{2,1,0:T(4,128)S(1)} all-to-all(f32[32,4,128]{2,1,0:T(4,128)S(1)} %get-tuple-element.47), channel_id=1, replica_groups=mesh['sec'=4,'tile'=8] {'sec','tile'}, dimensions={0} | all-to-all | bytes 131072 | tf_op jit(solution)/shard_map/all_to_all | solution.py:720
  49.7 1.3 %solve.1 = f32[4,6]{1,0:T(4,128)} custom-call(f32[32,4,128]{2,1,0:T(4,128)S(1)} %all_to_all.5.received), custom_call_target="tpu_custom_call" | custom-call | flops 100000 | bytes 262144 | tf_op jit(solution)/shard_map/solve/pallas_call | solution.py:724
  (1 shorter events, 0.0 us)
Async XLA Ops:
  0.6 20.1 %copy-start.4 = (s32[1,32,16,1]{1,3,2,0:T(1,128)S(1)}, s32[1,32,16,1]{1,3,2,0:T(1,128)}, u32[]{:S(2)}) copy-start(s32[1,32,16,1]{1,3,2,0:T(1,128)} %param.10) | copy-start | bytes 6148
  0.6 23.5 %copy-start.3 = (s32[1,2,32]{2,1,0:T(2,128)S(1)}, s32[1,2,32]{2,1,0:T(2,128)}, u32[]{:S(2)}) copy-start(s32[1,2,32]{2,1,0:T(2,128)} %param.9) | copy-start | bytes 772
  0.7 23.5 %copy-start.2 = (f32[1,2,32]{2,1,0:T(2,128)S(1)}, f32[1,2,32]{2,1,0:T(2,128)}, u32[]{:S(2)}) copy-start(f32[1,2,32]{2,1,0:T(2,128)} %param.8) | copy-start | bytes 772
  0.7 23.5 %copy-start.1 = (f32[1,2,32]{2,1,0:T(2,128)S(1)}, f32[1,2,32]{2,1,0:T(2,128)}, u32[]{:S(2)}) copy-start(f32[1,2,32]{2,1,0:T(2,128)} %param.7) | copy-start | bytes 772
  0.7 32.9 %copy-start = (bf16[1,256,256]{2,1,0:T(8,128)(2,1)S(1)}, bf16[1,256,256]{2,1,0:T(8,128)(2,1)}, u32[]{:S(2)}) copy-start(bf16[1,256,256]{2,1,0:T(8,128)(2,1)} %param.11) | copy-start | bytes 393220
  4.1 13.5 %collective-permute-start = (bf16[58,16,128]{2,1,0:T(8,128)(2,1)S(1)}, bf16[58,16,128]{2,1,0:T(8,128)(2,1)S(1)}, u32[]{:S(2)}, u32[]{:S(2)}) collective-permute-start(bf16[58,16,128]{2,1,0:T(8,128)(2,1)S(1)} %get-tuple-element.29), channel_id=1, source_target_pairs={{0,2},{1,3},{2,0},{3,1},{4,6},{5,7},{6,4},{7,5},{8,10},{9,11},{10,... | collective-permute-start | bytes 712712 | tf_op jit(solution)/shard_map/ppermute | solution.py:641
  7.2 10.5 %collective-permute-start.1 = (bf16[29,16,128]{2,1,0:T(8,128)(2,1)S(1)}, bf16[29,16,128]{2,1,0:T(8,128)(2,1)S(1)}, u32[]{:S(2)}, u32[]{:S(2)}) collective-permute-start(bf16[29,16,128]{2,1,0:T(8,128)(2,1)S(1)} %get-tuple-element.30), channel_id=1, source_target_pairs={{0,4},{1,5},{2,6},{3,7},{4,0},{5,1},{6,2},{7,3},{8,12},{9,13},{10,... | collective-permute-start | bytes 356360 | tf_op jit(solution)/shard_map/ppermute | solution.py:641
  9.8 17.3 %collective-permute-start.2 = (bf16[29,16,128]{2,1,0:T(8,128)(2,1)S(1)}, bf16[29,16,128]{2,1,0:T(8,128)(2,1)S(1)}, u32[]{:S(2)}, u32[]{:S(2)}) collective-permute-start(bf16[29,16,128]{2,1,0:T(8,128)(2,1)S(1)} %get-tuple-element.31), channel_id=1, source_target_pairs={{0,5},{1,4},{2,7},{3,6},{4,1},{5,0},{6,3},{7,2},{8,13},{9,12},{10,... | collective-permute-start | bytes 356360 | tf_op jit(solution)/shard_map/ppermute | solution.py:641
  9.8 17.3 %collective-permute-start.3 = (bf16[29,16,128]{2,1,0:T(8,128)(2,1)S(1)}, bf16[29,16,128]{2,1,0:T(8,128)(2,1)S(1)}, u32[]{:S(2)}, u32[]{:S(2)}) collective-permute-start(bf16[29,16,128]{2,1,0:T(8,128)(2,1)S(1)} %get-tuple-element.32), channel_id=1, source_target_pairs={{0,6},{1,7},{2,4},{3,5},{4,2},{5,3},{6,0},{7,1},{8,14},{9,15},{10,... | collective-permute-start | bytes 356360 | tf_op jit(solution)/shard_map/ppermute | solution.py:641
  11.5 15.6 %collective-permute-start.4 = (bf16[29,16,128]{2,1,0:T(8,128)(2,1)S(1)}, bf16[29,16,128]{2,1,0:T(8,128)(2,1)S(1)}, u32[]{:S(2)}, u32[]{:S(2)}) collective-permute-start(bf16[29,16,128]{2,1,0:T(8,128)(2,1)S(1)} %get-tuple-element.33), channel_id=1, source_target_pairs={{0,1},{1,0},{2,3},{3,2},{4,5},{5,4},{6,7},{7,6},{8,9},{9,8},{10,11... | collective-permute-start | bytes 356360 | tf_op jit(solution)/shard_map/ppermute | solution.py:641
  17.7 9.5 %collective-permute-start.5 = (bf16[29,16,128]{2,1,0:T(8,128)(2,1)S(1)}, bf16[29,16,128]{2,1,0:T(8,128)(2,1)S(1)}, u32[]{:S(2)}, u32[]{:S(2)}) collective-permute-start(bf16[29,16,128]{2,1,0:T(8,128)(2,1)S(1)} %slice.4), channel_id=1, source_target_pairs={{0,1},{1,0},{2,3},{3,2},{4,5},{5,4},{6,7},{7,6},{8,9},{9,8},{10,11... | collective-permute-start | bytes 356360 | tf_op jit(solution)/shard_map/ppermute | solution.py:641
  17.8 10.5 %collective-permute-start.6 = (bf16[29,16,128]{2,1,0:T(8,128)(2,1)S(1)}, bf16[29,16,128]{2,1,0:T(8,128)(2,1)S(1)}, u32[]{:S(2)}, u32[]{:S(2)}) collective-permute-start(bf16[29,16,128]{2,1,0:T(8,128)(2,1)S(1)} %get-tuple-element.35), channel_id=1, source_target_pairs={{0,7},{1,6},{2,5},{3,4},{4,3},{5,2},{6,1},{7,0},{8,15},{9,14},{10,... | collective-permute-start | bytes 356360 | tf_op jit(solution)/shard_map/ppermute | solution.py:641
  28.6 5.0 %collective-permute-start.7 = (bf16[16,16,256]{2,1,0:T(8,128)(2,1)S(1)}, bf16[16,16,256]{2,1,0:T(8,128)(2,1)S(1)}, u32[]{:S(2)}, u32[]{:S(2)}) collective-permute-start(bf16[16,16,256]{2,1,0:T(8,128)(2,1)S(1)} %get-tuple-element.36.grid), channel_id=1, source_target_pairs={{0,24},{8,0},{16,8},{24,16},{1,25},{9,1},{17,9},{25,17},{2,26},{10... | collective-permute-start | bytes 393224 | tf_op jit(solution)/shard_map/ppermute | solution.py:691

commit v8 on v7

--- a/solution.py
+++ b/solution.py
@@ -359,14 +359,30 @@
     grid[...] = (total[:bands] / (1.0 + cover_sum[:bands])).astype(jnp.bfloat16)
 
 
+def weight_kernel(sizes, slot_lines, weights, sums):
+    tiles, bands, frame, source, capacity, devices = sizes
+    sums[...] = jnp.zeros_like(sums)
+    spots = spots_along((BAND, LANES), 0)
+    raised = spots * (2.0 / frame)
+
+    @pl.loop(0, devices * capacity // ROWS)
+    def _(group):
+        for k in range(ROWS):
+            slot = group * ROWS + k
+            here = pl.ds(slot, 1)
+            cover = cover_of(spots * slot_lines[0, here, :] + slot_lines[1, here, :], source)
+            weights[0, slot] = cover
+            weights[1, slot] = cover * (raised + slot_lines[2, here, :])
+
+
 GRADIENT_ROWS = ({0: 0, 1: 1}, {2: 0}, {3: 0, 4: 1}, {5: 0})
 
 
 def gradient_kernel(
-    sizes, slot_bands, from_next, top_grid, col_cover, slot_lines, base, grid, *blocks_and_rest
+    sizes, slot_bands, from_next, top_grid, col_cover, weights, _, base, grid, *blocks_and_rest
 ):
     tiles, bands, frame, source, capacity, devices = sizes
-    *blocks, payload, grid_out, above, sums, grid_sem = blocks_and_rest
+    *blocks, payload, grid_out, sums, above, grid_sem = blocks_and_rest
     written = pltpu.make_async_copy(grid, grid_out, grid_sem)
     written.start()
     sec = lax.axis_index("sec")
@@ -381,19 +397,13 @@
         above[:bands] = from_next[...].astype(jnp.float32)
 
     above[bands] = jnp.zeros((BAND, frame), jnp.float32)
-    sums[...] = jnp.zeros_like(sums)
-    spots = spots_along((BAND, LANES), 0)
-    raised = spots * (2.0 / frame)
     halves = range(frame // LANES)
 
     for block, (array, _) in enumerate(exchange_plan(devices)[1]):
         running = None
         for k in range(capacity):
             slot = block * capacity + k
-            here = slice(slot, slot + 1)
-            points = spots * slot_lines[0, here] + slot_lines[1, here]
-            cover = cover_of(points, source)
-            lifted = cover * (raised + slot_lines[2, here])
+            cover, lifted = weights[0, slot], weights[1, slot]
             level = blocks[array][k].astype(jnp.float32)
             error = above[slot_bands[0, slot]] - level
             product = error * level
@@ -690,20 +700,32 @@
 
     from_next = lax.ppermute(grid, "sec", [(i, (i - 1) % sections) for i in range(sections)])
 
-    payload, grid_out = pl.pallas_call(
+    sums = jax.ShapeDtypeStruct((4 * frame // LANES, (all_tiles + 1) * ROWS, LANES), jnp.float32)
+    weights, zeros = pl.pallas_call(
+        functools.partial(weight_kernel, sizes),
+        name="weights",
+        in_specs=[VMEM],
+        out_specs=[VMEM] * 2,
+        out_shape=[jax.ShapeDtypeStruct((2, slots, BAND, LANES), jnp.float32), sums],
+        compiler_params=params(24),
+        cost_estimate=cost(1_000_000, 1 << 20),
+    )(slot_lines)
+
+    payload, grid_out, _ = pl.pallas_call(
         functools.partial(gradient_kernel, sizes),
         name="gradient",
-        in_specs=[SMEM] + [VMEM] * (6 + len(incoming)),
-        out_specs=[VMEM, HBM],
+        in_specs=[SMEM] + [VMEM] * (7 + len(incoming)),
+        out_specs=[VMEM, HBM, VMEM],
         out_shape=[
             jax.ShapeDtypeStruct((sections * devices, PAYLOAD_ROWS, width), jnp.float32),
             jax.ShapeDtypeStruct((bands, BAND, frame), jnp.bfloat16),
+            sums,
         ],
         scratch_shapes=[
             pltpu.VMEM((bands + 1, BAND, frame), jnp.float32),
-            pltpu.VMEM((4 * frame // LANES, (all_tiles + 1) * ROWS, LANES), jnp.float32),
             pltpu.SemaphoreType.DMA,
         ],
+        input_output_aliases={5: 2},
         compiler_params=params(24),
         cost_estimate=cost(8_000_000, 2 << 20),
     )(
@@ -711,7 +733,8 @@
         from_next,
         top_grid.reshape(bands, BAND, frame),
         col_cover,
-        slot_lines,
+        weights,
+        zeros,
         base,
         grid,
         *incoming,

time: 51.1 us -> 50.9 us (level)
  transfers between devices with their start and end apart: 8 -> 8, of which waited for: 2 -> 2; matrix products, arithmetic and copies ran while one was open for 0% -> 0% of each run, Pallas kernels for 18% -> 19%
where the time goes in v8:
time: 50.9 us; the launch traced here: 50.7 us
  Pallas kernels  15.9 us (31%)
  blocking collectives  14.7 us (29%)
  starting transfers between devices  13.9 us (27%)
  waiting for transfers between devices  5.38 us (11%)
  between operations  0.79 us (2%)
    all_to_all x1, blocking collectives, shards(): lax.all_to_all(payload, ('sec', 'tile'), split_axis=0, concat_axis=0, til...  14.7 us
    ppermute x7, starting transfers between devices, swapped(): lax.ppermute(block, 'tile', [(i, i ^ distance) for i in range(devices)])  11.4 us
    ppermute x7, waiting for transfers between devices, swapped(): lax.ppermute(block, 'tile', [(i, i ^ distance) for i in range(devices)])  5.19 us
    pallas_call x1, Pallas kernels, shards(): pl.pallas_call(functools.partial(render_kernel, sizes), name='render', in...  3.46 us
    pallas_call x1, Pallas kernels, shards(): pl.pallas_call(functools.partial(scan_kernel, sizes), name='scan', in_spe...  3.17 us
    pallas_call x1, Pallas kernels, shards(): pl.pallas_call(functools.partial(slot_kernel, sizes), name='slots', in_sp...  2.96 us
    ppermute x1, starting transfers between devices, shards(): lax.ppermute(grid, 'sec', [(i, (i - 1) % sections) for i in range(section...  2.57 us
    pallas_call x1, Pallas kernels, shards(): pl.pallas_call(functools.partial(moment_kernel, sizes), name='moments', i...  1.9 us
  transfers between devices with their start and end apart: 8, of which 2 were waited for; matrix products, arithmetic and copies ran while one was open for 0% of the time, Pallas kernels for 19%

profile of v8, /device:TPU:0, one launch (start us, length us, event | category | flops | bytes accessed | tf_op | source)
XLA Modules:
  0.0 50.7 jit_solution(13940883385466846236)
XLA Ops:
  0.6 0.0 copy-start.4
  0.6 0.0 copy-start.3
  0.7 0.0 copy-start.2
  0.7 0.0 copy-start.1
  0.7 3.5 %render.1 = (bf16[64,16,256]{2,1,0:T(8,128)(2,1)S(1)}, bf16[16,16,256]{2,1,0:T(8,128)(2,1)S(1)}, bf16[58,16,128]{2,1,0:T(8,128)(2,1)S(1)}, bf16[29,16,128]{2,1,0...) custom-call(f32[2,32]{1,0:T(2,128)} %bitcast.15, ...), custom_call_target="tpu_custom_call" | custom-call | flops 800000000 | bytes 4194304 | tf_op jit(solution)/shard_map/render/pallas_call | solution.py:593
  4.1 0.0 copy-start
  4.1 3.1 %collective-permute-start = (bf16[58,16,128]{2,1,0:T(8,128)(2,1)S(1)}, bf16[58,16,128]{2,1,0:T(8,128)(2,1)S(1)}, u32[]{:S(2)}, u32[]{:S(2)}) collective-permute-start(bf16[58,16,128]{2,1,0:T(8,128)(2,1)S(1)} %get-tuple-element.31), channel_id=1, source_target_pairs={{0,2},{1,3},{2,0},{3,1},{4,6},{5,7},{6,4},{7,5},{8,10},{9,11},{10,... | collective-permute-start | bytes 712712 | tf_op jit(solution)/shard_map/ppermute | solution.py:651
  7.2 2.6 %collective-permute-start.1 = (bf16[29,16,128]{2,1,0:T(8,128)(2,1)S(1)}, bf16[29,16,128]{2,1,0:T(8,128)(2,1)S(1)}, u32[]{:S(2)}, u32[]{:S(2)}) collective-permute-start(bf16[29,16,128]{2,1,0:T(8,128)(2,1)S(1)} %get-tuple-element.32), channel_id=1, source_target_pairs={{0,4},{1,5},{2,6},{3,7},{4,0},{5,1},{6,2},{7,3},{8,12},{9,13},{10,... | collective-permute-start | bytes 356360 | tf_op jit(solution)/shard_map/ppermute | solution.py:651
  9.8 0.0 collective-permute-start.2
  9.8 1.7 %collective-permute-start.3 = (bf16[29,16,128]{2,1,0:T(8,128)(2,1)S(1)}, bf16[29,16,128]{2,1,0:T(8,128)(2,1)S(1)}, u32[]{:S(2)}, u32[]{:S(2)}) collective-permute-start(bf16[29,16,128]{2,1,0:T(8,128)(2,1)S(1)} %get-tuple-element.34), channel_id=1, source_target_pairs={{0,6},{1,7},{2,4},{3,5},{4,2},{5,3},{6,0},{7,1},{8,14},{9,15},{10,... | collective-permute-start | bytes 356360 | tf_op jit(solution)/shard_map/ppermute | solution.py:651
  11.5 1.0 %collective-permute-start.4 = (bf16[29,16,128]{2,1,0:T(8,128)(2,1)S(1)}, bf16[29,16,128]{2,1,0:T(8,128)(2,1)S(1)}, u32[]{:S(2)}, u32[]{:S(2)}) collective-permute-start(bf16[29,16,128]{2,1,0:T(8,128)(2,1)S(1)} %get-tuple-element.35), channel_id=1, source_target_pairs={{0,1},{1,0},{2,3},{3,2},{4,5},{5,4},{6,7},{7,6},{8,9},{9,8},{10,11... | collective-permute-start | bytes 356360 | tf_op jit(solution)/shard_map/ppermute | solution.py:651
  12.5 5.2 %collective-permute-done.refs_1_ = bf16[58,16,128]{2,1,0:T(8,128)(2,1)S(1)} collective-permute-done((bf16[58,16,128]{2,1,0:T(8,128)(2,1)S(1)}, bf16[58,16,128]{2,1,0:T(8,128)(2,1)S(1)}, u32[]{:S(2)}, u32[]{:S(2)}) %collective-permute-start) | collective-permute-done | bytes 237600 | tf_op jit(solution)/shard_map/ppermute | solution.py:651
  17.7 0.1 collective-permute-start.5
  17.7 0.0 collective-permute-done.1.refs_2_
  17.7 3.0 %collective-permute-start.6 = (bf16[29,16,128]{2,1,0:T(8,128)(2,1)S(1)}, bf16[29,16,128]{2,1,0:T(8,128)(2,1)S(1)}, u32[]{:S(2)}, u32[]{:S(2)}) collective-permute-start(bf16[29,16,128]{2,1,0:T(8,128)(2,1)S(1)} %get-tuple-element.37), channel_id=1, source_target_pairs={{0,7},{1,6},{2,5},{3,4},{4,3},{5,2},{6,1},{7,0},{8,15},{9,14},{10,... | collective-permute-start | bytes 356360 | tf_op jit(solution)/shard_map/ppermute | solution.py:651
  20.7 0.0 copy-done.4
  20.7 3.2 %scan.1.codes = s32[129]{0:T(256)S(1)} custom-call(s32[16,1,32]{2,1,0:T(1,128)S(1)} %bitcast.25), custom_call_target="tpu_custom_call" | custom-call | flops 20000000 | bytes 1048576 | tf_op jit(solution)/shard_map/scan/pallas_call | solution.py:625
  23.9 0.0 copy-done.3
  23.9 0.0 copy-done.2
  23.9 0.0 copy-done.1
  23.9 3.0 %slots.1 = (f32[17,16,256]{2,1,0:T(8,128)S(1)}, f32[40,256]{1,0:T(8,128)S(1)}, f32[3,128,128]{2,1,0:T(8,128)S(1)}, s32[3,128]{1,0:T(4,128)S(4)}) custom-call(f32[2,32]{1,0:T(2,128)S(1)} %bitcast.16, f32[2,32]{1,0:T(2,128)S(1)} %bitcast.19, s32[2,32]{1,0:T(2,128)S(1)} %bitcast.22, s32[129]{0:T(256)S(1)} %scan.1.codes), custom_call_target="tpu_custom_call" | custom-call | flops 20000000 | bytes 1048576 | tf_op jit(solution)/shard_map/slots/pallas_call | solution.py:635
  26.9 0.0 collective-permute-done.2.refs_3_
  26.9 0.0 collective-permute-done.3.refs_4_
  26.9 0.0 collective-permute-done.4.refs_5_
  26.9 0.0 collective-permute-done.5.refs_6_
  26.9 1.2 %first_blend.1 = (f32[17,16,256]{2,1,0:T(8,128)S(1)}, bf16[16,16,256]{2,1,0:T(8,128)(2,1)S(1)}, bf16[16,16,256]{2,1,0:T(8,128)(2,1)S(1)}, bf16[16,16,256]{2,1,0:...) custom-call(s32[3,128]{1,0:T(4,128)S(4)} %get-tuple-element.27.slot_, ...), custom_call_target="tpu_custom_call" | custom-call | flops 1000000 | bytes 2097152 | tf_op jit(solution)/shard_map/first_blend/pallas_call | solution.py:673
  28.1 0.0 collective-permute-done.6.refs_0_
  28.1 0.3 last_blend.1
  28.4 2.6 %collective-permute-start.7 = (bf16[16,16,256]{2,1,0:T(8,128)(2,1)S(1)}, bf16[16,16,256]{2,1,0:T(8,128)(2,1)S(1)}, u32[]{:S(2)}, u32[]{:S(2)}) collective-permute-start(bf16[16,16,256]{2,1,0:T(8,128)(2,1)S(1)} %get-tuple-element.38.grid), channel_id=1, source_target_pairs={{0,24},{8,0},{16,8},{24,16},{1,25},{9,1},{17,9},{25,17},{2,26},{10... | collective-permute-start | bytes 393224 | tf_op jit(solution)/shard_map/ppermute | solution.py:701
  30.9 0.4 weights.1
  31.4 1.9 %moments.1.base = f32[4,128]{1,0:T(4,128)S(1)} custom-call(f32[2,32]{1,0:T(2,128)S(1)} %bitcast.17, f32[2,32]{1,0:T(2,128)S(1)} %bitcast.20, s32[2,32]{1,0:T(2,128)S(1)} %bitcast.23, bf16[64,16,256]{2,1,0:T(8,128)(2,1)S(1)} %get-tuple-element.42.frames), custom_call_target="tpu_custom_call" | custom-call | flops 20000000 | bytes 1048576 | tf_op jit(solution)/shard_map/moments/pallas_call | solution.py:614
  33.3 0.2 collective-permute-done.7.from_next
  33.5 0.0 copy-done
  33.5 1.2 %gradient.1 = (f32[32,4,128]{2,1,0:T(4,128)S(1)}, bf16[16,16,256]{2,1,0:T(8,128)(2,1)}, f32[8,264,128]{2,1,0:T(8,128)S(1)}) custom-call(s32[3,128]{1,0:T(4,128)S(4)} %get-tuple-element.27.slot_bands, bf16[16,16,256]{2,1,0:T(8,128)(2,1)S(1)} %collective-permute-done.7.from_next, bf16[16,16,256]{2,1,0:T(8,128)(2,1)S(1)} %bitcast.14, ...), custom_call_target="tpu_custom_call", output_to_operand_aliasing={{2}: (5, {})} | custom-call | flops 8000000 | bytes 2097152 | tf_op jit(solution)/shard_map/gradient/pallas_call | solution.py:714
  34.7 14.7 %all_to_all.5.received = f32[32,4,128]{2,1,0:T(4,128)S(1)} all-to-all(f32[32,4,128]{2,1,0:T(4,128)S(1)} %get-tuple-element.51), channel_id=1, replica_groups=mesh['sec'=4,'tile'=8] {'sec','tile'}, dimensions={0} | all-to-all | bytes 131072 | tf_op jit(solution)/shard_map/all_to_all | solution.py:743
  49.4 1.3 %solve.1 = f32[4,6]{1,0:T(4,128)} custom-call(f32[32,4,128]{2,1,0:T(4,128)S(1)} %all_to_all.5.received), custom_call_target="tpu_custom_call" | custom-call | flops 100000 | bytes 262144 | tf_op jit(solution)/shard_map/solve/pallas_call | solution.py:747
  (1 shorter events, 0.0 us)
Async XLA Ops:
  0.6 20.1 %copy-start.4 = (s32[1,32,16,1]{1,3,2,0:T(1,128)S(1)}, s32[1,32,16,1]{1,3,2,0:T(1,128)}, u32[]{:S(2)}) copy-start(s32[1,32,16,1]{1,3,2,0:T(1,128)} %param.10) | copy-start | bytes 6148
  0.6 23.3 %copy-start.3 = (s32[1,2,32]{2,1,0:T(2,128)S(1)}, s32[1,2,32]{2,1,0:T(2,128)}, u32[]{:S(2)}) copy-start(s32[1,2,32]{2,1,0:T(2,128)} %param.9) | copy-start | bytes 772
  0.7 23.3 %copy-start.2 = (f32[1,2,32]{2,1,0:T(2,128)S(1)}, f32[1,2,32]{2,1,0:T(2,128)}, u32[]{:S(2)}) copy-start(f32[1,2,32]{2,1,0:T(2,128)} %param.8) | copy-start | bytes 772
  0.7 23.3 %copy-start.1 = (f32[1,2,32]{2,1,0:T(2,128)S(1)}, f32[1,2,32]{2,1,0:T(2,128)}, u32[]{:S(2)}) copy-start(f32[1,2,32]{2,1,0:T(2,128)} %param.7) | copy-start | bytes 772
  4.1 29.3 %copy-start = (bf16[1,256,256]{2,1,0:T(8,128)(2,1)S(1)}, bf16[1,256,256]{2,1,0:T(8,128)(2,1)}, u32[]{:S(2)}) copy-start(bf16[1,256,256]{2,1,0:T(8,128)(2,1)} %param.11) | copy-start | bytes 393220
  4.1 13.5 %collective-permute-start = (bf16[58,16,128]{2,1,0:T(8,128)(2,1)S(1)}, bf16[58,16,128]{2,1,0:T(8,128)(2,1)S(1)}, u32[]{:S(2)}, u32[]{:S(2)}) collective-permute-start(bf16[58,16,128]{2,1,0:T(8,128)(2,1)S(1)} %get-tuple-element.31), channel_id=1, source_target_pairs={{0,2},{1,3},{2,0},{3,1},{4,6},{5,7},{6,4},{7,5},{8,10},{9,11},{10,... | collective-permute-start | bytes 712712 | tf_op jit(solution)/shard_map/ppermute | solution.py:651
  7.2 10.5 %collective-permute-start.1 = (bf16[29,16,128]{2,1,0:T(8,128)(2,1)S(1)}, bf16[29,16,128]{2,1,0:T(8,128)(2,1)S(1)}, u32[]{:S(2)}, u32[]{:S(2)}) collective-permute-start(bf16[29,16,128]{2,1,0:T(8,128)(2,1)S(1)} %get-tuple-element.32), channel_id=1, source_target_pairs={{0,4},{1,5},{2,6},{3,7},{4,0},{5,1},{6,2},{7,3},{8,12},{9,13},{10,... | collective-permute-start | bytes 356360 | tf_op jit(solution)/shard_map/ppermute | solution.py:651
  9.8 17.1 %collective-permute-start.2 = (bf16[29,16,128]{2,1,0:T(8,128)(2,1)S(1)}, bf16[29,16,128]{2,1,0:T(8,128)(2,1)S(1)}, u32[]{:S(2)}, u32[]{:S(2)}) collective-permute-start(bf16[29,16,128]{2,1,0:T(8,128)(2,1)S(1)} %get-tuple-element.33), channel_id=1, source_target_pairs={{0,5},{1,4},{2,7},{3,6},{4,1},{5,0},{6,3},{7,2},{8,13},{9,12},{10,... | collective-permute-start | bytes 356360 | tf_op jit(solution)/shard_map/ppermute | solution.py:651
  9.8 17.1 %collective-permute-start.3 = (bf16[29,16,128]{2,1,0:T(8,128)(2,1)S(1)}, bf16[29,16,128]{2,1,0:T(8,128)(2,1)S(1)}, u32[]{:S(2)}, u32[]{:S(2)}) collective-permute-start(bf16[29,16,128]{2,1,0:T(8,128)(2,1)S(1)} %get-tuple-element.34), channel_id=1, source_target_pairs={{0,6},{1,7},{2,4},{3,5},{4,2},{5,3},{6,0},{7,1},{8,14},{9,15},{10,... | collective-permute-start | bytes 356360 | tf_op jit(solution)/shard_map/ppermute | solution.py:651
  11.5 15.4 %collective-permute-start.4 = (bf16[29,16,128]{2,1,0:T(8,128)(2,1)S(1)}, bf16[29,16,128]{2,1,0:T(8,128)(2,1)S(1)}, u32[]{:S(2)}, u32[]{:S(2)}) collective-permute-start(bf16[29,16,128]{2,1,0:T(8,128)(2,1)S(1)} %get-tuple-element.35), channel_id=1, source_target_pairs={{0,1},{1,0},{2,3},{3,2},{4,5},{5,4},{6,7},{7,6},{8,9},{9,8},{10,11... | collective-permute-start | bytes 356360 | tf_op jit(solution)/shard_map/ppermute | solution.py:651
  17.7 9.3 %collective-permute-start.5 = (bf16[29,16,128]{2,1,0:T(8,128)(2,1)S(1)}, bf16[29,16,128]{2,1,0:T(8,128)(2,1)S(1)}, u32[]{:S(2)}, u32[]{:S(2)}) collective-permute-start(bf16[29,16,128]{2,1,0:T(8,128)(2,1)S(1)} %slice.4), channel_id=1, source_target_pairs={{0,1},{1,0},{2,3},{3,2},{4,5},{5,4},{6,7},{7,6},{8,9},{9,8},{10,11... | collective-permute-start | bytes 356360 | tf_op jit(solution)/shard_map/ppermute | solution.py:651
  17.7 10.4 %collective-permute-start.6 = (bf16[29,16,128]{2,1,0:T(8,128)(2,1)S(1)}, bf16[29,16,128]{2,1,0:T(8,128)(2,1)S(1)}, u32[]{:S(2)}, u32[]{:S(2)}) collective-permute-start(bf16[29,16,128]{2,1,0:T(8,128)(2,1)S(1)} %get-tuple-element.37), channel_id=1, source_target_pairs={{0,7},{1,6},{2,5},{3,4},{4,3},{5,2},{6,1},{7,0},{8,15},{9,14},{10,... | collective-permute-start | bytes 356360 | tf_op jit(solution)/shard_map/ppermute | solution.py:651
  28.4 5.1 %collective-permute-start.7 = (bf16[16,16,256]{2,1,0:T(8,128)(2,1)S(1)}, bf16[16,16,256]{2,1,0:T(8,128)(2,1)S(1)}, u32[]{:S(2)}, u32[]{:S(2)}) collective-permute-start(bf16[16,16,256]{2,1,0:T(8,128)(2,1)S(1)} %get-tuple-element.38.grid), channel_id=1, source_target_pairs={{0,24},{8,0},{16,8},{24,16},{1,25},{9,1},{17,9},{25,17},{2,26},{10... | collective-permute-start | bytes 393224 | tf_op jit(solution)/shard_map/ppermute | solution.py:701

commit v9 on v8

--- a/solution.py
+++ b/solution.py
@@ -144,6 +144,7 @@
         rows[slot] = 0
     for copy in small:
         copy.wait()
+    halves = []
     for j in range(tiles):
         tile = first_tile + j
         row_points = points_of(spots_along((frame, LANES), 0), zoom, frac, offset, 0, tile, ratio)
@@ -154,15 +155,6 @@
             ],
             axis=1,
         )
-        col_points = points_of(spots_along((ROWS, frame), 1), zoom, frac, offset, 1, tile, ratio)
-        over = moved(col_points[:, frame - LANES :], LANES - SPARE, 0)
-        lane = lax.broadcasted_iota(jnp.int32, over.shape, 1)
-        folded = (lane < SPARE) & (cover_of(over, source) > 0.0)
-        col_points = jnp.concatenate(
-            [jnp.where(folded, over, col_points[:, :LANES]), col_points[:, LANES:]], axis=1
-        )
-        col_points = jnp.broadcast_to(col_points[:1], (source, frame))
-        col_weights = hat_weight(col_points - spots_along((source, frame), 0)).astype(jnp.bfloat16)
         fetched[j].wait()
         half, quarter = source // 2, frame // 4
         upper = jnp.dot(
@@ -177,16 +169,29 @@
         )
         halfway = jnp.concatenate(
             [upper[:quarter], upper[quarter:] + lower[: 2 * quarter], lower[2 * quarter :]]
-        )
-        rendered = jnp.dot(
-            halfway.astype(jnp.bfloat16), col_weights, preferred_element_type=jnp.float32
         ).astype(jnp.bfloat16)
-        frames[j * bands : (j + 1) * bands] = rendered.reshape(bands, BAND, frame)
         for band in range(bands):
             target = owner[band, 0, tile]
             slot = named[target]
             named[target] = slot + 1
             rows[target * capacity + slot] = j * bands + band
+        halves.append(halfway)
+    for j in range(tiles):
+        tile = first_tile + j
+        col_points = points_of(spots_along((ROWS, frame), 1), zoom, frac, offset, 1, tile, ratio)
+        over = moved(col_points[:, frame - LANES :], LANES - SPARE, 0)
+        lane = lax.broadcasted_iota(jnp.int32, over.shape, 1)
+        folded = (lane < SPARE) & (cover_of(over, source) > 0.0)
+        col_points = jnp.concatenate(
+            [jnp.where(folded, over, col_points[:, :LANES]), col_points[:, LANES:]], axis=1
+        )
+        col_points = jnp.broadcast_to(col_points[:1], (source, frame))
+        col_weights = hat_weight(col_points - spots_along((source, frame), 0)).astype(jnp.bfloat16)
+        halfway = halves[j]
+        rendered = jnp.dot(
+            halfway, col_weights, preferred_element_type=jnp.float32
+        ).astype(jnp.bfloat16)
+        frames[j * bands : (j + 1) * bands] = rendered.reshape(bands, BAND, frame)
     for there, group in zip(outgoing, plan):
         for position, distance in enumerate(group):
             target = me ^ distance

time: 50.9 us -> 50.3 us (0.988)
    pallas_call x1, Pallas kernels: 3.46 us -> 2.89 us  [shards(): pl.pallas_call(functools.partial(render_kernel, sizes), name='render', in...]
where the time goes in v9:
time: 50.3 us; the launch traced here: 50.1 us
  Pallas kernels  15.4 us (31%)
  blocking collectives  14.6 us (29%)
  starting transfers between devices  13.8 us (27%)
  waiting for transfers between devices  5.45 us (11%)
  between operations  0.79 us (2%)
    all_to_all x1, blocking collectives, shards(): lax.all_to_all(payload, ('sec', 'tile'), split_axis=0, concat_axis=0, til...  14.6 us
    ppermute x7, starting transfers between devices, swapped(): lax.ppermute(block, 'tile', [(i, i ^ distance) for i in range(devices)])  11.4 us
    ppermute x7, waiting for transfers between devices, swapped(): lax.ppermute(block, 'tile', [(i, i ^ distance) for i in range(devices)])  5.21 us
    pallas_call x1, Pallas kernels, shards(): pl.pallas_call(functools.partial(scan_kernel, sizes), name='scan', in_spe...  3.29 us
    pallas_call x1, Pallas kernels, shards(): pl.pallas_call(functools.partial(slot_kernel, sizes), name='slots', in_sp...  2.96 us
    pallas_call x1, Pallas kernels, shards(): pl.pallas_call(functools.partial(render_kernel, sizes), name='render', in...  2.89 us
    ppermute x1, starting transfers between devices, shards(): lax.ppermute(grid, 'sec', [(i, (i - 1) % sections) for i in range(section...  2.44 us
    pallas_call x1, Pallas kernels, shards(): pl.pallas_call(functools.partial(moment_kernel, sizes), name='moments', i...  1.9 us
  transfers between devices with their start and end apart: 8, of which 2 were waited for; matrix products, arithmetic and copies ran while one was open for 0% of the time, Pallas kernels for 19%

profile of v9, /device:TPU:0, one launch (start us, length us, event | category | flops | bytes accessed | tf_op | source)
XLA Modules:
  0.0 50.1 jit_solution(956596463305301857)
XLA Ops:
  0.6 0.0 copy-start.4
  0.6 0.0 copy-start.3
  0.7 0.0 copy-start.2
  0.7 0.0 copy-start.1
  0.7 2.9 %render.1 = (bf16[64,16,256]{2,1,0:T(8,128)(2,1)S(1)}, bf16[16,16,256]{2,1,0:T(8,128)(2,1)S(1)}, bf16[58,16,128]{2,1,0:T(8,128)(2,1)S(1)}, bf16[29,16,128]{2,1,0...) custom-call(f32[2,32]{1,0:T(2,128)} %bitcast.15, ...), custom_call_target="tpu_custom_call" | custom-call | flops 800000000 | bytes 4194304 | tf_op jit(solution)/shard_map/render/pallas_call | solution.py:598
  3.6 0.0 copy-start
  3.6 3.1 %collective-permute-start = (bf16[58,16,128]{2,1,0:T(8,128)(2,1)S(1)}, bf16[58,16,128]{2,1,0:T(8,128)(2,1)S(1)}, u32[]{:S(2)}, u32[]{:S(2)}) collective-permute-start(bf16[58,16,128]{2,1,0:T(8,128)(2,1)S(1)} %get-tuple-element.31), channel_id=1, source_target_pairs={{0,2},{1,3},{2,0},{3,1},{4,6},{5,7},{6,4},{7,5},{8,10},{9,11},{10,... | collective-permute-start | bytes 712712 | tf_op jit(solution)/shard_map/ppermute | solution.py:656
  6.7 2.6 %collective-permute-start.1 = (bf16[29,16,128]{2,1,0:T(8,128)(2,1)S(1)}, bf16[29,16,128]{2,1,0:T(8,128)(2,1)S(1)}, u32[]{:S(2)}, u32[]{:S(2)}) collective-permute-start(bf16[29,16,128]{2,1,0:T(8,128)(2,1)S(1)} %get-tuple-element.32), channel_id=1, source_target_pairs={{0,4},{1,5},{2,6},{3,7},{4,0},{5,1},{6,2},{7,3},{8,12},{9,13},{10,... | collective-permute-start | bytes 356360 | tf_op jit(solution)/shard_map/ppermute | solution.py:656
  9.3 0.0 collective-permute-start.2
  9.3 1.7 %collective-permute-start.3 = (bf16[29,16,128]{2,1,0:T(8,128)(2,1)S(1)}, bf16[29,16,128]{2,1,0:T(8,128)(2,1)S(1)}, u32[]{:S(2)}, u32[]{:S(2)}) collective-permute-start(bf16[29,16,128]{2,1,0:T(8,128)(2,1)S(1)} %get-tuple-element.34), channel_id=1, source_target_pairs={{0,6},{1,7},{2,4},{3,5},{4,2},{5,3},{6,0},{7,1},{8,14},{9,15},{10,... | collective-permute-start | bytes 356360 | tf_op jit(solution)/shard_map/ppermute | solution.py:656
  11.0 1.0 %collective-permute-start.4 = (bf16[29,16,128]{2,1,0:T(8,128)(2,1)S(1)}, bf16[29,16,128]{2,1,0:T(8,128)(2,1)S(1)}, u32[]{:S(2)}, u32[]{:S(2)}) collective-permute-start(bf16[29,16,128]{2,1,0:T(8,128)(2,1)S(1)} %get-tuple-element.35), channel_id=1, source_target_pairs={{0,1},{1,0},{2,3},{3,2},{4,5},{5,4},{6,7},{7,6},{8,9},{9,8},{10,11... | collective-permute-start | bytes 356360 | tf_op jit(solution)/shard_map/ppermute | solution.py:656
  11.9 5.2 %collective-permute-done.refs_1_ = bf16[58,16,128]{2,1,0:T(8,128)(2,1)S(1)} collective-permute-done((bf16[58,16,128]{2,1,0:T(8,128)(2,1)S(1)}, bf16[58,16,128]{2,1,0:T(8,128)(2,1)S(1)}, u32[]{:S(2)}, u32[]{:S(2)}) %collective-permute-start) | collective-permute-done | bytes 237600 | tf_op jit(solution)/shard_map/ppermute | solution.py:656
  17.1 0.1 collective-permute-start.5
  17.2 0.0 collective-permute-done.1.refs_2_
  17.2 3.0 %collective-permute-start.6 = (bf16[29,16,128]{2,1,0:T(8,128)(2,1)S(1)}, bf16[29,16,128]{2,1,0:T(8,128)(2,1)S(1)}, u32[]{:S(2)}, u32[]{:S(2)}) collective-permute-start(bf16[29,16,128]{2,1,0:T(8,128)(2,1)S(1)} %get-tuple-element.37), channel_id=1, source_target_pairs={{0,7},{1,6},{2,5},{3,4},{4,3},{5,2},{6,1},{7,0},{8,15},{9,14},{10,... | collective-permute-start | bytes 356360 | tf_op jit(solution)/shard_map/ppermute | solution.py:656
  20.2 0.0 copy-done.4
  20.2 3.3 %scan.1.codes = s32[129]{0:T(256)S(1)} custom-call(s32[16,1,32]{2,1,0:T(1,128)S(1)} %bitcast.25), custom_call_target="tpu_custom_call" | custom-call | flops 20000000 | bytes 1048576 | tf_op jit(solution)/shard_map/scan/pallas_call | solution.py:630
  23.5 0.0 copy-done.3
  23.5 0.0 copy-done.2
  23.5 0.0 copy-done.1
  23.5 3.0 %slots.1 = (f32[17,16,256]{2,1,0:T(8,128)S(1)}, f32[40,256]{1,0:T(8,128)S(1)}, f32[3,128,128]{2,1,0:T(8,128)S(1)}, s32[3,128]{1,0:T(4,128)S(4)}) custom-call(f32[2,32]{1,0:T(2,128)S(1)} %bitcast.16, f32[2,32]{1,0:T(2,128)S(1)} %bitcast.19, s32[2,32]{1,0:T(2,128)S(1)} %bitcast.22, s32[129]{0:T(256)S(1)} %scan.1.codes), custom_call_target="tpu_custom_call" | custom-call | flops 20000000 | bytes 1048576 | tf_op jit(solution)/shard_map/slots/pallas_call | solution.py:640
  26.5 0.0 collective-permute-done.2.refs_3_
  26.5 0.0 collective-permute-done.3.refs_4_
  26.5 0.0 collective-permute-done.4.refs_5_
  26.5 0.0 collective-permute-done.5.refs_6_
  26.5 1.2 %first_blend.1 = (f32[17,16,256]{2,1,0:T(8,128)S(1)}, bf16[16,16,256]{2,1,0:T(8,128)(2,1)S(1)}, bf16[16,16,256]{2,1,0:T(8,128)(2,1)S(1)}, bf16[16,16,256]{2,1,0:...) custom-call(s32[3,128]{1,0:T(4,128)S(4)} %get-tuple-element.27.slot_, ...), custom_call_target="tpu_custom_call" | custom-call | flops 1000000 | bytes 2097152 | tf_op jit(solution)/shard_map/first_blend/pallas_call | solution.py:678
  27.7 0.0 collective-permute-done.6.refs_0_
  27.7 0.3 last_blend.1
  27.9 2.4 %collective-permute-start.7 = (bf16[16,16,256]{2,1,0:T(8,128)(2,1)S(1)}, bf16[16,16,256]{2,1,0:T(8,128)(2,1)S(1)}, u32[]{:S(2)}, u32[]{:S(2)}) collective-permute-start(bf16[16,16,256]{2,1,0:T(8,128)(2,1)S(1)} %get-tuple-element.38.grid), channel_id=1, source_target_pairs={{0,24},{8,0},{16,8},{24,16},{1,25},{9,1},{17,9},{25,17},{2,26},{10... | collective-permute-start | bytes 393224 | tf_op jit(solution)/shard_map/ppermute | solution.py:706
  30.4 0.4 weights.1
  30.8 1.9 %moments.1.base = f32[4,128]{1,0:T(4,128)S(1)} custom-call(f32[2,32]{1,0:T(2,128)S(1)} %bitcast.17, f32[2,32]{1,0:T(2,128)S(1)} %bitcast.20, s32[2,32]{1,0:T(2,128)S(1)} %bitcast.23, bf16[64,16,256]{2,1,0:T(8,128)(2,1)S(1)} %get-tuple-element.42.frames), custom_call_target="tpu_custom_call" | custom-call | flops 20000000 | bytes 1048576 | tf_op jit(solution)/shard_map/moments/pallas_call | solution.py:619
  32.7 0.2 collective-permute-done.7.from_next
  33.0 0.0 copy-done
  33.0 1.2 %gradient.1 = (f32[32,4,128]{2,1,0:T(4,128)S(1)}, bf16[16,16,256]{2,1,0:T(8,128)(2,1)}, f32[8,264,128]{2,1,0:T(8,128)S(1)}) custom-call(s32[3,128]{1,0:T(4,128)S(4)} %get-tuple-element.27.slot_bands, bf16[16,16,256]{2,1,0:T(8,128)(2,1)S(1)} %collective-permute-done.7.from_next, bf16[16,16,256]{2,1,0:T(8,128)(2,1)S(1)} %bitcast.14, ...), custom_call_target="tpu_custom_call", output_to_operand_aliasing={{2}: (5, {})} | custom-call | flops 8000000 | bytes 2097152 | tf_op jit(solution)/shard_map/gradient/pallas_call | solution.py:719
  34.2 14.6 %all_to_all.5.received = f32[32,4,128]{2,1,0:T(4,128)S(1)} all-to-all(f32[32,4,128]{2,1,0:T(4,128)S(1)} %get-tuple-element.51), channel_id=1, replica_groups=mesh['sec'=4,'tile'=8] {'sec','tile'}, dimensions={0} | all-to-all | bytes 131072 | tf_op jit(solution)/shard_map/all_to_all | solution.py:748
  48.8 1.3 %solve.1 = f32[4,6]{1,0:T(4,128)} custom-call(f32[32,4,128]{2,1,0:T(4,128)S(1)} %all_to_all.5.received), custom_call_target="tpu_custom_call" | custom-call | flops 100000 | bytes 262144 | tf_op jit(solution)/shard_map/solve/pallas_call | solution.py:752
  (1 shorter events, 0.0 us)
Async XLA Ops:
  0.6 19.6 %copy-start.4 = (s32[1,32,16,1]{1,3,2,0:T(1,128)S(1)}, s32[1,32,16,1]{1,3,2,0:T(1,128)}, u32[]{:S(2)}) copy-start(s32[1,32,16,1]{1,3,2,0:T(1,128)} %param.10) | copy-start | bytes 6148
  0.6 22.8 %copy-start.3 = (s32[1,2,32]{2,1,0:T(2,128)S(1)}, s32[1,2,32]{2,1,0:T(2,128)}, u32[]{:S(2)}) copy-start(s32[1,2,32]{2,1,0:T(2,128)} %param.9) | copy-start | bytes 772
  0.7 22.8 %copy-start.2 = (f32[1,2,32]{2,1,0:T(2,128)S(1)}, f32[1,2,32]{2,1,0:T(2,128)}, u32[]{:S(2)}) copy-start(f32[1,2,32]{2,1,0:T(2,128)} %param.8) | copy-start | bytes 772
  0.7 22.8 %copy-start.1 = (f32[1,2,32]{2,1,0:T(2,128)S(1)}, f32[1,2,32]{2,1,0:T(2,128)}, u32[]{:S(2)}) copy-start(f32[1,2,32]{2,1,0:T(2,128)} %param.7) | copy-start | bytes 772
  3.6 29.4 %copy-start = (bf16[1,256,256]{2,1,0:T(8,128)(2,1)S(1)}, bf16[1,256,256]{2,1,0:T(8,128)(2,1)}, u32[]{:S(2)}) copy-start(bf16[1,256,256]{2,1,0:T(8,128)(2,1)} %param.11) | copy-start | bytes 393220
  3.6 13.5 %collective-permute-start = (bf16[58,16,128]{2,1,0:T(8,128)(2,1)S(1)}, bf16[58,16,128]{2,1,0:T(8,128)(2,1)S(1)}, u32[]{:S(2)}, u32[]{:S(2)}) collective-permute-start(bf16[58,16,128]{2,1,0:T(8,128)(2,1)S(1)} %get-tuple-element.31), channel_id=1, source_target_pairs={{0,2},{1,3},{2,0},{3,1},{4,6},{5,7},{6,4},{7,5},{8,10},{9,11},{10,... | collective-permute-start | bytes 712712 | tf_op jit(solution)/shard_map/ppermute | solution.py:656
  6.7 10.5 %collective-permute-start.1 = (bf16[29,16,128]{2,1,0:T(8,128)(2,1)S(1)}, bf16[29,16,128]{2,1,0:T(8,128)(2,1)S(1)}, u32[]{:S(2)}, u32[]{:S(2)}) collective-permute-start(bf16[29,16,128]{2,1,0:T(8,128)(2,1)S(1)} %get-tuple-element.32), channel_id=1, source_target_pairs={{0,4},{1,5},{2,6},{3,7},{4,0},{5,1},{6,2},{7,3},{8,12},{9,13},{10,... | collective-permute-start | bytes 356360 | tf_op jit(solution)/shard_map/ppermute | solution.py:656
  9.3 17.2 %collective-permute-start.2 = (bf16[29,16,128]{2,1,0:T(8,128)(2,1)S(1)}, bf16[29,16,128]{2,1,0:T(8,128)(2,1)S(1)}, u32[]{:S(2)}, u32[]{:S(2)}) collective-permute-start(bf16[29,16,128]{2,1,0:T(8,128)(2,1)S(1)} %get-tuple-element.33), channel_id=1, source_target_pairs={{0,5},{1,4},{2,7},{3,6},{4,1},{5,0},{6,3},{7,2},{8,13},{9,12},{10,... | collective-permute-start | bytes 356360 | tf_op jit(solution)/shard_map/ppermute | solution.py:656
  9.3 17.2 %collective-permute-start.3 = (bf16[29,16,128]{2,1,0:T(8,128)(2,1)S(1)}, bf16[29,16,128]{2,1,0:T(8,128)(2,1)S(1)}, u32[]{:S(2)}, u32[]{:S(2)}) collective-permute-start(bf16[29,16,128]{2,1,0:T(8,128)(2,1)S(1)} %get-tuple-element.34), channel_id=1, source_target_pairs={{0,6},{1,7},{2,4},{3,5},{4,2},{5,3},{6,0},{7,1},{8,14},{9,15},{10,... | collective-permute-start | bytes 356360 | tf_op jit(solution)/shard_map/ppermute | solution.py:656
  11.0 15.5 %collective-permute-start.4 = (bf16[29,16,128]{2,1,0:T(8,128)(2,1)S(1)}, bf16[29,16,128]{2,1,0:T(8,128)(2,1)S(1)}, u32[]{:S(2)}, u32[]{:S(2)}) collective-permute-start(bf16[29,16,128]{2,1,0:T(8,128)(2,1)S(1)} %get-tuple-element.35), channel_id=1, source_target_pairs={{0,1},{1,0},{2,3},{3,2},{4,5},{5,4},{6,7},{7,6},{8,9},{9,8},{10,11... | collective-permute-start | bytes 356360 | tf_op jit(solution)/shard_map/ppermute | solution.py:656
  17.1 9.4 %collective-permute-start.5 = (bf16[29,16,128]{2,1,0:T(8,128)(2,1)S(1)}, bf16[29,16,128]{2,1,0:T(8,128)(2,1)S(1)}, u32[]{:S(2)}, u32[]{:S(2)}) collective-permute-start(bf16[29,16,128]{2,1,0:T(8,128)(2,1)S(1)} %slice.4), channel_id=1, source_target_pairs={{0,1},{1,0},{2,3},{3,2},{4,5},{5,4},{6,7},{7,6},{8,9},{9,8},{10,11... | collective-permute-start | bytes 356360 | tf_op jit(solution)/shard_map/ppermute | solution.py:656
  17.2 10.5 %collective-permute-start.6 = (bf16[29,16,128]{2,1,0:T(8,128)(2,1)S(1)}, bf16[29,16,128]{2,1,0:T(8,128)(2,1)S(1)}, u32[]{:S(2)}, u32[]{:S(2)}) collective-permute-start(bf16[29,16,128]{2,1,0:T(8,128)(2,1)S(1)} %get-tuple-element.37), channel_id=1, source_target_pairs={{0,7},{1,6},{2,5},{3,4},{4,3},{5,2},{6,1},{7,0},{8,15},{9,14},{10,... | collective-permute-start | bytes 356360 | tf_op jit(solution)/shard_map/ppermute | solution.py:656
  27.9 5.0 %collective-permute-start.7 = (bf16[16,16,256]{2,1,0:T(8,128)(2,1)S(1)}, bf16[16,16,256]{2,1,0:T(8,128)(2,1)S(1)}, u32[]{:S(2)}, u32[]{:S(2)}) collective-permute-start(bf16[16,16,256]{2,1,0:T(8,128)(2,1)S(1)} %get-tuple-element.38.grid), channel_id=1, source_target_pairs={{0,24},{8,0},{16,8},{24,16},{1,25},{9,1},{17,9},{25,17},{2,26},{10... | collective-permute-start | bytes 393224 | tf_op jit(solution)/shard_map/ppermute | solution.py:706

commit v10 on v9

--- a/solution.py
+++ b/solution.py
@@ -357,16 +357,19 @@
 
 
 def last_blend_kernel(sizes, chosen, slot_bands, col_cover, cover_sum, before, *refs):
-    bands = sizes[1]
-    blocks, (grid, *whole, total) = refs[: len(chosen)], refs[len(chosen) :]
+    bands, frame = sizes[1], sizes[2]
+    blocks, (left, right, *whole, total) = refs[: len(chosen)], refs[len(chosen) :]
     total[...] = before[...]
     add_blocks(sizes, chosen, slot_bands, col_cover, blocks, whole, total)
-    grid[...] = (total[:bands] / (1.0 + cover_sum[:bands])).astype(jnp.bfloat16)
-
-
-def weight_kernel(sizes, slot_lines, weights, sums):
+    grid = (total[:bands] / (1.0 + cover_sum[:bands])).astype(jnp.bfloat16)
+    left[...] = grid[:, :, : frame // 2]
+    right[...] = grid[:, :, frame // 2 :]
+
+
+def weight_kernel(sizes, slot_lines, weights, *sums):
     tiles, bands, frame, source, capacity, devices = sizes
-    sums[...] = jnp.zeros_like(sums)
+    for ref in sums:
+        ref[...] = jnp.zeros_like(ref)
     spots = spots_along((BAND, LANES), 0)
     raised = spots * (2.0 / frame)
 
@@ -383,46 +386,31 @@
 GRADIENT_ROWS = ({0: 0, 1: 1}, {2: 0}, {3: 0, 4: 1}, {5: 0})
 
 
-def gradient_kernel(
-    sizes, slot_bands, from_next, top_grid, col_cover, weights, _, base, grid, *blocks_and_rest
-):
+def add_gradients(sizes, half, slot_bands, from_next, top_grid, weights, blocks, sums, above):
     tiles, bands, frame, source, capacity, devices = sizes
-    *blocks, payload, grid_out, sums, above, grid_sem = blocks_and_rest
-    written = pltpu.make_async_copy(grid, grid_out, grid_sem)
-    written.start()
-    sec = lax.axis_index("sec")
-    all_tiles = tiles * devices
-
-    @pl.when(sec == lax.axis_size("sec") - 1)
+    part = slice(half * LANES, (half + 1) * LANES)
+    at_top = lax.axis_index("sec") == lax.axis_size("sec") - 1
+
+    @pl.when(at_top)
     def _():
-        above[:bands] = top_grid[...].astype(jnp.float32)
-
-    @pl.when(sec != lax.axis_size("sec") - 1)
+        above[:bands] = top_grid[:, :, part].astype(jnp.float32)
+
+    @pl.when(jnp.logical_not(at_top))
     def _():
         above[:bands] = from_next[...].astype(jnp.float32)
 
-    above[bands] = jnp.zeros((BAND, frame), jnp.float32)
-    halves = range(frame // LANES)
+    above[bands] = jnp.zeros((BAND, LANES), jnp.float32)
 
     for block, (array, _) in enumerate(exchange_plan(devices)[1]):
         running = None
         for k in range(capacity):
             slot = block * capacity + k
             cover, lifted = weights[0, slot], weights[1, slot]
-            level = blocks[array][k].astype(jnp.float32)
+            level = blocks[array][k, :, part].astype(jnp.float32)
             error = above[slot_bands[0, slot]] - level
             product = error * level
-            terms = []
-            for half in halves:
-                part = slice(half * LANES, (half + 1) * LANES)
-                for weight, value in (
-                    (cover, error),
-                    (lifted, error),
-                    (cover, product),
-                    (lifted, product),
-                ):
-                    term = weight * value[:, part]
-                    terms.append(term[:ROWS] + term[ROWS:])
+            terms = [cover * error, lifted * error, cover * product, lifted * product]
+            terms = [term[:ROWS] + term[ROWS:] for term in terms]
             if running is not None:
                 same = slot_bands[2, slot] == 1
                 terms = [
@@ -430,18 +418,52 @@
                 ]
             running = terms
             rows = pl.ds(pl.multiple_of(slot_bands[1, slot] * ROWS, ROWS), ROWS)
-            for index, term in enumerate(terms):
-                sums[index, rows, :] = term
+            for kind, term in enumerate(terms):
+                sums[kind, rows, :] = term
+
+
+def left_gradient_kernel(sizes, slot_bands, from_next, top_grid, weights, _, *refs):
+    *blocks, sums, above = refs
+    add_gradients(sizes, 0, slot_bands, from_next, top_grid, weights, blocks, sums, above)
+
+
+def gradient_kernel(
+    sizes,
+    slot_bands,
+    from_next,
+    top_grid,
+    weights,
+    _,
+    left_sums,
+    col_cover,
+    base,
+    left_grid,
+    right_grid,
+    *refs,
+):
+    tiles, bands, frame, source, capacity, devices = sizes
+    *blocks, payload, grid_out, sums, above, grid_sems = refs
+    halves = range(frame // LANES)
+    written = [
+        pltpu.make_async_copy(
+            grid, grid_out.at[:, :, pl.ds(half * LANES, LANES)], grid_sems.at[half]
+        )
+        for half, grid in enumerate((left_grid, right_grid))
+    ]
+    for copy in written:
+        copy.start()
+    all_tiles = tiles * devices
+    add_gradients(sizes, 1, slot_bands, from_next, top_grid, weights, blocks, sums, above)
 
     values = [jnp.zeros((all_tiles, 1), jnp.float32)] * 6
     for half in halves:
         columns = col_cover[:all_tiles, half * LANES : (half + 1) * LANES]
         x = coords(spots_along((all_tiles, LANES), 1, half * LANES), frame)
         for kind, wanted in enumerate(GRADIENT_ROWS):
-            index = half * len(GRADIENT_ROWS) + kind
-            value = sums[index, pl.ds(0, all_tiles, stride=ROWS), :]
+            ref = (left_sums, sums)[half]
+            value = ref[kind, pl.ds(0, all_tiles, stride=ROWS), :]
             for r in range(1, ROWS):
-                value += sums[index, pl.ds(r, all_tiles, stride=ROWS), :]
+                value += ref[kind, pl.ds(r, all_tiles, stride=ROWS), :]
             value = value * columns
             for row, power in wanted.items():
                 term = value * x if power else value
@@ -458,7 +480,8 @@
         total.append(jnp.concatenate(rows + [jnp.zeros_like(rows[0])], axis=0))
     total = base[...] + jnp.concatenate(total, axis=1)
     payload[...] = jnp.broadcast_to(total[None], payload.shape)
-    written.wait()
+    for copy in written:
+        copy.wait()
 
 
 def solve_kernel(sizes, received, corrections):
@@ -675,73 +698,87 @@
             if is_packed(capacity, devices, distance)
         ]
         whole = jax.ShapeDtypeStruct((capacity, BAND, frame), jnp.bfloat16)
-        result, *unpacked = pl.pallas_call(
+        found = pl.pallas_call(
             functools.partial(kernel, sizes, distances),
             name=name,
             in_specs=[SMEM] + [VMEM] * (len(operands) + len(chosen)),
-            out_specs=[VMEM] * (1 + len(packed)),
-            out_shape=[results] + [whole] * len(packed),
+            out_specs=[VMEM] * (len(results) + len(packed)),
+            out_shape=results + [whole] * len(packed),
             scratch_shapes=scratch,
             compiler_params=params(24),
             cost_estimate=cost(1_000_000, 2 << 20),
         )(slot_bands, *operands, *(incoming[array] for array in arrays))
-        for array, block in zip(packed, unpacked):
+        for array, block in zip(packed, found[len(results) :]):
             incoming[array] = block
-        return result
+        return found[: len(results)]
 
     last = [5] if devices == 8 else range(devices - devices // 4, devices)
     early = [block for block in range(devices) if block not in last]
-    before = blend(first_blend_kernel, "first_blend", early, total, [], col_cover)
-    grid = blend(
+    (before,) = blend(first_blend_kernel, "first_blend", early, [total], [], col_cover)
+    half = jax.ShapeDtypeStruct((bands, BAND, frame // 2), jnp.bfloat16)
+    grids = blend(
         last_blend_kernel,
         "last_blend",
         last,
-        jax.ShapeDtypeStruct((bands, BAND, frame), jnp.bfloat16),
+        [half, half],
         [pltpu.VMEM(total.shape, total.dtype)],
         col_cover,
         cover_sum,
         before,
     )
 
-    from_next = lax.ppermute(grid, "sec", [(i, (i - 1) % sections) for i in range(sections)])
-
-    sums = jax.ShapeDtypeStruct((4 * frame // LANES, (all_tiles + 1) * ROWS, LANES), jnp.float32)
-    weights, zeros = pl.pallas_call(
+    ring = [(i, (i - 1) % sections) for i in range(sections)]
+    from_next = [lax.ppermute(grid, "sec", ring) for grid in grids]
+
+    sums = jax.ShapeDtypeStruct((4, (all_tiles + 1) * ROWS, LANES), jnp.float32)
+    weights, *zeros = pl.pallas_call(
         functools.partial(weight_kernel, sizes),
         name="weights",
         in_specs=[VMEM],
-        out_specs=[VMEM] * 2,
-        out_shape=[jax.ShapeDtypeStruct((2, slots, BAND, LANES), jnp.float32), sums],
+        out_specs=[VMEM] * 3,
+        out_shape=[jax.ShapeDtypeStruct((2, slots, BAND, LANES), jnp.float32), sums, sums],
         compiler_params=params(24),
         cost_estimate=cost(1_000_000, 1 << 20),
     )(slot_lines)
 
+    top_bands = top_grid.reshape(bands, BAND, frame)
+    above = pltpu.VMEM((bands + 1, BAND, LANES), jnp.float32)
+    left_sums = pl.pallas_call(
+        functools.partial(left_gradient_kernel, sizes),
+        name="left_gradient",
+        in_specs=[SMEM] + [VMEM] * (4 + len(incoming)),
+        out_specs=VMEM,
+        out_shape=sums,
+        scratch_shapes=[above],
+        input_output_aliases={4: 0},
+        compiler_params=params(24),
+        cost_estimate=cost(8_000_000, 2 << 20),
+    )(slot_bands, from_next[0], top_bands, weights, zeros[0], *incoming)
+
     payload, grid_out, _ = pl.pallas_call(
         functools.partial(gradient_kernel, sizes),
         name="gradient",
-        in_specs=[SMEM] + [VMEM] * (7 + len(incoming)),
+        in_specs=[SMEM] + [VMEM] * (9 + len(incoming)),
         out_specs=[VMEM, HBM, VMEM],
         out_shape=[
             jax.ShapeDtypeStruct((sections * devices, PAYLOAD_ROWS, width), jnp.float32),
             jax.ShapeDtypeStruct((bands, BAND, frame), jnp.bfloat16),
             sums,
         ],
-        scratch_shapes=[
-            pltpu.VMEM((bands + 1, BAND, frame), jnp.float32),
-            pltpu.SemaphoreType.DMA,
-        ],
-        input_output_aliases={5: 2},
+        scratch_shapes=[above, pltpu.SemaphoreType.DMA((2,))],
+        input_output_aliases={4: 2},
         compiler_params=params(24),
         cost_estimate=cost(8_000_000, 2 << 20),
     )(
         slot_bands,
-        from_next,
-        top_grid.reshape(bands, BAND, frame),
+        from_next[1],
+        top_bands,
+        weights,
+        zeros[1],
+        left_sums,
         col_cover,
-        weights,
-        zeros,
         base,
-        grid,
+        *grids,
         *incoming,
     )
 

time: 50.3 us -> 49.8 us (0.990)
  blocking collectives: 14.6 us -> 13 us
  waiting for transfers between devices: 5.45 us -> 6.17 us
  starting transfers between devices: 13.8 us -> 14.5 us
    all_to_all x1, blocking collectives: 14.6 us -> 13 us  [shards(): lax.all_to_all(payload, ('sec', 'tile'), split_axis=0, concat_axis=0, til...]
    ppermute x1 -> x2, waiting for transfers between devices: 0.25 us -> 0.96 us  [shards(): from_next = [lax.ppermute(grid, 'sec', ring) for grid in grids]]
    ppermute x1 -> x2, starting transfers between devices: 2.44 us -> 3.12 us  [shards(): from_next = [lax.ppermute(grid, 'sec', ring) for grid in grids]]
    pallas_call x0 -> x1, Pallas kernels: none -> 0.56 us  [shards(): pl.pallas_call(functools.partial(left_gradient_kernel, sizes), name='left...]
  transfers between devices with their start and end apart: 8 -> 9, of which waited for: 2 -> 2; matrix products, arithmetic and copies ran while one was open for 0% -> 0% of each run, Pallas kernels for 19% -> 20%
where the time goes in v10:
time: 49.8 us; the launch traced here: 49.7 us
  Pallas kernels  15.1 us (30%)
  starting transfers between devices  14.5 us (29%)
  blocking collectives  13 us (26%)
  waiting for transfers between devices  6.17 us (12%)
  between operations  0.83 us (2%)
    all_to_all x1, blocking collectives, shards(): lax.all_to_all(payload, ('sec', 'tile'), split_axis=0, concat_axis=0, til...  13 us
    ppermute x7, starting transfers between devices, swapped(): lax.ppermute(block, 'tile', [(i, i ^ distance) for i in range(devices)])  11.4 us
    ppermute x7, waiting for transfers between devices, swapped(): lax.ppermute(block, 'tile', [(i, i ^ distance) for i in range(devices)])  5.21 us
    ppermute x2, starting transfers between devices, shards(): from_next = [lax.ppermute(grid, 'sec', ring) for grid in grids]  3.12 us
    pallas_call x1, Pallas kernels, shards(): pl.pallas_call(functools.partial(slot_kernel, sizes), name='slots', in_sp...  2.96 us
    pallas_call x1, Pallas kernels, shards(): pl.pallas_call(functools.partial(scan_kernel, sizes), name='scan', in_spe...  2.9 us
    pallas_call x1, Pallas kernels, shards(): pl.pallas_call(functools.partial(render_kernel, sizes), name='render', in...  2.89 us
    pallas_call x1, Pallas kernels, shards(): pl.pallas_call(functools.partial(moment_kernel, sizes), name='moments', i...  1.9 us
  transfers between devices with their start and end apart: 9, of which 2 were waited for; matrix products, arithmetic and copies ran while one was open for 0% of the time, Pallas kernels for 20%

profile of v10, /device:TPU:0, one launch (start us, length us, event | category | flops | bytes accessed | tf_op | source)
XLA Modules:
  0.0 49.7 jit_solution(939398614725389570)
XLA Ops:
  0.6 0.0 copy-start.4
  0.6 0.0 copy-start.3
  0.7 0.0 copy-start.2
  0.7 0.0 copy-start.1
  0.7 2.9 %render.1 = (bf16[64,16,256]{2,1,0:T(8,128)(2,1)S(1)}, bf16[16,16,256]{2,1,0:T(8,128)(2,1)S(1)}, bf16[58,16,128]{2,1,0:T(8,128)(2,1)S(1)}, bf16[29,16,128]{2,1,0...) custom-call(f32[2,32]{1,0:T(2,128)} %bitcast.16, ...), custom_call_target="tpu_custom_call" | custom-call | flops 800000000 | bytes 4194304 | tf_op jit(solution)/shard_map/render/pallas_call | solution.py:621
  3.6 0.0 copy-start
  3.6 3.1 %collective-permute-start = (bf16[58,16,128]{2,1,0:T(8,128)(2,1)S(1)}, bf16[58,16,128]{2,1,0:T(8,128)(2,1)S(1)}, u32[]{:S(2)}, u32[]{:S(2)}) collective-permute-start(bf16[58,16,128]{2,1,0:T(8,128)(2,1)S(1)} %get-tuple-element.33), channel_id=1, source_target_pairs={{0,2},{1,3},{2,0},{3,1},{4,6},{5,7},{6,4},{7,5},{8,10},{9,11},{10,... | collective-permute-start | bytes 712712 | tf_op jit(solution)/shard_map/ppermute | solution.py:679
  6.7 2.6 %collective-permute-start.1 = (bf16[29,16,128]{2,1,0:T(8,128)(2,1)S(1)}, bf16[29,16,128]{2,1,0:T(8,128)(2,1)S(1)}, u32[]{:S(2)}, u32[]{:S(2)}) collective-permute-start(bf16[29,16,128]{2,1,0:T(8,128)(2,1)S(1)} %get-tuple-element.34), channel_id=1, source_target_pairs={{0,4},{1,5},{2,6},{3,7},{4,0},{5,1},{6,2},{7,3},{8,12},{9,13},{10,... | collective-permute-start | bytes 356360 | tf_op jit(solution)/shard_map/ppermute | solution.py:679
  9.3 0.0 collective-permute-start.2
  9.3 1.7 %collective-permute-start.3 = (bf16[29,16,128]{2,1,0:T(8,128)(2,1)S(1)}, bf16[29,16,128]{2,1,0:T(8,128)(2,1)S(1)}, u32[]{:S(2)}, u32[]{:S(2)}) collective-permute-start(bf16[29,16,128]{2,1,0:T(8,128)(2,1)S(1)} %get-tuple-element.36), channel_id=1, source_target_pairs={{0,6},{1,7},{2,4},{3,5},{4,2},{5,3},{6,0},{7,1},{8,14},{9,15},{10,... | collective-permute-start | bytes 356360 | tf_op jit(solution)/shard_map/ppermute | solution.py:679
  11.0 1.0 %collective-permute-start.4 = (bf16[29,16,128]{2,1,0:T(8,128)(2,1)S(1)}, bf16[29,16,128]{2,1,0:T(8,128)(2,1)S(1)}, u32[]{:S(2)}, u32[]{:S(2)}) collective-permute-start(bf16[29,16,128]{2,1,0:T(8,128)(2,1)S(1)} %get-tuple-element.37), channel_id=1, source_target_pairs={{0,1},{1,0},{2,3},{3,2},{4,5},{5,4},{6,7},{7,6},{8,9},{9,8},{10,11... | collective-permute-start | bytes 356360 | tf_op jit(solution)/shard_map/ppermute | solution.py:679
  11.9 5.2 %collective-permute-done.refs_1_ = bf16[58,16,128]{2,1,0:T(8,128)(2,1)S(1)} collective-permute-done((bf16[58,16,128]{2,1,0:T(8,128)(2,1)S(1)}, bf16[58,16,128]{2,1,0:T(8,128)(2,1)S(1)}, u32[]{:S(2)}, u32[]{:S(2)}) %collective-permute-start) | collective-permute-done | bytes 237600 | tf_op jit(solution)/shard_map/ppermute | solution.py:679
  17.1 0.1 collective-permute-start.5
  17.2 0.0 collective-permute-done.1.refs_2_
  17.2 3.0 %collective-permute-start.6 = (bf16[29,16,128]{2,1,0:T(8,128)(2,1)S(1)}, bf16[29,16,128]{2,1,0:T(8,128)(2,1)S(1)}, u32[]{:S(2)}, u32[]{:S(2)}) collective-permute-start(bf16[29,16,128]{2,1,0:T(8,128)(2,1)S(1)} %get-tuple-element.39), channel_id=1, source_target_pairs={{0,7},{1,6},{2,5},{3,4},{4,3},{5,2},{6,1},{7,0},{8,15},{9,14},{10,... | collective-permute-start | bytes 356360 | tf_op jit(solution)/shard_map/ppermute | solution.py:679
  20.2 0.0 copy-done.4
  20.2 2.9 %scan.1.codes = s32[129]{0:T(256)S(1)} custom-call(s32[16,1,32]{2,1,0:T(1,128)S(1)} %bitcast.26), custom_call_target="tpu_custom_call" | custom-call | flops 20000000 | bytes 1048576 | tf_op jit(solution)/shard_map/scan/pallas_call | solution.py:653
  23.1 0.0 copy-done.3
  23.1 0.0 copy-done.2
  23.1 0.0 copy-done.1
  23.1 3.0 %slots.1 = (f32[17,16,256]{2,1,0:T(8,128)S(1)}, f32[40,256]{1,0:T(8,128)S(1)}, f32[3,128,128]{2,1,0:T(8,128)S(1)}, s32[3,128]{1,0:T(4,128)S(4)}) custom-call(f32[2,32]{1,0:T(2,128)S(1)} %bitcast.17, f32[2,32]{1,0:T(2,128)S(1)} %bitcast.20, s32[2,32]{1,0:T(2,128)S(1)} %bitcast.23, s32[129]{0:T(256)S(1)} %scan.1.codes), custom_call_target="tpu_custom_call" | custom-call | flops 20000000 | bytes 1048576 | tf_op jit(solution)/shard_map/slots/pallas_call | solution.py:663
  26.1 0.0 collective-permute-done.2.refs_3_
  26.1 0.0 collective-permute-done.3.refs_4_
  26.1 0.0 collective-permute-done.4.refs_5_
  26.1 0.0 collective-permute-done.5.refs_6_
  26.1 1.2 %first_blend.1 = (f32[17,16,256]{2,1,0:T(8,128)S(1)}, bf16[16,16,256]{2,1,0:T(8,128)(2,1)S(1)}, bf16[16,16,256]{2,1,0:T(8,128)(2,1)S(1)}, bf16[16,16,256]{2,1,0:...) custom-call(s32[3,128]{1,0:T(4,128)S(4)} %get-tuple-element.29.slot_, ...), custom_call_target="tpu_custom_call" | custom-call | flops 1000000 | bytes 2097152 | tf_op jit(solution)/shard_map/first_blend/pallas_call | solution.py:701
  27.3 0.0 collective-permute-done.6.refs_0_
  27.3 0.2 last_blend.1
  27.5 2.6 %collective-permute-start.8 = (bf16[16,16,128]{2,1,0:T(8,128)(2,1)S(1)}, bf16[16,16,128]{2,1,0:T(8,128)(2,1)S(1)}, u32[]{:S(2)}, u32[]{:S(2)}) collective-permute-start(bf16[16,16,128]{2,1,0:T(8,128)(2,1)S(1)} %get-tuple-element.44.left_grid), channel_id=1, source_target_pairs={{0,24},{8,0},{16,8},{24,16},{1,25},{9,1},{17,9},{25,17},{2,26},{10... | collective-permute-start | bytes 196616 | tf_op jit(solution)/shard_map/ppermute | solution.py:731
  30.1 0.6 %collective-permute-start.7 = (bf16[16,16,128]{2,1,0:T(8,128)(2,1)S(1)}, bf16[16,16,128]{2,1,0:T(8,128)(2,1)S(1)}, u32[]{:S(2)}, u32[]{:S(2)}) collective-permute-start(bf16[16,16,128]{2,1,0:T(8,128)(2,1)S(1)} %get-tuple-element.40.right_grid), channel_id=1, source_target_pairs={{0,24},{8,0},{16,8},{24,16},{1,25},{9,1},{17,9},{25,17},{2,26},{10... | collective-permute-start | bytes 196616 | tf_op jit(solution)/shard_map/ppermute | solution.py:731
  30.7 0.4 weights.1
  31.1 1.9 %moments.1.base = f32[4,128]{1,0:T(4,128)S(1)} custom-call(f32[2,32]{1,0:T(2,128)S(1)} %bitcast.18, f32[2,32]{1,0:T(2,128)S(1)} %bitcast.21, s32[2,32]{1,0:T(2,128)S(1)} %bitcast.24, bf16[64,16,256]{2,1,0:T(8,128)(2,1)S(1)} %get-tuple-element.53.frames), custom_call_target="tpu_custom_call" | custom-call | flops 20000000 | bytes 1048576 | tf_op jit(solution)/shard_map/moments/pallas_call | solution.py:642
  33.0 0.0 collective-permute-done.8.from_next
  33.0 0.0 copy-done
  33.0 0.6 %left_gradient.1.left_sums = f32[4,264,128]{2,1,0:T(8,128)S(1)} custom-call(s32[3,128]{1,0:T(4,128)S(4)} %get-tuple-element.29.slot_bands, bf16[16,16,128]{2,1,0:T(8,128)(2,1)S(1)} %collective-permute-done.8.from_next, bf16[16,16,256]{2,1,0:T(8,128)(2,1)S(1)} %bitcast.14, ...), custom_call_target="tpu_custom_call", output_to_operand_aliasing={{}: (4, {})} | custom-call | flops 8000000 | bytes 2097152 | tf_op jit(solution)/shard_map/left_gradient/pallas_call | solution.py:746
  33.6 1.0 %collective-permute-done.7.from_next = bf16[16,16,128]{2,1,0:T(8,128)(2,1)S(1)} collective-permute-done((bf16[16,16,128]{2,1,0:T(8,128)(2,1)S(1)}, bf16[16,16,128]{2,1,0:T(8,128)(2,1)S(1)}, u32[]{:S(2)}, u32[]{:S(2)}) %collective-permute-start.7) | collective-permute-done | bytes 65568 | tf_op jit(solution)/shard_map/ppermute | solution.py:731
  34.6 0.8 %gradient.1 = (f32[32,4,128]{2,1,0:T(4,128)S(1)}, bf16[16,16,256]{2,1,0:T(8,128)(2,1)}, f32[4,264,128]{2,1,0:T(8,128)S(1)}) custom-call(s32[3,128]{1,0:T(4,128)S(4)} %get-tuple-element.29.slot_bands, bf16[16,16,128]{2,1,0:T(8,128)(2,1)S(1)} %collective-permute-done.7.from_next, bf16[16,16,256]{2,1,0:T(8,128)(2,1)S(1)} %bitcast.15, ...), custom_call_target="tpu_custom_call", output_to_operand_aliasing={{2}: (4, {})} | custom-call | flops 8000000 | bytes 2097152 | tf_op jit(solution)/shard_map/gradient/pallas_call | solution.py:758
  35.3 13.0 %all_to_all.5.received = f32[32,4,128]{2,1,0:T(4,128)S(1)} all-to-all(f32[32,4,128]{2,1,0:T(4,128)S(1)} %get-tuple-element.55), channel_id=1, replica_groups=mesh['sec'=4,'tile'=8] {'sec','tile'}, dimensions={0} | all-to-all | bytes 131072 | tf_op jit(solution)/shard_map/all_to_all | solution.py:785
  48.3 1.3 %solve.1 = f32[4,6]{1,0:T(4,128)} custom-call(f32[32,4,128]{2,1,0:T(4,128)S(1)} %all_to_all.5.received), custom_call_target="tpu_custom_call" | custom-call | flops 100000 | bytes 262144 | tf_op jit(solution)/shard_map/solve/pallas_call | solution.py:789
  (1 shorter events, 0.0 us)
Async XLA Ops:
  0.6 19.6 %copy-start.4 = (s32[1,32,16,1]{1,3,2,0:T(1,128)S(1)}, s32[1,32,16,1]{1,3,2,0:T(1,128)}, u32[]{:S(2)}) copy-start(s32[1,32,16,1]{1,3,2,0:T(1,128)} %param.10) | copy-start | bytes 6148
  0.6 22.5 %copy-start.3 = (s32[1,2,32]{2,1,0:T(2,128)S(1)}, s32[1,2,32]{2,1,0:T(2,128)}, u32[]{:S(2)}) copy-start(s32[1,2,32]{2,1,0:T(2,128)} %param.9) | copy-start | bytes 772
  0.7 22.5 %copy-start.2 = (f32[1,2,32]{2,1,0:T(2,128)S(1)}, f32[1,2,32]{2,1,0:T(2,128)}, u32[]{:S(2)}) copy-start(f32[1,2,32]{2,1,0:T(2,128)} %param.8) | copy-start | bytes 772
  0.7 22.5 %copy-start.1 = (f32[1,2,32]{2,1,0:T(2,128)S(1)}, f32[1,2,32]{2,1,0:T(2,128)}, u32[]{:S(2)}) copy-start(f32[1,2,32]{2,1,0:T(2,128)} %param.7) | copy-start | bytes 772
  3.6 29.4 %copy-start = (bf16[1,256,256]{2,1,0:T(8,128)(2,1)S(1)}, bf16[1,256,256]{2,1,0:T(8,128)(2,1)}, u32[]{:S(2)}) copy-start(bf16[1,256,256]{2,1,0:T(8,128)(2,1)} %param.11) | copy-start | bytes 393220
  3.6 13.5 %collective-permute-start = (bf16[58,16,128]{2,1,0:T(8,128)(2,1)S(1)}, bf16[58,16,128]{2,1,0:T(8,128)(2,1)S(1)}, u32[]{:S(2)}, u32[]{:S(2)}) collective-permute-start(bf16[58,16,128]{2,1,0:T(8,128)(2,1)S(1)} %get-tuple-element.33), channel_id=1, source_target_pairs={{0,2},{1,3},{2,0},{3,1},{4,6},{5,7},{6,4},{7,5},{8,10},{9,11},{10,... | collective-permute-start | bytes 712712 | tf_op jit(solution)/shard_map/ppermute | solution.py:679
  6.7 10.5 %collective-permute-start.1 = (bf16[29,16,128]{2,1,0:T(8,128)(2,1)S(1)}, bf16[29,16,128]{2,1,0:T(8,128)(2,1)S(1)}, u32[]{:S(2)}, u32[]{:S(2)}) collective-permute-start(bf16[29,16,128]{2,1,0:T(8,128)(2,1)S(1)} %get-tuple-element.34), channel_id=1, source_target_pairs={{0,4},{1,5},{2,6},{3,7},{4,0},{5,1},{6,2},{7,3},{8,12},{9,13},{10,... | collective-permute-start | bytes 356360 | tf_op jit(solution)/shard_map/ppermute | solution.py:679
  9.3 16.8 %collective-permute-start.2 = (bf16[29,16,128]{2,1,0:T(8,128)(2,1)S(1)}, bf16[29,16,128]{2,1,0:T(8,128)(2,1)S(1)}, u32[]{:S(2)}, u32[]{:S(2)}) collective-permute-start(bf16[29,16,128]{2,1,0:T(8,128)(2,1)S(1)} %get-tuple-element.35), channel_id=1, source_target_pairs={{0,5},{1,4},{2,7},{3,6},{4,1},{5,0},{6,3},{7,2},{8,13},{9,12},{10,... | collective-permute-start | bytes 356360 | tf_op jit(solution)/shard_map/ppermute | solution.py:679
  9.3 16.8 %collective-permute-start.3 = (bf16[29,16,128]{2,1,0:T(8,128)(2,1)S(1)}, bf16[29,16,128]{2,1,0:T(8,128)(2,1)S(1)}, u32[]{:S(2)}, u32[]{:S(2)}) collective-permute-start(bf16[29,16,128]{2,1,0:T(8,128)(2,1)S(1)} %get-tuple-element.36), channel_id=1, source_target_pairs={{0,6},{1,7},{2,4},{3,5},{4,2},{5,3},{6,0},{7,1},{8,14},{9,15},{10,... | collective-permute-start | bytes 356360 | tf_op jit(solution)/shard_map/ppermute | solution.py:679
  11.0 15.2 %collective-permute-start.4 = (bf16[29,16,128]{2,1,0:T(8,128)(2,1)S(1)}, bf16[29,16,128]{2,1,0:T(8,128)(2,1)S(1)}, u32[]{:S(2)}, u32[]{:S(2)}) collective-permute-start(bf16[29,16,128]{2,1,0:T(8,128)(2,1)S(1)} %get-tuple-element.37), channel_id=1, source_target_pairs={{0,1},{1,0},{2,3},{3,2},{4,5},{5,4},{6,7},{7,6},{8,9},{9,8},{10,11... | collective-permute-start | bytes 356360 | tf_op jit(solution)/shard_map/ppermute | solution.py:679
  17.1 9.0 %collective-permute-start.5 = (bf16[29,16,128]{2,1,0:T(8,128)(2,1)S(1)}, bf16[29,16,128]{2,1,0:T(8,128)(2,1)S(1)}, u32[]{:S(2)}, u32[]{:S(2)}) collective-permute-start(bf16[29,16,128]{2,1,0:T(8,128)(2,1)S(1)} %slice.4), channel_id=1, source_target_pairs={{0,1},{1,0},{2,3},{3,2},{4,5},{5,4},{6,7},{7,6},{8,9},{9,8},{10,11... | collective-permute-start | bytes 356360 | tf_op jit(solution)/shard_map/ppermute | solution.py:679
  17.2 10.1 %collective-permute-start.6 = (bf16[29,16,128]{2,1,0:T(8,128)(2,1)S(1)}, bf16[29,16,128]{2,1,0:T(8,128)(2,1)S(1)}, u32[]{:S(2)}, u32[]{:S(2)}) collective-permute-start(bf16[29,16,128]{2,1,0:T(8,128)(2,1)S(1)} %get-tuple-element.39), channel_id=1, source_target_pairs={{0,7},{1,6},{2,5},{3,4},{4,3},{5,2},{6,1},{7,0},{8,15},{9,14},{10,... | collective-permute-start | bytes 356360 | tf_op jit(solution)/shard_map/ppermute | solution.py:679
  27.5 5.5 %collective-permute-start.8 = (bf16[16,16,128]{2,1,0:T(8,128)(2,1)S(1)}, bf16[16,16,128]{2,1,0:T(8,128)(2,1)S(1)}, u32[]{:S(2)}, u32[]{:S(2)}) collective-permute-start(bf16[16,16,128]{2,1,0:T(8,128)(2,1)S(1)} %get-tuple-element.44.left_grid), channel_id=1, source_target_pairs={{0,24},{8,0},{16,8},{24,16},{1,25},{9,1},{17,9},{25,17},{2,26},{10... | collective-permute-start | bytes 196616 | tf_op jit(solution)/shard_map/ppermute | solution.py:731
  30.1 4.4 %collective-permute-start.7 = (bf16[16,16,128]{2,1,0:T(8,128)(2,1)S(1)}, bf16[16,16,128]{2,1,0:T(8,128)(2,1)S(1)}, u32[]{:S(2)}, u32[]{:S(2)}) collective-permute-start(bf16[16,16,128]{2,1,0:T(8,128)(2,1)S(1)} %get-tuple-element.40.right_grid), channel_id=1, source_target_pairs={{0,24},{8,0},{16,8},{24,16},{1,25},{9,1},{17,9},{25,17},{2,26},{10... | collective-permute-start | bytes 196616 | tf_op jit(solution)/shard_map/ppermute | solution.py:731

commit v11 on v10

--- a/solution.py
+++ b/solution.py
@@ -28,16 +28,6 @@
     return pl.CostEstimate(flops=flops, bytes_accessed=size, transcendentals=0)
 
 
-def exact_dot(left, right):
-    return lax.dot_general(
-        left,
-        right,
-        (((1,), (1,)), ((), ())),
-        precision=lax.Precision.HIGHEST,
-        preferred_element_type=jnp.float32,
-    )
-
-
 def points_of(spots, zoom, frac, offset, axis, tile, ratio):
     scale = zoom[axis, tile] * ratio
     return (spots - offset[axis, tile].astype(jnp.float32) - frac[axis, tile]) / scale
@@ -115,14 +105,23 @@
 
 
 def render_kernel(
-    sizes, zoom_in, frac_in, offset_in, owner_in, patches_in, frames, *outgoing_and_scratch
+    sizes,
+    zoom_in,
+    frac_in,
+    offset_in,
+    owner_in,
+    patches_in,
+    frames,
+    zoom,
+    frac,
+    offset,
+    owner,
+    *outgoing_and_scratch,
 ):
     tiles, bands, frame, source, capacity, devices = sizes
     plan, _ = exchange_plan(devices)
     outgoing = outgoing_and_scratch[: len(plan)]
-    zoom, frac, offset, owner, patches, named, rows, small_sems, patch_sems = (
-        outgoing_and_scratch[len(plan) :]
-    )
+    patches, named, rows, small_sems, patch_sems = outgoing_and_scratch[len(plan) :]
     me = lax.axis_index("tile")
     first_tile = me * tiles
     ratio = frame / source
@@ -206,16 +205,6 @@
                 continue
             for slot in range(capacity):
                 there[position * capacity + slot] = frames[rows[target * capacity + slot]]
-
-
-def feature_rows(frame, wanted):
-    shape = (ROWS, frame)
-    x = coords(spots_along(shape, 1), frame)
-    row = lax.broadcasted_iota(jnp.int32, shape, 0)
-    rows = jnp.zeros(shape, jnp.float32)
-    for r, power in wanted.items():
-        rows = jnp.where(row == r, (jnp.ones_like(x), x, x * x)[power], rows)
-    return rows
 
 
 MOMENT_ROWS = ((0, 0, {0: 0, 1: 1}), (0, 1, {2: 0}), (1, 0, {0: 2}), (1, 1, {1: 1}), (1, 2, {2: 0}))
@@ -306,7 +295,8 @@
     me = lax.axis_index("tile")
     all_tiles = tiles * devices
     ratio = frame / source
-    parts[...] = jnp.zeros_like(parts)
+    x = coords(spots_along((1, frame), 1), frame)
+    x_powers = (jnp.ones_like(x), x, x * x)
     for j in range(tiles):
         tile = me * tiles + j
         spots = spots_along((frame, frame), 0)
@@ -321,13 +311,21 @@
                 columns * jnp.sum(rows if image is None else rows * image, axis=0, keepdims=True)
                 for rows in weighted
             ]
-            for k, (half, a, _) in enumerate(MOMENT_ROWS):
-                place = 2 * all_tiles + tiles * (2 * power + half) + j
-                parts[k, place : place + 1, :] = sums[a]
-    total = 0.0
-    for k, (_, _, wanted) in enumerate(MOMENT_ROWS):
-        total += exact_dot(feature_rows(frame, wanted), parts[k])
-    base[...] = total[:PAYLOAD_ROWS]
+            for half, a, wanted in MOMENT_ROWS:
+                group = tiles * (2 * power + half) + j
+                for r, degree in wanted.items():
+                    parts[r, group : group + 1, :] = sums[a] * x_powers[degree]
+    values = [jnp.sum(parts[r], axis=1, keepdims=True) for r in range(3)]
+    count = parts.shape[1]
+    place = lax.broadcasted_iota(jnp.int32, (count, LANES), 0) + 2 * all_tiles
+    total = []
+    for start in range(0, base.shape[1], LANES):
+        here = lax.broadcasted_iota(jnp.int32, (count, LANES), 1) + start == place
+        rows = [
+            jnp.sum(jnp.where(here, value, 0.0), axis=0, keepdims=True) for value in values
+        ]
+        total.append(jnp.concatenate(rows + [jnp.zeros_like(rows[0])], axis=0))
+    base[...] = jnp.concatenate(total, axis=1)
 
 
 def add_blocks(sizes, chosen, slot_bands, col_cover, blocks, whole, total):
@@ -353,6 +351,12 @@
 def first_blend_kernel(sizes, chosen, slot_bands, col_cover, *refs):
     blocks, (total, *whole) = refs[: len(chosen)], refs[len(chosen) :]
     total[...] = jnp.zeros_like(total)
+    add_blocks(sizes, chosen, slot_bands, col_cover, blocks, whole, total)
+
+
+def middle_blend_kernel(sizes, chosen, slot_bands, col_cover, before, *refs):
+    blocks, (total, *whole) = refs[: len(chosen)], refs[len(chosen) :]
+    total[...] = before[...]
     add_blocks(sizes, chosen, slot_bands, col_cover, blocks, whole, total)
 
 
@@ -618,17 +622,15 @@
         )
         for group in plan
     ]
-    frames, *outgoing = pl.pallas_call(
+    frames, zoom, frac, offset, routes, *outgoing = pl.pallas_call(
         functools.partial(render_kernel, sizes),
         name="render",
         in_specs=[HBM] * 5,
-        out_specs=[VMEM] * (1 + len(plan)),
-        out_shape=[jax.ShapeDtypeStruct((rows, BAND, frame), jnp.bfloat16)] + blocks,
+        out_specs=[VMEM] + [SMEM] * 4 + [VMEM] * len(plan),
+        out_shape=[jax.ShapeDtypeStruct((rows, BAND, frame), jnp.bfloat16)]
+        + [pltpu.SMEM(x.shape, x.dtype) for x in (*place, routes)]
+        + blocks,
         scratch_shapes=[
-            pltpu.SMEM(place[0].shape, jnp.float32),
-            pltpu.SMEM(place[1].shape, jnp.float32),
-            pltpu.SMEM(place[2].shape, jnp.int32),
-            pltpu.SMEM(routes.shape, jnp.int32),
             pltpu.VMEM((tiles, source, source), jnp.bfloat16),
             pltpu.SMEM((devices,), jnp.int32),
             pltpu.SMEM((slots,), jnp.int32),
@@ -638,6 +640,9 @@
         compiler_params=params(24),
         cost_estimate=cost(800_000_000, 4 << 20),
     )(*(pltpu.with_memory_space_constraint(x, pltpu.HBM) for x in (*place, routes, patches[0])))
+    *place, routes = (
+        pltpu.with_memory_space_constraint(x, pltpu.SMEM) for x in (zoom, frac, offset, routes)
+    )
 
     base = pl.pallas_call(
         functools.partial(moment_kernel, sizes),
@@ -645,7 +650,7 @@
         in_specs=[SMEM] * 3 + [VMEM],
         out_specs=VMEM,
         out_shape=jax.ShapeDtypeStruct((PAYLOAD_ROWS, width), jnp.float32),
-        scratch_shapes=[pltpu.VMEM((len(MOMENT_ROWS), width, frame), jnp.float32)],
+        scratch_shapes=[pltpu.VMEM((3, 6 * tiles, frame), jnp.float32)],
         compiler_params=params(24),
         cost_estimate=cost(20_000_000, 1 << 20),
     )(*place, frames)
@@ -655,7 +660,7 @@
         name="scan",
         in_specs=[SMEM],
         out_specs=SMEM,
-        out_shape=jax.ShapeDtypeStruct((slots + 1,), jnp.int32),
+        out_shape=pltpu.SMEM((slots + 1,), jnp.int32),
         compiler_params=params(24),
         cost_estimate=cost(20_000_000, 1 << 20),
     )(routes)
@@ -673,7 +678,7 @@
         ],
         compiler_params=params(24),
         cost_estimate=cost(20_000_000, 1 << 20),
-    )(*place, codes)
+    )(*place, pltpu.with_memory_space_constraint(codes, pltpu.SMEM))
 
     def swapped(block, distance):
         return lax.ppermute(block, "tile", [(i, i ^ distance) for i in range(devices)])
@@ -713,8 +718,13 @@
         return found[: len(results)]
 
     last = [5] if devices == 8 else range(devices - devices // 4, devices)
-    early = [block for block in range(devices) if block not in last]
+    middle = [4, 7] if devices == 8 else []
+    early = [block for block in range(devices) if block not in [*middle, *last]]
     (before,) = blend(first_blend_kernel, "first_blend", early, [total], [], col_cover)
+    if middle:
+        (before,) = blend(
+            middle_blend_kernel, "middle_blend", middle, [total], [], col_cover, before
+        )
     half = jax.ShapeDtypeStruct((bands, BAND, frame // 2), jnp.bfloat16)
     grids = blend(
         last_blend_kernel,

time: 49.8 us -> 49.8 us (level)
  Pallas kernels: 15.1 us -> 10.9 us
  waiting for transfers between devices: 6.17 us -> 8.67 us
  blocking collectives: 13 us -> 14.7 us
    pallas_call x1, Pallas kernels: 2.9 us -> 0.01 us  [shards(): pl.pallas_call(functools.partial(scan_kernel, sizes), name='scan', in_spe...]
    all_to_all x1, blocking collectives: 13 us -> 14.7 us  [shards(): lax.all_to_all(payload, ('sec', 'tile'), split_axis=0, concat_axis=0, til...]
    ppermute x7, waiting for transfers between devices: 5.21 us -> 6.81 us  [swapped(): lax.ppermute(block, 'tile', [(i, i ^ distance) for i in range(devices)])]
    ppermute x2, waiting for transfers between devices: 0.96 us -> 1.86 us  [shards(): from_next = [lax.ppermute(grid, 'sec', ring) for grid in grids]]
    pallas_call x1, Pallas kernels: 1.9 us -> 1.01 us  [shards(): pl.pallas_call(functools.partial(moment_kernel, sizes), name='moments', i...]
    pallas_call x1, Pallas kernels: 2.96 us -> 2.46 us  [shards(): pl.pallas_call(functools.partial(slot_kernel, sizes), name='slots', in_sp...]
    pallas_call x2 -> x3, Pallas kernels: 1.4 us -> 1.46 us  [blend(): pl.pallas_call(functools.partial(kernel, sizes, distances), name=name, in...]
  transfers between devices with their start and end apart: 9 -> 9, of which waited for: 2 -> 3; matrix products, arithmetic and copies ran while one was open for 0% -> 0% of each run, Pallas kernels for 20% -> 11%
where the time goes in v11:
time: 49.8 us; the launch traced here: 49.6 us
  starting transfers between devices  14.7 us (30%)
  blocking collectives  14.7 us (30%)
  Pallas kernels  10.9 us (22%)
  waiting for transfers between devices  8.67 us (17%)
  between operations  0.72 us (1%)
    all_to_all x1, blocking collectives, shards(): lax.all_to_all(payload, ('sec', 'tile'), split_axis=0, concat_axis=0, til...  14.7 us
    ppermute x7, starting transfers between devices, swapped(): lax.ppermute(block, 'tile', [(i, i ^ distance) for i in range(devices)])  11.7 us
    ppermute x7, waiting for transfers between devices, swapped(): lax.ppermute(block, 'tile', [(i, i ^ distance) for i in range(devices)])  6.81 us
    ppermute x2, starting transfers between devices, shards(): from_next = [lax.ppermute(grid, 'sec', ring) for grid in grids]  3.03 us
    pallas_call x1, Pallas kernels, shards(): pl.pallas_call(functools.partial(render_kernel, sizes), name='render', in...  2.92 us
    pallas_call x1, Pallas kernels, shards(): pl.pallas_call(functools.partial(slot_kernel, sizes), name='slots', in_sp...  2.46 us
    ppermute x2, waiting for transfers between devices, shards(): from_next = [lax.ppermute(grid, 'sec', ring) for grid in grids]  1.86 us
    pallas_call x3, Pallas kernels, blend(): pl.pallas_call(functools.partial(kernel, sizes, distances), name=name, in...  1.46 us
  transfers between devices with their start and end apart: 9, of which 3 were waited for; matrix products, arithmetic and copies ran while one was open for 0% of the time, Pallas kernels for 11%

profile of v11, /device:TPU:0, one launch (start us, length us, event | category | flops | bytes accessed | tf_op | source)
XLA Modules:
  0.0 49.6 jit_solution(9958026507790766531)
XLA Ops:
  0.6 2.9 %render.1 = (bf16[64,16,256]{2,1,0:T(8,128)(2,1)S(1)}, f32[2,32]{1,0:T(2,128)S(4)}, f32[2,32]{1,0:T(2,128)S(4)}, s32[2,32]{1,0:T(2,128)S(4)}, s32[16,1,32]{2,1,0...) custom-call(f32[2,32]{1,0:T(2,128)} %bitcast.20, ...), custom_call_target="tpu_custom_call" | custom-call | flops 800000000 | bytes 4194304 | tf_op jit(solution)/shard_map/render/pallas_call | solution.py:625
  3.6 0.0 copy-start
  3.6 3.1 %collective-permute-start = (bf16[58,16,128]{2,1,0:T(8,128)(2,1)S(1)}, bf16[58,16,128]{2,1,0:T(8,128)(2,1)S(1)}, u32[]{:S(2)}, u32[]{:S(2)}) collective-permute-start(bf16[58,16,128]{2,1,0:T(8,128)(2,1)S(1)} %get-tuple-element.42), channel_id=1, source_target_pairs={{0,2},{1,3},{2,0},{3,1},{4,6},{5,7},{6,4},{7,5},{8,10},{9,11},{10,... | collective-permute-start | bytes 712712 | tf_op jit(solution)/shard_map/ppermute | solution.py:684
  6.7 2.6 %collective-permute-start.1 = (bf16[29,16,128]{2,1,0:T(8,128)(2,1)S(1)}, bf16[29,16,128]{2,1,0:T(8,128)(2,1)S(1)}, u32[]{:S(2)}, u32[]{:S(2)}) collective-permute-start(bf16[29,16,128]{2,1,0:T(8,128)(2,1)S(1)} %get-tuple-element.43), channel_id=1, source_target_pairs={{0,4},{1,5},{2,6},{3,7},{4,0},{5,1},{6,2},{7,3},{8,12},{9,13},{10,... | collective-permute-start | bytes 356360 | tf_op jit(solution)/shard_map/ppermute | solution.py:684
  9.3 0.0 collective-permute-start.2
  9.3 0.4 collective-permute-start.3
  9.7 2.5 %collective-permute-start.4 = (bf16[29,16,128]{2,1,0:T(8,128)(2,1)S(1)}, bf16[29,16,128]{2,1,0:T(8,128)(2,1)S(1)}, u32[]{:S(2)}, u32[]{:S(2)}) collective-permute-start(bf16[29,16,128]{2,1,0:T(8,128)(2,1)S(1)} %get-tuple-element.47), channel_id=1, source_target_pairs={{0,6},{1,7},{2,4},{3,5},{4,2},{5,3},{6,0},{7,1},{8,14},{9,15},{10,... | collective-permute-start | bytes 356360 | tf_op jit(solution)/shard_map/ppermute | solution.py:684
  12.2 4.9 %collective-permute-done.refs_1_ = bf16[58,16,128]{2,1,0:T(8,128)(2,1)S(1)} collective-permute-done((bf16[58,16,128]{2,1,0:T(8,128)(2,1)S(1)}, bf16[58,16,128]{2,1,0:T(8,128)(2,1)S(1)}, u32[]{:S(2)}, u32[]{:S(2)}) %collective-permute-start) | collective-permute-done | bytes 237600 | tf_op jit(solution)/shard_map/ppermute | solution.py:684
  17.1 0.1 collective-permute-start.5
  17.2 0.0 collective-permute-done.1.refs_2_
  17.2 3.0 %collective-permute-start.6 = (bf16[29,16,128]{2,1,0:T(8,128)(2,1)S(1)}, bf16[29,16,128]{2,1,0:T(8,128)(2,1)S(1)}, u32[]{:S(2)}, u32[]{:S(2)}) collective-permute-start(bf16[29,16,128]{2,1,0:T(8,128)(2,1)S(1)} %get-tuple-element.49), channel_id=1, source_target_pairs={{0,7},{1,6},{2,5},{3,4},{4,3},{5,2},{6,1},{7,0},{8,15},{9,14},{10,... | collective-permute-start | bytes 356360 | tf_op jit(solution)/shard_map/ppermute | solution.py:684
  20.2 2.5 %slots.1 = (f32[17,16,256]{2,1,0:T(8,128)S(1)}, f32[40,256]{1,0:T(8,128)S(1)}, f32[3,128,128]{2,1,0:T(8,128)S(1)}, s32[3,128]{1,0:T(4,128)S(4)}) custom-call(f32[2,32]{1,0:T(2,128)S(4)} %get-tuple-element.34.zoom, f32[2,32]{1,0:T(2,128)S(4)} %get-tuple-element.35.frac, s32[2,32]{1,0:T(2,128)S(4)} %get-tuple-element.36.offset, s32[129]{0:T(256)S(4)} %scan.1.codes), custom_call_target="tpu_custom_call" | custom-call | flops 20000000 | bytes 1048576 | tf_op jit(solution)/shard_map/slots/pallas_call | solution.py:668
  22.6 1.9 %collective-permute-done.2.refs_3_ = bf16[29,16,128]{2,1,0:T(8,128)(2,1)S(1)} collective-permute-done((bf16[29,16,128]{2,1,0:T(8,128)(2,1)S(1)}, bf16[29,16,128]{2,1,0:T(8,128)(2,1)S(1)}, u32[]{:S(2)}, u32[]{:S(2)}) %collective-permute-start.2) | collective-permute-done | bytes 118816 | tf_op jit(solution)/shard_map/ppermute | solution.py:684
  24.5 0.0 collective-permute-done.3.refs_4_
  24.5 0.8 %first_blend.1 = (f32[17,16,256]{2,1,0:T(8,128)S(1)}, bf16[16,16,256]{2,1,0:T(8,128)(2,1)S(1)}, bf16[16,16,256]{2,1,0:T(8,128)(2,1)S(1)}, bf16[16,16,256]{2,1,0:T(8,128)(2,1)S(1)}, bf16[16,16,256]{2,1,0:T(8,128)(2,1)S(1)}) custom-call(s32[3,128]{1,0:T(4,128)S(4)} %get-tuple-element.38.slot_bands, f32[40,256]{1,0:T(8,128)S(1)} %get-tuple-element.39.col_cover, ...), custom_call_target="tpu_custom_call" | custom-call | flops 1000000 | bytes 2097152 | tf_op jit(solution)/shard_map/first_blend/pallas_call | solution.py:706
  25.3 0.0 collective-permute-done.4.refs_0_
  25.3 0.0 collective-permute-done.5.refs_1_
  25.4 0.4 middle_blend.1
  25.7 0.0 collective-permute-done.6.refs_0_
  25.8 0.3 last_blend.1
  26.0 2.5 %collective-permute-start.8 = (bf16[16,16,128]{2,1,0:T(8,128)(2,1)S(1)}, bf16[16,16,128]{2,1,0:T(8,128)(2,1)S(1)}, u32[]{:S(2)}, u32[]{:S(2)}) collective-permute-start(bf16[16,16,128]{2,1,0:T(8,128)(2,1)S(1)} %get-tuple-element.54.left_grid), channel_id=1, source_target_pairs={{0,24},{8,0},{16,8},{24,16},{1,25},{9,1},{17,9},{25,17},{2,26},{10... | collective-permute-start | bytes 196616 | tf_op jit(solution)/shard_map/ppermute | solution.py:741
  28.5 0.5 %collective-permute-start.7 = (bf16[16,16,128]{2,1,0:T(8,128)(2,1)S(1)}, bf16[16,16,128]{2,1,0:T(8,128)(2,1)S(1)}, u32[]{:S(2)}, u32[]{:S(2)}) collective-permute-start(bf16[16,16,128]{2,1,0:T(8,128)(2,1)S(1)} %get-tuple-element.50.right_grid), channel_id=1, source_target_pairs={{0,24},{8,0},{16,8},{24,16},{1,25},{9,1},{17,9},{25,17},{2,26},{10... | collective-permute-start | bytes 196616 | tf_op jit(solution)/shard_map/ppermute | solution.py:741
  29.0 0.4 weights.1
  29.5 1.0 %moments.1.base = f32[4,128]{1,0:T(4,128)S(1)} custom-call(f32[2,32]{1,0:T(2,128)S(4)} %get-tuple-element.34.zoom, f32[2,32]{1,0:T(2,128)S(4)} %get-tuple-element.35.frac, s32[2,32]{1,0:T(2,128)S(4)} %get-tuple-element.36.offset, bf16[64,16,256]{2,1,0:T(8,128)(2,1)S(1)} %get-tuple-element.63.frames), custom_call_target="tpu_custom_call" | custom-call | flops 20000000 | bytes 1048576 | tf_op jit(solution)/shard_map/moments/pallas_call | solution.py:647
  30.5 0.0 collective-permute-done.8.from_next
  30.5 0.0 copy-done
  30.5 0.5 %left_gradient.1.left_sums = f32[4,264,128]{2,1,0:T(8,128)S(1)} custom-call(s32[3,128]{1,0:T(4,128)S(4)} %get-tuple-element.38.slot_bands, bf16[16,16,128]{2,1,0:T(8,128)(2,1)S(1)} %collective-permute-done.8.from_next, bf16[16,16,256]{2,1,0:T(8,128)(2,1)S(1)} %bitcast.14, ...), custom_call_target="tpu_custom_call", output_to_operand_aliasing={{}: (4, {})} | custom-call | flops 8000000 | bytes 2097152 | tf_op jit(solution)/shard_map/left_gradient/pallas_call | solution.py:756
  31.0 1.9 %collective-permute-done.7.from_next = bf16[16,16,128]{2,1,0:T(8,128)(2,1)S(1)} collective-permute-done((bf16[16,16,128]{2,1,0:T(8,128)(2,1)S(1)}, bf16[16,16,128]{2,1,0:T(8,128)(2,1)S(1)}, u32[]{:S(2)}, u32[]{:S(2)}) %collective-permute-start.7) | collective-permute-done | bytes 65568 | tf_op jit(solution)/shard_map/ppermute | solution.py:741
  32.9 0.8 %gradient.1 = (f32[32,4,128]{2,1,0:T(4,128)S(1)}, bf16[16,16,256]{2,1,0:T(8,128)(2,1)}, f32[4,264,128]{2,1,0:T(8,128)S(1)}) custom-call(s32[3,128]{1,0:T(4,128)S(4)} %get-tuple-element.38.slot_bands, bf16[16,16,128]{2,1,0:T(8,128)(2,1)S(1)} %collective-permute-done.7.from_next, bf16[16,16,256]{2,1,0:T(8,128)(2,1)S(1)} %bitcast.15, ...), custom_call_target="tpu_custom_call", output_to_operand_aliasing={{2}: (4, {})} | custom-call | flops 8000000 | bytes 2097152 | tf_op jit(solution)/shard_map/gradient/pallas_call | solution.py:768
  33.7 14.7 %all_to_all.5.received = f32[32,4,128]{2,1,0:T(4,128)S(1)} all-to-all(f32[32,4,128]{2,1,0:T(4,128)S(1)} %get-tuple-element.65), channel_id=1, replica_groups=mesh['sec'=4,'tile'=8] {'sec','tile'}, dimensions={0} | all-to-all | bytes 131072 | tf_op jit(solution)/shard_map/all_to_all | solution.py:795
  48.3 1.3 %solve.1 = f32[4,6]{1,0:T(4,128)} custom-call(f32[32,4,128]{2,1,0:T(4,128)S(1)} %all_to_all.5.received), custom_call_target="tpu_custom_call" | custom-call | flops 100000 | bytes 262144 | tf_op jit(solution)/shard_map/solve/pallas_call | solution.py:799
  (2 shorter events, 0.0 us)
Async XLA Ops:
  3.6 26.9 %copy-start = (bf16[1,256,256]{2,1,0:T(8,128)(2,1)S(1)}, bf16[1,256,256]{2,1,0:T(8,128)(2,1)}, u32[]{:S(2)}) copy-start(bf16[1,256,256]{2,1,0:T(8,128)(2,1)} %param.11) | copy-start | bytes 393220
  3.6 13.5 %collective-permute-start = (bf16[58,16,128]{2,1,0:T(8,128)(2,1)S(1)}, bf16[58,16,128]{2,1,0:T(8,128)(2,1)S(1)}, u32[]{:S(2)}, u32[]{:S(2)}) collective-permute-start(bf16[58,16,128]{2,1,0:T(8,128)(2,1)S(1)} %get-tuple-element.42), channel_id=1, source_target_pairs={{0,2},{1,3},{2,0},{3,1},{4,6},{5,7},{6,4},{7,5},{8,10},{9,11},{10,... | collective-permute-start | bytes 712712 | tf_op jit(solution)/shard_map/ppermute | solution.py:684
  6.7 10.5 %collective-permute-start.1 = (bf16[29,16,128]{2,1,0:T(8,128)(2,1)S(1)}, bf16[29,16,128]{2,1,0:T(8,128)(2,1)S(1)}, u32[]{:S(2)}, u32[]{:S(2)}) collective-permute-start(bf16[29,16,128]{2,1,0:T(8,128)(2,1)S(1)} %get-tuple-element.43), channel_id=1, source_target_pairs={{0,4},{1,5},{2,6},{3,7},{4,0},{5,1},{6,2},{7,3},{8,12},{9,13},{10,... | collective-permute-start | bytes 356360 | tf_op jit(solution)/shard_map/ppermute | solution.py:684
  9.3 15.3 %collective-permute-start.2 = (bf16[29,16,128]{2,1,0:T(8,128)(2,1)S(1)}, bf16[29,16,128]{2,1,0:T(8,128)(2,1)S(1)}, u32[]{:S(2)}, u32[]{:S(2)}) collective-permute-start(bf16[29,16,128]{2,1,0:T(8,128)(2,1)S(1)} %get-tuple-element.44), channel_id=1, source_target_pairs={{0,5},{1,4},{2,7},{3,6},{4,1},{5,0},{6,3},{7,2},{8,13},{9,12},{10,... | collective-permute-start | bytes 356360 | tf_op jit(solution)/shard_map/ppermute | solution.py:684
  9.3 15.3 %collective-permute-start.3 = (bf16[29,16,128]{2,1,0:T(8,128)(2,1)S(1)}, bf16[29,16,128]{2,1,0:T(8,128)(2,1)S(1)}, u32[]{:S(2)}, u32[]{:S(2)}) collective-permute-start(bf16[29,16,128]{2,1,0:T(8,128)(2,1)S(1)} %get-tuple-element.45), channel_id=1, source_target_pairs={{0,1},{1,0},{2,3},{3,2},{4,5},{5,4},{6,7},{7,6},{8,9},{9,8},{10,11... | collective-permute-start | bytes 356360 | tf_op jit(solution)/shard_map/ppermute | solution.py:684
  9.7 15.7 %collective-permute-start.4 = (bf16[29,16,128]{2,1,0:T(8,128)(2,1)S(1)}, bf16[29,16,128]{2,1,0:T(8,128)(2,1)S(1)}, u32[]{:S(2)}, u32[]{:S(2)}) collective-permute-start(bf16[29,16,128]{2,1,0:T(8,128)(2,1)S(1)} %get-tuple-element.47), channel_id=1, source_target_pairs={{0,6},{1,7},{2,4},{3,5},{4,2},{5,3},{6,0},{7,1},{8,14},{9,15},{10,... | collective-permute-start | bytes 356360 | tf_op jit(solution)/shard_map/ppermute | solution.py:684
  17.1 8.3 %collective-permute-start.5 = (bf16[29,16,128]{2,1,0:T(8,128)(2,1)S(1)}, bf16[29,16,128]{2,1,0:T(8,128)(2,1)S(1)}, u32[]{:S(2)}, u32[]{:S(2)}) collective-permute-start(bf16[29,16,128]{2,1,0:T(8,128)(2,1)S(1)} %slice.4), channel_id=1, source_target_pairs={{0,1},{1,0},{2,3},{3,2},{4,5},{5,4},{6,7},{7,6},{8,9},{9,8},{10,11... | collective-permute-start | bytes 356360 | tf_op jit(solution)/shard_map/ppermute | solution.py:684
  17.2 8.6 %collective-permute-start.6 = (bf16[29,16,128]{2,1,0:T(8,128)(2,1)S(1)}, bf16[29,16,128]{2,1,0:T(8,128)(2,1)S(1)}, u32[]{:S(2)}, u32[]{:S(2)}) collective-permute-start(bf16[29,16,128]{2,1,0:T(8,128)(2,1)S(1)} %get-tuple-element.49), channel_id=1, source_target_pairs={{0,7},{1,6},{2,5},{3,4},{4,3},{5,2},{6,1},{7,0},{8,15},{9,14},{10,... | collective-permute-start | bytes 356360 | tf_op jit(solution)/shard_map/ppermute | solution.py:684
  26.0 4.5 %collective-permute-start.8 = (bf16[16,16,128]{2,1,0:T(8,128)(2,1)S(1)}, bf16[16,16,128]{2,1,0:T(8,128)(2,1)S(1)}, u32[]{:S(2)}, u32[]{:S(2)}) collective-permute-start(bf16[16,16,128]{2,1,0:T(8,128)(2,1)S(1)} %get-tuple-element.54.left_grid), channel_id=1, source_target_pairs={{0,24},{8,0},{16,8},{24,16},{1,25},{9,1},{17,9},{25,17},{2,26},{10... | collective-permute-start | bytes 196616 | tf_op jit(solution)/shard_map/ppermute | solution.py:741
  28.5 4.4 %collective-permute-start.7 = (bf16[16,16,128]{2,1,0:T(8,128)(2,1)S(1)}, bf16[16,16,128]{2,1,0:T(8,128)(2,1)S(1)}, u32[]{:S(2)}, u32[]{:S(2)}) collective-permute-start(bf16[16,16,128]{2,1,0:T(8,128)(2,1)S(1)} %get-tuple-element.50.right_grid), channel_id=1, source_target_pairs={{0,24},{8,0},{16,8},{24,16},{1,25},{9,1},{17,9},{25,17},{2,26},{10... | collective-permute-start | bytes 196616 | tf_op jit(solution)/shard_map/ppermute | solution.py:741

commit v12 on v11

--- a/solution.py
+++ b/solution.py
@@ -211,7 +211,7 @@
 PAYLOAD_ROWS = 4
 
 
-def scan_kernel(sizes, owner, codes):
+def scan_kernel(sizes, owner, _, codes):
     tiles, bands, frame, source, capacity, devices = sizes
     me = lax.axis_index("tile")
 
@@ -658,12 +658,12 @@
     codes = pl.pallas_call(
         functools.partial(scan_kernel, sizes),
         name="scan",
-        in_specs=[SMEM],
+        in_specs=[SMEM, VMEM],
         out_specs=SMEM,
         out_shape=pltpu.SMEM((slots + 1,), jnp.int32),
         compiler_params=params(24),
         cost_estimate=cost(20_000_000, 1 << 20),
-    )(routes)
+    )(routes, base)
 
     cover_sum, col_cover, slot_lines, slot_bands = pl.pallas_call(
         functools.partial(slot_kernel, sizes),

time: 49.8 us -> 49.8 us (level)
  Pallas kernels: 10.9 us -> 12.9 us
  blocking collectives: 14.7 us -> 13.1 us
  waiting for transfers between devices: 8.67 us -> 8.15 us
    pallas_call x1, Pallas kernels: 0.01 us -> 2.1 us  [shards(): pl.pallas_call(functools.partial(scan_kernel, sizes), name='scan', in_spe...]
    ppermute x7, waiting for transfers between devices: 6.81 us -> 4.92 us  [swapped(): lax.ppermute(block, 'tile', [(i, i ^ distance) for i in range(devices)])]
    all_to_all x1, blocking collectives: 14.7 us -> 13.1 us  [shards(): lax.all_to_all(payload, ('sec', 'tile'), split_axis=0, concat_axis=0, til...]
    ppermute x2, waiting for transfers between devices: 1.86 us -> 3.23 us  [shards(): from_next = [lax.ppermute(grid, 'sec', ring) for grid in grids]]
  transfers between devices with their start and end apart: 9 -> 9, of which waited for: 3 -> 3; matrix products, arithmetic and copies ran while one was open for 0% -> 0% of each run, Pallas kernels for 11% -> 16%
where the time goes in v12:
time: 49.8 us; the launch traced here: 49.6 us
  starting transfers between devices  14.7 us (30%)
  blocking collectives  13.1 us (26%)
  Pallas kernels  12.9 us (26%)
  waiting for transfers between devices  8.15 us (16%)
  between operations  0.74 us (1%)
    all_to_all x1, blocking collectives, shards(): lax.all_to_all(payload, ('sec', 'tile'), split_axis=0, concat_axis=0, til...  13.1 us
    ppermute x7, starting transfers between devices, swapped(): lax.ppermute(block, 'tile', [(i, i ^ distance) for i in range(devices)])  11.7 us
    ppermute x7, waiting for transfers between devices, swapped(): lax.ppermute(block, 'tile', [(i, i ^ distance) for i in range(devices)])  4.92 us
    ppermute x2, waiting for transfers between devices, shards(): from_next = [lax.ppermute(grid, 'sec', ring) for grid in grids]  3.23 us
    ppermute x2, starting transfers between devices, shards(): from_next = [lax.ppermute(grid, 'sec', ring) for grid in grids]  3 us
    pallas_call x1, Pallas kernels, shards(): pl.pallas_call(functools.partial(render_kernel, sizes), name='render', in...  2.92 us
    pallas_call x1, Pallas kernels, shards(): pl.pallas_call(functools.partial(slot_kernel, sizes), name='slots', in_sp...  2.47 us
    pallas_call x1, Pallas kernels, shards(): pl.pallas_call(functools.partial(scan_kernel, sizes), name='scan', in_spe...  2.1 us
  transfers between devices with their start and end apart: 9, of which 3 were waited for; matrix products, arithmetic and copies ran while one was open for 0% of the time, Pallas kernels for 16%

profile of v12, /device:TPU:0, one launch (start us, length us, event | category | flops | bytes accessed | tf_op | source)
XLA Modules:
  0.0 49.6 jit_solution(5926429499399490778)
XLA Ops:
  0.6 2.9 %render.1 = (bf16[64,16,256]{2,1,0:T(8,128)(2,1)S(1)}, f32[2,32]{1,0:T(2,128)S(4)}, f32[2,32]{1,0:T(2,128)S(4)}, s32[2,32]{1,0:T(2,128)S(4)}, s32[16,1,32]{2,1,0...) custom-call(f32[2,32]{1,0:T(2,128)} %bitcast.20, ...), custom_call_target="tpu_custom_call" | custom-call | flops 800000000 | bytes 4194304 | tf_op jit(solution)/shard_map/render/pallas_call | solution.py:625
  3.6 0.0 copy-start
  3.6 3.1 %collective-permute-start = (bf16[58,16,128]{2,1,0:T(8,128)(2,1)S(1)}, bf16[58,16,128]{2,1,0:T(8,128)(2,1)S(1)}, u32[]{:S(2)}, u32[]{:S(2)}) collective-permute-start(bf16[58,16,128]{2,1,0:T(8,128)(2,1)S(1)} %get-tuple-element.43), channel_id=1, source_target_pairs={{0,2},{1,3},{2,0},{3,1},{4,6},{5,7},{6,4},{7,5},{8,10},{9,11},{10,... | collective-permute-start | bytes 712712 | tf_op jit(solution)/shard_map/ppermute | solution.py:684
  6.7 2.6 %collective-permute-start.1 = (bf16[29,16,128]{2,1,0:T(8,128)(2,1)S(1)}, bf16[29,16,128]{2,1,0:T(8,128)(2,1)S(1)}, u32[]{:S(2)}, u32[]{:S(2)}) collective-permute-start(bf16[29,16,128]{2,1,0:T(8,128)(2,1)S(1)} %get-tuple-element.44), channel_id=1, source_target_pairs={{0,4},{1,5},{2,6},{3,7},{4,0},{5,1},{6,2},{7,3},{8,12},{9,13},{10,... | collective-permute-start | bytes 356360 | tf_op jit(solution)/shard_map/ppermute | solution.py:684
  9.3 0.0 collective-permute-start.2
  9.3 0.4 collective-permute-start.3
  9.7 2.5 %collective-permute-start.4 = (bf16[29,16,128]{2,1,0:T(8,128)(2,1)S(1)}, bf16[29,16,128]{2,1,0:T(8,128)(2,1)S(1)}, u32[]{:S(2)}, u32[]{:S(2)}) collective-permute-start(bf16[29,16,128]{2,1,0:T(8,128)(2,1)S(1)} %get-tuple-element.48), channel_id=1, source_target_pairs={{0,6},{1,7},{2,4},{3,5},{4,2},{5,3},{6,0},{7,1},{8,14},{9,15},{10,... | collective-permute-start | bytes 356360 | tf_op jit(solution)/shard_map/ppermute | solution.py:684
  12.2 4.9 %collective-permute-done.refs_1_ = bf16[58,16,128]{2,1,0:T(8,128)(2,1)S(1)} collective-permute-done((bf16[58,16,128]{2,1,0:T(8,128)(2,1)S(1)}, bf16[58,16,128]{2,1,0:T(8,128)(2,1)S(1)}, u32[]{:S(2)}, u32[]{:S(2)}) %collective-permute-start) | collective-permute-done | bytes 237600 | tf_op jit(solution)/shard_map/ppermute | solution.py:684
  17.1 0.1 collective-permute-start.5
  17.2 0.0 collective-permute-done.1.refs_2_
  17.2 3.0 %collective-permute-start.6 = (bf16[29,16,128]{2,1,0:T(8,128)(2,1)S(1)}, bf16[29,16,128]{2,1,0:T(8,128)(2,1)S(1)}, u32[]{:S(2)}, u32[]{:S(2)}) collective-permute-start(bf16[29,16,128]{2,1,0:T(8,128)(2,1)S(1)} %get-tuple-element.50), channel_id=1, source_target_pairs={{0,7},{1,6},{2,5},{3,4},{4,3},{5,2},{6,1},{7,0},{8,15},{9,14},{10,... | collective-permute-start | bytes 356360 | tf_op jit(solution)/shard_map/ppermute | solution.py:684
  20.2 1.0 %moments.1._.base = f32[4,128]{1,0:T(4,128)S(1)} custom-call(f32[2,32]{1,0:T(2,128)S(4)} %get-tuple-element.34.zoom, f32[2,32]{1,0:T(2,128)S(4)} %get-tuple-element.35.frac, s32[2,32]{1,0:T(2,128)S(4)} %get-tuple-element.36.offset, bf16[64,16,256]{2,1,0:T(8,128)(2,1)S(1)} %get-tuple-element.38.frames), custom_call_target="tpu_custom_call" | custom-call | flops 20000000 | bytes 1048576 | tf_op jit(solution)/shard_map/moments/pallas_call | solution.py:647
  21.2 2.1 %scan.1.codes = s32[129]{0:T(256)S(4)} custom-call(s32[16,1,32]{2,1,0:T(1,128)S(4)} %get-tuple-element.37.owner, f32[4,128]{1,0:T(4,128)S(1)} %moments.1._.base), custom_call_target="tpu_custom_call" | custom-call | flops 20000000 | bytes 1048576 | tf_op jit(solution)/shard_map/scan/pallas_call | solution.py:658
  23.3 2.5 %slots.1 = (f32[17,16,256]{2,1,0:T(8,128)S(1)}, f32[40,256]{1,0:T(8,128)S(1)}, f32[3,128,128]{2,1,0:T(8,128)S(1)}, s32[3,128]{1,0:T(4,128)S(4)}) custom-call(f32[2,32]{1,0:T(2,128)S(4)} %get-tuple-element.34.zoom, f32[2,32]{1,0:T(2,128)S(4)} %get-tuple-element.35.frac, s32[2,32]{1,0:T(2,128)S(4)} %get-tuple-element.36.offset, s32[129]{0:T(256)S(4)} %scan.1.codes), custom_call_target="tpu_custom_call" | custom-call | flops 20000000 | bytes 1048576 | tf_op jit(solution)/shard_map/slots/pallas_call | solution.py:668
  25.8 0.0 collective-permute-done.2.refs_3_
  25.8 0.0 collective-permute-done.3.refs_4_
  25.8 0.8 %first_blend.1 = (f32[17,16,256]{2,1,0:T(8,128)S(1)}, bf16[16,16,256]{2,1,0:T(8,128)(2,1)S(1)}, bf16[16,16,256]{2,1,0:T(8,128)(2,1)S(1)}, bf16[16,16,256]{2,1,0:T(8,128)(2,1)S(1)}, bf16[16,16,256]{2,1,0:T(8,128)(2,1)S(1)}) custom-call(s32[3,128]{1,0:T(4,128)S(4)} %get-tuple-element.39.slot_bands, f32[40,256]{1,0:T(8,128)S(1)} %get-tuple-element.40.col_cover, ...), custom_call_target="tpu_custom_call" | custom-call | flops 1000000 | bytes 2097152 | tf_op jit(solution)/shard_map/first_blend/pallas_call | solution.py:706
  26.6 0.0 collective-permute-done.4.refs_0_
  26.6 0.0 collective-permute-done.5.refs_1_
  26.6 0.4 middle_blend.1
  27.0 0.0 collective-permute-done.6.refs_0_
  27.0 0.3 last_blend.1
  27.3 2.5 %collective-permute-start.8 = (bf16[16,16,128]{2,1,0:T(8,128)(2,1)S(1)}, bf16[16,16,128]{2,1,0:T(8,128)(2,1)S(1)}, u32[]{:S(2)}, u32[]{:S(2)}) collective-permute-start(bf16[16,16,128]{2,1,0:T(8,128)(2,1)S(1)} %get-tuple-element.55.left_grid), channel_id=1, source_target_pairs={{0,24},{8,0},{16,8},{24,16},{1,25},{9,1},{17,9},{25,17},{2,26},{10... | collective-permute-start | bytes 196616 | tf_op jit(solution)/shard_map/ppermute | solution.py:741
  29.7 0.5 %collective-permute-start.7 = (bf16[16,16,128]{2,1,0:T(8,128)(2,1)S(1)}, bf16[16,16,128]{2,1,0:T(8,128)(2,1)S(1)}, u32[]{:S(2)}, u32[]{:S(2)}) collective-permute-start(bf16[16,16,128]{2,1,0:T(8,128)(2,1)S(1)} %get-tuple-element.51.right_grid), channel_id=1, source_target_pairs={{0,24},{8,0},{16,8},{24,16},{1,25},{9,1},{17,9},{25,17},{2,26},{10... | collective-permute-start | bytes 196616 | tf_op jit(solution)/shard_map/ppermute | solution.py:741
  30.3 0.4 weights.1
  30.7 0.9 %collective-permute-done.8.from_next = bf16[16,16,128]{2,1,0:T(8,128)(2,1)S(1)} collective-permute-done((bf16[16,16,128]{2,1,0:T(8,128)(2,1)S(1)}, bf16[16,16,128]{2,1,0:T(8,128)(2,1)S(1)}, u32[]{:S(2)}, u32[]{:S(2)}) %collective-permute-start.8) | collective-permute-done | bytes 65568 | tf_op jit(solution)/shard_map/ppermute | solution.py:741
  31.6 0.0 copy-done
  31.6 0.5 %left_gradient.1.left_sums = f32[4,264,128]{2,1,0:T(8,128)S(1)} custom-call(s32[3,128]{1,0:T(4,128)S(4)} %get-tuple-element.39.slot_bands, bf16[16,16,128]{2,1,0:T(8,128)(2,1)S(1)} %collective-permute-done.8.from_next, bf16[16,16,256]{2,1,0:T(8,128)(2,1)S(1)} %bitcast.14, ...), custom_call_target="tpu_custom_call", output_to_operand_aliasing={{}: (4, {})} | custom-call | flops 8000000 | bytes 2097152 | tf_op jit(solution)/shard_map/left_gradient/pallas_call | solution.py:756
  32.1 2.3 %collective-permute-done.7.from_next = bf16[16,16,128]{2,1,0:T(8,128)(2,1)S(1)} collective-permute-done((bf16[16,16,128]{2,1,0:T(8,128)(2,1)S(1)}, bf16[16,16,128]{2,1,0:T(8,128)(2,1)S(1)}, u32[]{:S(2)}, u32[]{:S(2)}) %collective-permute-start.7) | collective-permute-done | bytes 65568 | tf_op jit(solution)/shard_map/ppermute | solution.py:741
  34.4 0.8 %gradient.1 = (f32[32,4,128]{2,1,0:T(4,128)S(1)}, bf16[16,16,256]{2,1,0:T(8,128)(2,1)}, f32[4,264,128]{2,1,0:T(8,128)S(1)}) custom-call(s32[3,128]{1,0:T(4,128)S(4)} %get-tuple-element.39.slot_bands, bf16[16,16,128]{2,1,0:T(8,128)(2,1)S(1)} %collective-permute-done.7.from_next, bf16[16,16,256]{2,1,0:T(8,128)(2,1)S(1)} %bitcast.15, ...), custom_call_target="tpu_custom_call", output_to_operand_aliasing={{2}: (4, {})} | custom-call | flops 8000000 | bytes 2097152 | tf_op jit(solution)/shard_map/gradient/pallas_call | solution.py:768
  35.2 13.1 %all_to_all.5.received = f32[32,4,128]{2,1,0:T(4,128)S(1)} all-to-all(f32[32,4,128]{2,1,0:T(4,128)S(1)} %get-tuple-element.65), channel_id=1, replica_groups=mesh['sec'=4,'tile'=8] {'sec','tile'}, dimensions={0} | all-to-all | bytes 131072 | tf_op jit(solution)/shard_map/all_to_all | solution.py:795
  48.3 1.3 %solve.1 = f32[4,6]{1,0:T(4,128)} custom-call(f32[32,4,128]{2,1,0:T(4,128)S(1)} %all_to_all.5.received), custom_call_target="tpu_custom_call" | custom-call | flops 100000 | bytes 262144 | tf_op jit(solution)/shard_map/solve/pallas_call | solution.py:799
  (1 shorter events, 0.0 us)
Async XLA Ops:
  3.6 28.1 %copy-start = (bf16[1,256,256]{2,1,0:T(8,128)(2,1)S(1)}, bf16[1,256,256]{2,1,0:T(8,128)(2,1)}, u32[]{:S(2)}) copy-start(bf16[1,256,256]{2,1,0:T(8,128)(2,1)} %param.11) | copy-start | bytes 393220
  3.6 13.5 %collective-permute-start = (bf16[58,16,128]{2,1,0:T(8,128)(2,1)S(1)}, bf16[58,16,128]{2,1,0:T(8,128)(2,1)S(1)}, u32[]{:S(2)}, u32[]{:S(2)}) collective-permute-start(bf16[58,16,128]{2,1,0:T(8,128)(2,1)S(1)} %get-tuple-element.43), channel_id=1, source_target_pairs={{0,2},{1,3},{2,0},{3,1},{4,6},{5,7},{6,4},{7,5},{8,10},{9,11},{10,... | collective-permute-start | bytes 712712 | tf_op jit(solution)/shard_map/ppermute | solution.py:684
  6.7 10.5 %collective-permute-start.1 = (bf16[29,16,128]{2,1,0:T(8,128)(2,1)S(1)}, bf16[29,16,128]{2,1,0:T(8,128)(2,1)S(1)}, u32[]{:S(2)}, u32[]{:S(2)}) collective-permute-start(bf16[29,16,128]{2,1,0:T(8,128)(2,1)S(1)} %get-tuple-element.44), channel_id=1, source_target_pairs={{0,4},{1,5},{2,6},{3,7},{4,0},{5,1},{6,2},{7,3},{8,12},{9,13},{10,... | collective-permute-start | bytes 356360 | tf_op jit(solution)/shard_map/ppermute | solution.py:684
  9.3 16.5 %collective-permute-start.2 = (bf16[29,16,128]{2,1,0:T(8,128)(2,1)S(1)}, bf16[29,16,128]{2,1,0:T(8,128)(2,1)S(1)}, u32[]{:S(2)}, u32[]{:S(2)}) collective-permute-start(bf16[29,16,128]{2,1,0:T(8,128)(2,1)S(1)} %get-tuple-element.45), channel_id=1, source_target_pairs={{0,5},{1,4},{2,7},{3,6},{4,1},{5,0},{6,3},{7,2},{8,13},{9,12},{10,... | collective-permute-start | bytes 356360 | tf_op jit(solution)/shard_map/ppermute | solution.py:684
  9.3 16.5 %collective-permute-start.3 = (bf16[29,16,128]{2,1,0:T(8,128)(2,1)S(1)}, bf16[29,16,128]{2,1,0:T(8,128)(2,1)S(1)}, u32[]{:S(2)}, u32[]{:S(2)}) collective-permute-start(bf16[29,16,128]{2,1,0:T(8,128)(2,1)S(1)} %get-tuple-element.46), channel_id=1, source_target_pairs={{0,1},{1,0},{2,3},{3,2},{4,5},{5,4},{6,7},{7,6},{8,9},{9,8},{10,11... | collective-permute-start | bytes 356360 | tf_op jit(solution)/shard_map/ppermute | solution.py:684
  9.7 16.9 %collective-permute-start.4 = (bf16[29,16,128]{2,1,0:T(8,128)(2,1)S(1)}, bf16[29,16,128]{2,1,0:T(8,128)(2,1)S(1)}, u32[]{:S(2)}, u32[]{:S(2)}) collective-permute-start(bf16[29,16,128]{2,1,0:T(8,128)(2,1)S(1)} %get-tuple-element.48), channel_id=1, source_target_pairs={{0,6},{1,7},{2,4},{3,5},{4,2},{5,3},{6,0},{7,1},{8,14},{9,15},{10,... | collective-permute-start | bytes 356360 | tf_op jit(solution)/shard_map/ppermute | solution.py:684
  17.1 9.5 %collective-permute-start.5 = (bf16[29,16,128]{2,1,0:T(8,128)(2,1)S(1)}, bf16[29,16,128]{2,1,0:T(8,128)(2,1)S(1)}, u32[]{:S(2)}, u32[]{:S(2)}) collective-permute-start(bf16[29,16,128]{2,1,0:T(8,128)(2,1)S(1)} %slice.4), channel_id=1, source_target_pairs={{0,1},{1,0},{2,3},{3,2},{4,5},{5,4},{6,7},{7,6},{8,9},{9,8},{10,11... | collective-permute-start | bytes 356360 | tf_op jit(solution)/shard_map/ppermute | solution.py:684
  17.2 9.8 %collective-permute-start.6 = (bf16[29,16,128]{2,1,0:T(8,128)(2,1)S(1)}, bf16[29,16,128]{2,1,0:T(8,128)(2,1)S(1)}, u32[]{:S(2)}, u32[]{:S(2)}) collective-permute-start(bf16[29,16,128]{2,1,0:T(8,128)(2,1)S(1)} %get-tuple-element.50), channel_id=1, source_target_pairs={{0,7},{1,6},{2,5},{3,4},{4,3},{5,2},{6,1},{7,0},{8,15},{9,14},{10,... | collective-permute-start | bytes 356360 | tf_op jit(solution)/shard_map/ppermute | solution.py:684
  27.3 4.4 %collective-permute-start.8 = (bf16[16,16,128]{2,1,0:T(8,128)(2,1)S(1)}, bf16[16,16,128]{2,1,0:T(8,128)(2,1)S(1)}, u32[]{:S(2)}, u32[]{:S(2)}) collective-permute-start(bf16[16,16,128]{2,1,0:T(8,128)(2,1)S(1)} %get-tuple-element.55.left_grid), channel_id=1, source_target_pairs={{0,24},{8,0},{16,8},{24,16},{1,25},{9,1},{17,9},{25,17},{2,26},{10... | collective-permute-start | bytes 196616 | tf_op jit(solution)/shard_map/ppermute | solution.py:741
  29.7 4.7 %collective-permute-start.7 = (bf16[16,16,128]{2,1,0:T(8,128)(2,1)S(1)}, bf16[16,16,128]{2,1,0:T(8,128)(2,1)S(1)}, u32[]{:S(2)}, u32[]{:S(2)}) collective-permute-start(bf16[16,16,128]{2,1,0:T(8,128)(2,1)S(1)} %get-tuple-element.51.right_grid), channel_id=1, source_target_pairs={{0,24},{8,0},{16,8},{24,16},{1,25},{9,1},{17,9},{25,17},{2,26},{10... | collective-permute-start | bytes 196616 | tf_op jit(solution)/shard_map/ppermute | solution.py:741
